TPU v7x, 512 devices: a whole 4x4x16 slice. The times are simulated.
512 devices in a mesh: enc: 64 (over x, z), dec: 8 (over y, core).
Axes of the slice: x: 4, y: 4, z: 16, core: 2. Of those that a mesh axis runs over, the one named last changes fastest.
Arguments:
- pixels: bfloat16 [8, 576, 3072], P('dec', 'enc'), may hold values from -6 to 6
- tile_counts: int32 [8, 64], P('dec', 'enc'), may hold values from 1 to 9, as said below
- text_gaps: int32 [8, 64], P('dec', 'enc'), may hold values from 0 to 64
- stem_weight: bfloat16 [48, 384], replicated, may hold values from -0.875 to 0.875
- depth_weight: bfloat16 [49, 384], replicated, may hold values from -0.875 to 0.875
- norm_gain: float32 [384], replicated, may hold values from 0.5 to 2
- up_weight: bfloat16 [384, 768], replicated, may hold values from -0.3125 to 0.3125
- down_weight: bfloat16 [768, 384], replicated, may hold values from -0.21875 to 0.21875
- layer_scale: float32 [384], replicated, may hold values from 0.25 to 1
- embed_grad: bfloat16 [64, 1664, 384], P('enc', 'dec'), may hold values from -6 to 6
Outputs:
- image_embeds: bfloat16 [64, 1664, 384], P('enc', 'dec')
- stem_grad: float32 [48, 384], replicated
- depth_grad: float32 [49, 384], replicated
- gain_grad: float32 [384], replicated
- up_grad: float32 [384, 768], replicated
- down_grad: float32 [768, 384], replicated
- scale_grad: float32 [384], replicated
Inputs may be any that keep to these rules, and one draw needn't show every extreme that they name: `tile_counts`: for each index of dec, the counts of each aligned group of four consecutive indices of enc sum to exactly 12.
All inputs are finite; a program needn't handle non-finite values.
Results may differ from a plain program's by a relative error of at most 0.013.
Values may be sent and summed in bfloat16 or wider, within the bound.
No kernel may reach another device: no remote copies, remote signals or barrier semaphores. Data moves between devices by JAX's collectives and lax.ppermute only.
A program may use at most 64 MiB of HBM per device.

v0:
```python
import math

import jax
import jax.numpy as jnp
from jax import lax
from jax.sharding import PartitionSpec as P

WIDTH = 384
KERNEL = 7
PATCH_CH = 48
TILE = 8
MEAN_TILES = 3
SLOTS = 9
FEAT_TILE = 16


epsilon = 1e-06


def encode(tile_block, stem_weight, depth_weight, norm_gain, up_weight, down_weight, layer_scale):
    tile_total = tile_block.shape[0]
    reach = KERNEL // 2
    half_tile = TILE // 2
    patches = tile_block.reshape(tile_total * TILE * TILE, PATCH_CH)
    stem_out = jnp.dot(patches, stem_weight, preferred_element_type=jnp.float32).astype(
        jnp.bfloat16
    )
    stem_grid = stem_out.reshape(tile_total, TILE, TILE, WIDTH).astype(jnp.float32)
    padded = jnp.pad(stem_grid, ((0, 0), (reach, reach), (reach, reach), (0, 0)))
    kernel = depth_weight.astype(jnp.float32)
    mixed_field = jnp.zeros_like(stem_grid)
    for row_tap in range(KERNEL):
        for col_tap in range(KERNEL):
            mixed_field = (
                mixed_field
                + padded[:, row_tap : row_tap + TILE, col_tap : col_tap + TILE, :]
                * kernel[row_tap * KERNEL + col_tap]
            )
    flat_rows = mixed_field.reshape(-1, WIDTH)
    channel_mean = jnp.mean(flat_rows, axis=1, keepdims=True)
    deviation = flat_rows - channel_mean
    variance = jnp.mean(deviation * deviation, axis=1, keepdims=True)
    inv_std = lax.rsqrt(variance + epsilon)
    centred = deviation * inv_std
    normed = (centred * norm_gain).astype(jnp.bfloat16)
    hidden = jnp.dot(normed, up_weight, preferred_element_type=jnp.float32)
    activated = jax.nn.gelu(hidden).astype(jnp.bfloat16)
    projected = jnp.dot(activated, down_weight, preferred_element_type=jnp.float32)
    block_out = stem_grid.reshape(-1, WIDTH) + layer_scale * projected
    pooled = jnp.mean(block_out.reshape(tile_total, half_tile, 2, half_tile, 2, WIDTH), axis=(2, 4))
    pooled = pooled.reshape(tile_total, half_tile * half_tile, WIDTH)
    stored = (patches, padded, centred, inv_std, normed, hidden, activated, projected)
    return (pooled, stored)


def backward_head(stored, cotangent, down_weight, layer_scale):
    patches, padded, centred, inv_std, normed, hidden, activated, projected = stored
    tile_total = cotangent.shape[0]
    half_tile = TILE // 2
    spread_out = jnp.broadcast_to(
        cotangent.reshape(tile_total, half_tile, 1, half_tile, 1, WIDTH),
        (tile_total, half_tile, 2, half_tile, 2, WIDTH),
    )
    grad_block = (0.25 * spread_out).reshape(-1, WIDTH)
    scale_term = jnp.sum(grad_block * projected, axis=0)
    grad_proj = (grad_block * layer_scale).astype(jnp.bfloat16)
    down_term = lax.dot_general(
        activated, grad_proj, (((0,), (0,)), ((), ())), preferred_element_type=jnp.float32
    )
    grad_act = lax.dot_general(
        grad_proj, down_weight, (((1,), (1,)), ((), ())), preferred_element_type=jnp.float32
    )
    grad_hidden = jax.vjp(jax.nn.gelu, hidden)[1](grad_act)[0].astype(jnp.bfloat16)
    return (scale_term, down_term, grad_hidden, grad_block)


def backward_middle(stored, grad_hidden, up_weight, norm_gain):
    patches, padded, centred, inv_std, normed, hidden, activated, projected = stored
    up_term = lax.dot_general(
        normed, grad_hidden, (((0,), (0,)), ((), ())), preferred_element_type=jnp.float32
    )
    grad_normed = lax.dot_general(
        grad_hidden, up_weight, (((1,), (1,)), ((), ())), preferred_element_type=jnp.float32
    )
    gain_term = jnp.sum(grad_normed * centred, axis=0)
    scaled = grad_normed * norm_gain
    grad_mixed = inv_std * (
        scaled
        - jnp.mean(scaled, axis=1, keepdims=True)
        - centred * jnp.mean(scaled * centred, axis=1, keepdims=True)
    )
    return (gain_term, up_term, grad_mixed)


def backward_tail(stored, grad_mixed, grad_block, depth_weight):
    patches, padded, centred, inv_std, normed, hidden, activated, projected = stored
    tile_total = padded.shape[0]
    reach = KERNEL // 2
    grid_grad = grad_mixed.reshape(tile_total, TILE, TILE, WIDTH)
    grad_padded = jnp.pad(grid_grad, ((0, 0), (reach, reach), (reach, reach), (0, 0)))
    kernel = depth_weight.astype(jnp.float32)
    depth_rows = []
    inner = jnp.zeros_like(grid_grad)
    for row_tap in range(KERNEL):
        for col_tap in range(KERNEL):
            window = padded[:, row_tap : row_tap + TILE, col_tap : col_tap + TILE, :]
            depth_rows.append(jnp.sum(window * grid_grad, axis=(0, 1, 2)))
            row_start = KERNEL - 1 - row_tap
            col_start = KERNEL - 1 - col_tap
            inner = (
                inner
                + grad_padded[:, row_start : row_start + TILE, col_start : col_start + TILE, :]
                * kernel[row_tap * KERNEL + col_tap]
            )
    depth_term = jnp.stack(depth_rows)
    grad_stem = (grad_block + inner.reshape(-1, WIDTH)).astype(jnp.bfloat16)
    stem_term = lax.dot_general(
        patches, grad_stem, (((0,), (0,)), ((), ())), preferred_element_type=jnp.float32
    )
    return (depth_term, stem_term)


def on_device(
    pixels,
    tile_counts,
    text_gaps,
    stem_weight,
    depth_weight,
    norm_gain,
    up_weight,
    down_weight,
    layer_scale,
    embed_grad,
):
    n_enc = lax.axis_size("enc")
    n_dec = lax.axis_size("dec")
    dec_here = lax.axis_index("dec")
    count_here = tile_counts[0, 0]
    block_rows = SLOTS * FEAT_TILE
    seq_rows = embed_grad.shape[1]
    weights = (stem_weight, depth_weight, norm_gain, up_weight, down_weight, layer_scale)
    column = lax.all_gather(
        jnp.concatenate([tile_counts[0], text_gaps[0]])[None, :], "dec", axis=0, tiled=True
    )
    col_counts = column[:, 0]
    col_gaps = column[:, 1]
    owner_span = col_counts * FEAT_TILE + col_gaps
    offsets = jnp.cumsum(owner_span) - owner_span + col_gaps
    dec_ids = jnp.arange(n_dec)
    own_offset = jnp.sum(jnp.where(dec_ids == dec_here, offsets, 0))
    occupied = jnp.arange(SLOTS) < count_here
    pooled, stored = encode(pixels[0], *weights)
    owner_block = (
        jnp.where(occupied[:, None, None], pooled, 0.0).astype(jnp.bfloat16).reshape(SLOTS, -1)
    )
    row_block = owner_block.reshape(block_rows, WIDTH)
    shard_rows = lax.all_gather(row_block, "dec", axis=0, tiled=True)
    row_total = shard_rows.shape[0]
    global_row = jnp.arange(row_total)
    source = global_row // block_rows
    within = global_row % block_rows
    pick_mask = dec_ids[None, :] == source[:, None]
    source_count = jnp.sum(jnp.where(pick_mask, col_counts[None, :], 0), axis=1)
    source_offset = jnp.sum(jnp.where(pick_mask, offsets[None, :], 0), axis=1)
    target = source_offset + within - dec_here * seq_rows
    keep_mask = (within < source_count * FEAT_TILE) & (target >= 0) & (target < seq_rows)
    target_row = jnp.where(keep_mask, target, seq_rows)
    sequence = (
        jnp.zeros((seq_rows, WIDTH), jnp.bfloat16).at[target_row].add(shard_rows, mode="drop")
    )
    shard_rows = lax.all_gather(embed_grad[0], "dec", axis=0, tiled=True)
    row_total = shard_rows.shape[0]
    row_ids = jnp.arange(block_rows)
    local_row = own_offset + row_ids
    inside = (local_row >= 0) & (local_row < row_total) & (row_ids < count_here * FEAT_TILE)
    taken_rows = jnp.take(shard_rows, jnp.clip(local_row, 0, row_total - 1), axis=0)
    own_grad = jnp.where(inside[:, None], taken_rows, jnp.zeros((block_rows, WIDTH), jnp.bfloat16))
    cotangent = own_grad.reshape(SLOTS, FEAT_TILE, WIDTH).astype(jnp.float32)
    scale_term, down_term, grad_hidden, grad_block = backward_head(
        stored, cotangent, down_weight, layer_scale
    )
    gain_term, up_term, grad_mixed = backward_middle(stored, grad_hidden, up_weight, norm_gain)
    depth_term, stem_term = backward_tail(stored, grad_mixed, grad_block, depth_weight)
    stem_sum, depth_sum, gain_sum, up_sum, down_sum, scale_sum = lax.psum(
        (stem_term, depth_term, gain_term, up_term, down_term, scale_term), ("enc", "dec")
    )
    grad_scale = 1.0 / math.sqrt(n_dec * n_enc * MEAN_TILES * FEAT_TILE)
    return (
        sequence[None],
        stem_sum * grad_scale,
        depth_sum * grad_scale,
        gain_sum * grad_scale,
        up_sum * grad_scale,
        down_sum * grad_scale,
        scale_sum * grad_scale,
    )


def solution(mesh):
    return jax.shard_map(
        on_device,
        mesh=mesh,
        in_specs=(
            P("dec", "enc", None),
            P("dec", "enc"),
            P("dec", "enc"),
            P(),
            P(),
            P(),
            P(),
            P(),
            P(),
            P("enc", "dec", None),
        ),
        out_specs=(P("enc", "dec", None), P(), P(), P(), P(), P(), P()),
        check_vma=False,
    )
```

profile of v0, /device:TPU:1, one launch (start us, length us, event | category | flops | bytes accessed | tf_op | source)
XLA Modules:
  0.0 578.7 jit_solution(13373561499897208192)
XLA Ops:
  10.7 1.3 dynamic-slice
  12.8 9.0 %all-reduce.2 = s32[16]{0:T(128)S(1)} all-reduce(s32[16]{0:T(128)S(1)} %add_dynamic-update-slice_fusion), channel_id=2, replica_groups=mesh['enc'=64,'dec'=8] {'dec'}, use_global_device_ids=true, to_apply=%add.2 | all-reduce | flops 16 | bytes 128
  24.2 5.6 fusion.119
  34.4 2.9 fusion.106
  37.3 10.2 %all-gather.4.cloned.1.call-done = bf16[1,1664,384]{2,1,0:T(8,128)(2,1)} async-done(((bf16[1,208,384]{2,1,0:T(8,128)(2,1)}), bf16[1,1664,384]{2,1,0:T(8,128)(2,1)}) %all-gather.4.cloned.1.call-update) | async-done | bytes 1277968 | tf_op jit(solution)/shard_map/all_gather | solution.py:171
  47.5 2.4 gather_fusion
  51.3 1.8 reshape.321
  53.1 3.2 fusion.6
  56.3 1.2 multiply_reduce_fusion.1
  57.6 1.7 fusion.105
  59.3 2.0 fusion.107
  61.3 3.6 multiply_reduce_fusion
  64.9 1.4 multiply_reduce_fusion.39
  66.7 2.0 multiply_reduce_fusion.20
  68.7 1.6 multiply_reduce_fusion.2
  70.6 4.9 fusion.96
  79.4 4.4 stack.199
  84.0 13.6 %all_gather.10 = bf16[1152,384]{1,0:T(8,128)(2,1)S(1)} all-gather(bf16[144,384]{1,0:T(8,128)(2,1)S(1)} %select_convert_fusion), channel_id=1, replica_groups=mesh['enc'=64,'dec'=8] {'dec'}, dimensions={0}, use_global_device_ids=true | all-gather | bytes 995328 | tf_op jit(solution)/shard_map/all_gather | solution.py:157
  97.7 10.7 %scatter_custom_fusion = bf16[208,384]{1,0:T(8,128)(2,1)} fusion(s32[1152]{0:T(1024)} %fusion.116, bf16[1152,384]{1,0:T(8,128)(2,1)S(1)} %all_gather.10, bf16[]{:T(256)} %constant.33.clone.1), kind=kCustom, calls=%fused_computation.278 | custom fusion | flops 442368 | bytes 160256 | tf_op jit(solution)/shard_map/scatter-add | solution.py:169
  108.3 104.9 %all-reduce.3 = (f32[384]{0:T(512)S(1)}, f32[384]{0:T(512)S(1)}) all-reduce(f32[384]{0:T(512)S(1)} %copy-done.75, f32[384]{0:T(512)S(1)} %copy-done.76), channel_id=1, replica_groups=mesh['enc'=64,'dec'=8] {'enc','dec'}, use_global_device_ids=true, to_apply=%region_62.63 | all-reduce | flops 768 | bytes 6144 | tf_op jit(solution)/shard_map/psum | solution.py:184
  214.4 350.8 %all-reduce.7.cloned.1.call-done = (f32[48,384]{1,0:T(8,128)}, f32[49,384]{1,0:T(8,128)}, f32[384,768]{1,0:T(8,128)}, f32[768,384]{1,0:T(8,128)}) async-done(((f32[48,384]{1,0:T(8,128)}, f32[49,384]{1,0:T(8,128)}, f32[384,768]{1,0:T(8,128)}, f32[768,384]{1,0:T(8,128)}), (f32[48,384]{1,0:T(8,128)}, f32[49,384]{1,0:T(8,128)}, f32[384,768]{1,0:T(8,128)}, f32[768,384]{1,0:T(8,128)})) %all-reduce.7.cloned.1.call-update) | async-done | bytes 2508304 | tf_op jit(solution)/shard_map/psum | solution.py:184
  565.2 1.6 broadcast_multiply_fusion.4
  566.8 1.5 broadcast_multiply_fusion.3
  568.3 2.4 broadcast_multiply_fusion.1
  (257 shorter events, 16.1 us)
Async XLA Ops:
  7.2 45.9 %copy-start = (bf16[768,384]{1,0:T(8,128)(2,1)S(1)}, bf16[768,384]{1,0:T(8,128)(2,1)}, u32[]{:S(2)}) copy-start(bf16[768,384]{1,0:T(8,128)(2,1)} %param.17) | copy-start | bytes 1769476
  7.2 40.4 %all-gather.4.cloned.1.call-start = ((), (), s32[]{:S(2)}) async-start(), calls=%async_computation | async-start | bytes 1437696 | tf_op jit(solution)/shard_map/all_gather | solution.py:171
  7.9 557.2 %all-reduce.7.cloned.1.call-start = ((), (), s32[]{:S(2)}) async-start(), calls=%async_computation.1 | async-start | bytes 5038080 | tf_op jit(solution)/shard_map/psum | solution.py:184
  9.2 21.9 %copy-start.37 = (f32[384]{0:T(512)}, f32[384]{0:T(512)S(1)}, u32[]{:S(2)}) copy-start(f32[384]{0:T(512)S(1)} %get-tuple-element.58) | copy-start | bytes 4612
  9.2 21.9 %copy-start.39 = (f32[384]{0:T(512)}, f32[384]{0:T(512)S(1)}, u32[]{:S(2)}) copy-start(f32[384]{0:T(512)S(1)} %get-tuple-element.59) | copy-start | bytes 4612
  9.2 21.9 %copy-start.41 = (f32[384]{0:T(512)}, f32[384]{0:T(512)S(1)}, u32[]{:S(2)}) copy-start(f32[384]{0:T(512)S(1)} %get-tuple-element.60) | copy-start | bytes 4612
  9.2 21.9 %copy-start.43 = (f32[384]{0:T(512)}, f32[384]{0:T(512)S(1)}, u32[]{:S(2)}) copy-start(f32[384]{0:T(512)S(1)} %get-tuple-element.61) | copy-start | bytes 4612
  9.2 21.9 %copy-start.45 = (f32[384]{0:T(512)}, f32[384]{0:T(512)S(1)}, u32[]{:S(2)}) copy-start(f32[384]{0:T(512)S(1)} %get-tuple-element.62) | copy-start | bytes 4612
  9.2 21.9 %copy-start.47 = (f32[384]{0:T(512)}, f32[384]{0:T(512)S(1)}, u32[]{:S(2)}) copy-start(f32[384]{0:T(512)S(1)} %get-tuple-element.63) | copy-start | bytes 4612
  9.2 21.9 %copy-start.49 = (f32[384]{0:T(512)}, f32[384]{0:T(512)S(1)}, u32[]{:S(2)}) copy-start(f32[384]{0:T(512)S(1)} %get-tuple-element.64) | copy-start | bytes 4612
  9.2 21.9 %copy-start.51 = (f32[384]{0:T(512)}, f32[384]{0:T(512)S(1)}, u32[]{:S(2)}) copy-start(f32[384]{0:T(512)S(1)} %get-tuple-element.65) | copy-start | bytes 4612
  9.2 21.9 %copy-start.53 = (f32[384]{0:T(512)}, f32[384]{0:T(512)S(1)}, u32[]{:S(2)}) copy-start(f32[384]{0:T(512)S(1)} %get-tuple-element.66) | copy-start | bytes 4612
  9.3 21.9 %copy-start.55 = (f32[384]{0:T(512)}, f32[384]{0:T(512)S(1)}, u32[]{:S(2)}) copy-start(f32[384]{0:T(512)S(1)} %get-tuple-element.67) | copy-start | bytes 4612
  9.3 21.9 %copy-start.57 = (f32[384]{0:T(512)}, f32[384]{0:T(512)S(1)}, u32[]{:S(2)}) copy-start(f32[384]{0:T(512)S(1)} %get-tuple-element.68) | copy-start | bytes 4612
  9.3 21.9 %copy-start.59 = (f32[384]{0:T(512)}, f32[384]{0:T(512)S(1)}, u32[]{:S(2)}) copy-start(f32[384]{0:T(512)S(1)} %get-tuple-element.69) | copy-start | bytes 4612
  9.3 21.9 %copy-start.61 = (f32[384]{0:T(512)}, f32[384]{0:T(512)S(1)}, u32[]{:S(2)}) copy-start(f32[384]{0:T(512)S(1)} %get-tuple-element.70) | copy-start | bytes 4612
  9.3 21.9 %copy-start.63 = (f32[384]{0:T(512)}, f32[384]{0:T(512)S(1)}, u32[]{:S(2)}) copy-start(f32[384]{0:T(512)S(1)} %get-tuple-element.71) | copy-start | bytes 4612
  9.3 21.9 %copy-start.65 = (f32[384]{0:T(512)}, f32[384]{0:T(512)S(1)}, u32[]{:S(2)}) copy-start(f32[384]{0:T(512)S(1)} %get-tuple-element.72) | copy-start | bytes 4612
  9.3 21.9 %copy-start.67 = (f32[384]{0:T(512)}, f32[384]{0:T(512)S(1)}, u32[]{:S(2)}) copy-start(f32[384]{0:T(512)S(1)} %get-tuple-element.73) | copy-start | bytes 4612
  9.3 21.9 %copy-start.69 = (f32[384]{0:T(512)}, f32[384]{0:T(512)S(1)}, u32[]{:S(2)}) copy-start(f32[384]{0:T(512)S(1)} %get-tuple-element.74) | copy-start | bytes 4612
  9.3 21.9 %copy-start.71 = (f32[384]{0:T(512)}, f32[384]{0:T(512)S(1)}, u32[]{:S(2)}) copy-start(f32[384]{0:T(512)S(1)} %get-tuple-element.75) | copy-start | bytes 4612
  9.3 21.9 %copy-start.73 = (f32[384]{0:T(512)}, f32[384]{0:T(512)S(1)}, u32[]{:S(2)}) copy-start(f32[384]{0:T(512)S(1)} %get-tuple-element.76) | copy-start | bytes 4612
  83.8 24.6 %copy-start.75 = (f32[384]{0:T(512)S(1)}, f32[384]{0:T(512)}, u32[]{:S(2)}) copy-start(f32[384]{0:T(512)} %get-tuple-element.7) | copy-start | bytes 4612
  83.8 24.6 %copy-start.76 = (f32[384]{0:T(512)S(1)}, f32[384]{0:T(512)}, u32[]{:S(2)}) copy-start(f32[384]{0:T(512)} %get-tuple-element.123) | copy-start | bytes 4612
  (57 other events, 466.5 us)
Sparse Core Ops, SparseCore 0:
  10.1 37.3 all-gather.3
  83.9 481.1 all-reduce.6
where the time goes:
time: 580 us; the launch traced here: 579 us
  waiting for transfers between devices  362 us (62%)
  blocking collectives  128 us (22%)
  other arithmetic  40.1 us (7%)
  between operations  17.7 us (3%)
  matrix products  16.6 us (3%)
  local copies, waits for them, and re-layouts  14.9 us (3%)
    psum x1, waiting for transfers between devices, on_device(): lax.psum((stem_term, depth_term, gain_term, up_term, down_term, scale_ter...  351 us
    psum x1, blocking collectives, on_device(): lax.psum((stem_term, depth_term, gain_term, up_term, down_term, scale_ter...  105 us
    all_gather x1, blocking collectives, on_device(): shard_rows = lax.all_gather(row_block, 'dec', axis=0, tiled=True)  13.6 us
  transfers between devices with their start and end apart: 2, of which 2 were waited for; matrix products, arithmetic and copies ran while one was open for 5% of the time, Pallas kernels for 0%

commit v1 on v0

--- a/solution.py
+++ b/solution.py
@@ -3,6 +3,7 @@
 import jax
 import jax.numpy as jnp
 from jax import lax
+from jax.sharding import Mesh
 from jax.sharding import PartitionSpec as P
 
 WIDTH = 384
@@ -12,6 +13,11 @@
 MEAN_TILES = 3
 SLOTS = 9
 FEAT_TILE = 16
+LANES = 128
+PACK_ROWS = 5120
+DEC = ("y", "core")
+ENC = ("x", "zh", "zl")
+PLANE = ("x", "y")
 
 
 epsilon = 1e-06
@@ -120,6 +126,44 @@
     return (depth_term, stem_term)
 
 
+def pack(terms):
+    rows = [term.reshape(-1, LANES) for term in terms]
+    used = sum(part.shape[0] for part in rows)
+    rows.append(jnp.zeros((PACK_ROWS - used, LANES), jnp.float32))
+    return jnp.concatenate(rows).astype(jnp.bfloat16)
+
+
+def unpack(packed, like, scale):
+    out, at = [], 0
+    for term in like:
+        count = term.size // LANES
+        piece = packed[at : at + count].astype(jnp.float32) * scale
+        out.append(piece.reshape(term.shape))
+        at += count
+    return out
+
+
+def swap_blocks(blocks, axes):
+    return lax.all_to_all(blocks, axes, 0, 0, tiled=True)
+
+
+def sum_blocks(blocks):
+    return jnp.sum(blocks.astype(jnp.float32), axis=0).astype(jnp.bfloat16)
+
+
+def spread(block, copies):
+    return jnp.broadcast_to(block[None], (copies,) + block.shape)
+
+
+def sum_all(packed):
+    half = sum_blocks(swap_blocks(packed.reshape(2, PACK_ROWS // 2, LANES), "core"))
+    part = sum_blocks(swap_blocks(half.reshape(16, PACK_ROWS // 32, LANES), PLANE))
+    part = sum_blocks(swap_blocks(spread(part, 4), "zl"))
+    part = sum_blocks(swap_blocks(spread(part, 4), "zh"))
+    half = swap_blocks(spread(part, 16), PLANE).reshape(PACK_ROWS // 2, LANES)
+    return swap_blocks(spread(half, 2), "core").reshape(PACK_ROWS, LANES)
+
+
 def on_device(
     pixels,
     tile_counts,
@@ -132,15 +176,15 @@
     layer_scale,
     embed_grad,
 ):
-    n_enc = lax.axis_size("enc")
-    n_dec = lax.axis_size("dec")
-    dec_here = lax.axis_index("dec")
+    n_enc = 64
+    n_dec = lax.axis_size(DEC)
+    dec_here = lax.axis_index(DEC)
     count_here = tile_counts[0, 0]
     block_rows = SLOTS * FEAT_TILE
     seq_rows = embed_grad.shape[1]
     weights = (stem_weight, depth_weight, norm_gain, up_weight, down_weight, layer_scale)
     column = lax.all_gather(
-        jnp.concatenate([tile_counts[0], text_gaps[0]])[None, :], "dec", axis=0, tiled=True
+        jnp.concatenate([tile_counts[0], text_gaps[0]])[None, :], DEC, axis=0, tiled=True
     )
     col_counts = column[:, 0]
     col_gaps = column[:, 1]
@@ -149,69 +193,47 @@
     dec_ids = jnp.arange(n_dec)
     own_offset = jnp.sum(jnp.where(dec_ids == dec_here, offsets, 0))
     occupied = jnp.arange(SLOTS) < count_here
+    gathered = lax.all_gather(embed_grad[0], DEC, axis=0, tiled=True)
     pooled, stored = encode(pixels[0], *weights)
-    owner_block = (
-        jnp.where(occupied[:, None, None], pooled, 0.0).astype(jnp.bfloat16).reshape(SLOTS, -1)
-    )
-    row_block = owner_block.reshape(block_rows, WIDTH)
-    shard_rows = lax.all_gather(row_block, "dec", axis=0, tiled=True)
-    row_total = shard_rows.shape[0]
-    global_row = jnp.arange(row_total)
-    source = global_row // block_rows
-    within = global_row % block_rows
-    pick_mask = dec_ids[None, :] == source[:, None]
-    source_count = jnp.sum(jnp.where(pick_mask, col_counts[None, :], 0), axis=1)
-    source_offset = jnp.sum(jnp.where(pick_mask, offsets[None, :], 0), axis=1)
-    target = source_offset + within - dec_here * seq_rows
-    keep_mask = (within < source_count * FEAT_TILE) & (target >= 0) & (target < seq_rows)
-    target_row = jnp.where(keep_mask, target, seq_rows)
-    sequence = (
-        jnp.zeros((seq_rows, WIDTH), jnp.bfloat16).at[target_row].add(shard_rows, mode="drop")
-    )
-    shard_rows = lax.all_gather(embed_grad[0], "dec", axis=0, tiled=True)
-    row_total = shard_rows.shape[0]
-    row_ids = jnp.arange(block_rows)
-    local_row = own_offset + row_ids
-    inside = (local_row >= 0) & (local_row < row_total) & (row_ids < count_here * FEAT_TILE)
-    taken_rows = jnp.take(shard_rows, jnp.clip(local_row, 0, row_total - 1), axis=0)
-    own_grad = jnp.where(inside[:, None], taken_rows, jnp.zeros((block_rows, WIDTH), jnp.bfloat16))
-    cotangent = own_grad.reshape(SLOTS, FEAT_TILE, WIDTH).astype(jnp.float32)
+    owner_block = jnp.where(occupied[:, None, None], pooled, 0.0).astype(jnp.bfloat16)
+    placed = lax.dynamic_update_slice(
+        jnp.zeros((n_dec * seq_rows, WIDTH), jnp.bfloat16),
+        owner_block.reshape(block_rows, WIDTH),
+        (own_offset, 0),
+    )
+    sequence = lax.psum_scatter(placed, DEC, scatter_dimension=0, tiled=True)
+    taken_rows = lax.dynamic_slice(gathered, (own_offset, 0), (block_rows, WIDTH))
+    own_grad = jnp.where(
+        occupied[:, None, None], taken_rows.reshape(SLOTS, FEAT_TILE, WIDTH), jnp.bfloat16(0)
+    )
+    cotangent = own_grad.astype(jnp.float32)
     scale_term, down_term, grad_hidden, grad_block = backward_head(
         stored, cotangent, down_weight, layer_scale
     )
     gain_term, up_term, grad_mixed = backward_middle(stored, grad_hidden, up_weight, norm_gain)
     depth_term, stem_term = backward_tail(stored, grad_mixed, grad_block, depth_weight)
-    stem_sum, depth_sum, gain_sum, up_sum, down_sum, scale_sum = lax.psum(
-        (stem_term, depth_term, gain_term, up_term, down_term, scale_term), ("enc", "dec")
-    )
+    terms = (stem_term, depth_term, gain_term, up_term, down_term, scale_term)
     grad_scale = 1.0 / math.sqrt(n_dec * n_enc * MEAN_TILES * FEAT_TILE)
-    return (
-        sequence[None],
-        stem_sum * grad_scale,
-        depth_sum * grad_scale,
-        gain_sum * grad_scale,
-        up_sum * grad_scale,
-        down_sum * grad_scale,
-        scale_sum * grad_scale,
-    )
+    return (sequence[None], *unpack(sum_all(pack(terms)), terms, grad_scale))
 
 
 def solution(mesh):
+    fine = Mesh(mesh.devices.reshape(4, 4, 4, 4, 2), ("x", "zh", "zl", "y", "core"))
     return jax.shard_map(
         on_device,
-        mesh=mesh,
+        mesh=fine,
         in_specs=(
-            P("dec", "enc", None),
-            P("dec", "enc"),
-            P("dec", "enc"),
-            P(),
-            P(),
-            P(),
-            P(),
-            P(),
-            P(),
-            P("enc", "dec", None),
+            P(DEC, ENC, None),
+            P(DEC, ENC),
+            P(DEC, ENC),
+            P(),
+            P(),
+            P(),
+            P(),
+            P(),
+            P(),
+            P(ENC, DEC, None),
         ),
-        out_specs=(P("enc", "dec", None), P(), P(), P(), P(), P(), P()),
+        out_specs=(P(ENC, DEC, None), P(), P(), P(), P(), P(), P()),
         check_vma=False,
     )

time: 580 us -> 178 us (0.31)
  waiting for transfers between devices: 362 us -> 25.6 us
  blocking collectives: 128 us -> 55.2 us
  other arithmetic: 40.1 us -> 23.2 us
  starting transfers between devices: 0.08 us -> 15.3 us
  local copies, waits for them, and re-layouts: 14.9 us -> 22 us
    psum x1 -> x0, waiting for transfers between devices: 351 us -> none  [on_device(): lax.psum((stem_term, depth_term, gain_term, up_term, down_term, scale_ter...]
    psum x1 -> x0, blocking collectives: 105 us -> none  [on_device(): lax.psum((stem_term, depth_term, gain_term, up_term, down_term, scale_ter...]
    all_to_all x0 -> x4, blocking collectives: none -> 46.2 us  [swap_blocks(): return lax.all_to_all(blocks, axes, 0, 0, tiled=True)]
    all_to_all x0 -> x2, starting transfers between devices: none -> 15.2 us  [swap_blocks(): return lax.all_to_all(blocks, axes, 0, 0, tiled=True)]
    all_gather x1 -> x0, blocking collectives: 13.6 us -> none  [on_device(): shard_rows = lax.all_gather(row_block, 'dec', axis=0, tiled=True)]
    all_to_all x0 -> x2, waiting for transfers between devices: none -> 13.4 us  [swap_blocks(): return lax.all_to_all(blocks, axes, 0, 0, tiled=True)]
    scatter-add x1 -> x0, other arithmetic: 10.7 us -> none  [on_device(): jnp.zeros((seq_rows, WIDTH), jnp.bfloat16).at[target_row]]
    reshape x0 -> x9, local copies, waits for them, and re-layouts: none -> 7.02 us  [the longest x4 5.04 us: unpack(): out.append(piece.reshape(term.shape))]
  transfers between devices with their start and end apart: 2 -> 4, of which waited for: 2 -> 4; matrix products, arithmetic and copies ran while one was open for 5% -> 14% of each run, Pallas kernels for 0% -> 0%
where the time goes in v1:
time: 178 us; the launch traced here: 175 us
  blocking collectives  55.2 us (31%)
  waiting for transfers between devices  25.6 us (14%)
  other arithmetic  23.2 us (13%)
  local copies, waits for them, and re-layouts  22 us (12%)
  between operations  19.6 us (11%)
  starting transfers between devices  15.3 us (9%)
  matrix products  14.5 us (8%)
    all_to_all x4, blocking collectives, swap_blocks(): return lax.all_to_all(blocks, axes, 0, 0, tiled=True)  46.2 us
    all_to_all x2, starting transfers between devices, swap_blocks(): return lax.all_to_all(blocks, axes, 0, 0, tiled=True)  15.2 us
    all_to_all x2, waiting for transfers between devices, swap_blocks(): return lax.all_to_all(blocks, axes, 0, 0, tiled=True)  13.4 us
    all_gather x1, waiting for transfers between devices, on_device(): gathered = lax.all_gather(embed_grad[0], DEC, axis=0, tiled=True)  10.6 us
    unnamed x1, blocking collectives  9 us
    reduce_sum x1, other arithmetic, encode(): channel_mean = jnp.mean(flat_rows, axis=1, keepdims=True)  5.61 us
    reduce_sum x3, other arithmetic, backward_tail(): depth_rows.append(jnp.sum(window * grid_grad, axis=(0, 1, 2)))  5.04 us
    reshape x4, local copies, waits for them, and re-layouts, unpack(): out.append(piece.reshape(term.shape))  5.04 us
  transfers between devices with their start and end apart: 4, of which 4 were waited for; matrix products, arithmetic and copies ran while one was open for 14% of the time, Pallas kernels for 0%

profile of v1, /device:TPU:1, one launch (start us, length us, event | category | flops | bytes accessed | tf_op | source)
XLA Modules:
  0.0 175.2 jit_solution(8918441014734102786)
XLA Ops:
  11.4 5.6 %fusion.111 = (f32[9,8,8]{2,1,0:T(8,128)S(1)}, f32[9,8,8,384]{3,2,1,0:T(8,128)S(1)}) fusion(f32[384]{0:T(512)S(1)} %get-tuple-element.59, f32[384]{0:T(512)S(1)} %get-tuple-element.60, f32[384]{0:T(512)S(1)} %get-tuple-element.61, f32[384]{0:T(512)S(1)} %get-tuple-element.62, f32[384]{0:T(512)S(1)} %get-tuple-element.63, f32[384]{0:T(512)S(1)} %get-tuple-element.64, ...), kind=kLoop, calls=%fused_computation.346 | loop fusion | flops 21675456 | bytes 1847040 | tf_op jit(solution)/shard_map/reduce_sum | solution.py:46
  21.2 9.0 %all-reduce.2 = s32[16]{0:T(128)S(1)} all-reduce(s32[16]{0:T(128)S(1)} %add_dynamic-update-slice_fusion), channel_id=2, replica_groups=mesh['x'=4,'zh'=4,'zl'=4,'y'=4,'core'=2] {'y','core'}, use_global_device_ids=true, to_apply=%add.2 | all-reduce | flops 16 | bytes 128
  34.1 2.9 %fusion.106 = f32[576,768]{1,0:T(8,128)} fusion(bf16[384,768]{1,0:T(8,128)(2,1)} %param.16, f32[576,384]{1,0:T(8,128)S(1)} %fusion.105, f32[384]{0:T(512)S(1)} %copy-done.9), kind=kOutput, calls=%fused_computation.274 | convolution fusion | flops 340180992 | bytes 3245568 | tf_op jit(solution)/shard_map/dot_general | solution.py:52
  37.0 10.6 %all-gather.4.cloned.1.call-done = bf16[1,1664,384]{2,1,0:T(8,128)(2,1)} async-done(((bf16[1,208,384]{2,1,0:T(8,128)(2,1)}), bf16[1,1664,384]{2,1,0:T(8,128)(2,1)}) %all-gather.4.cloned.1.call-update) | async-done | bytes 1277968 | tf_op jit(solution)/shard_map/all_gather | solution.py:196
  49.0 1.5 reshape.240
  50.5 3.2 %fusion.6 = bf16[576,768]{1,0:T(8,128)(2,1)S(1)} fusion(f32[576,768]{1,0:T(8,128)} %fusion.106, bf16[768,384]{1,0:T(8,128)(2,1)S(1)} %copy-done, f32[576,384]{1,0:T(8,128)} %reshape.240, f32[384]{0:T(512)} %param.18), kind=kOutput, calls=%fused_computation.104 | convolution fusion | flops 349028352 | bytes 4130304 | tf_op jit(solution)/shard_map/dot_general | solution.py:76
  55.5 2.5 %multiply_reduce_fusion = (bf16[384]{0:T(512)(128)(2,1)}, f32[576,384]{1,0:T(8,128)}, bf16[384]{0:T(512)(128)(2,1)S(1)}, f32[576,384]{1,0:T(8,128)S(1)}) fusion(f32[576,384]{1,0:T(8,128)S(1)} %copy-done.4, f32[576,384]{1,0:T(8,128)S(1)} %fusion.7, f32[384]{0:T(512)S(1)} %copy-done.70, f32[576,384]{1,0:T(8,128)S(1)} %fusion.105, ...), kind=kOutput, calls=%fused_computation.212 | convolution fusion | flops 346152192 | bytes 7679232 | tf_op jit(solution)/shard_map/dot_general | solution.py:54
  58.0 2.0 %multiply_reduce_fusion.20 = (bf16[384]{0:T(512)(128)(2,1)S(1)}, bf16[384]{0:T(512)(128)(2,1)S(1)}, bf16[384]{0:T(512)(128)(2,1)S(1)}, bf16[384]{0:T(512)(128)(2...) fusion(f32[9,8,8,384]{3,2,1,0:T(8,128)S(1)} %bitcast.46, ...), kind=kLoop, calls=%fused_computation.232 | loop fusion | flops 7955712 | bytes 1783296 | tf_op jit(solution)/shard_map/reduce_sum | solution.py:113
  60.3 1.6 multiply_reduce_fusion.2
  61.9 1.4 multiply_reduce_fusion.39
  63.6 4.7 %fusion.97 = f32[9,8,8,384]{3,2,1,0:T(8,128)S(1)} fusion(f32[9,8,8,384]{3,2,1,0:T(8,128)S(1)} %bitcast.49, f32[384]{0:T(512)S(1)} %get-tuple-element.59, f32[384]{0:T(512)S(1)} %get-tuple-element.60, f32[384]{0:T(512)S(1)} %get-tuple-element.61, f32[384]{0:T(512)S(1)} %get-tuple-element.62, f32[384]{0:T(512)S(1)} %get-tuple-element.63, ...), kind=kLoop, calls=%fused_computation.202 | loop fusion | flops 21454848 | bytes 1844736 | tf_op jit(solution)/shard_map/add | solution.py:117
  68.4 1.5 convolution_convert_fusion.1
  69.9 1.8 %convolution_convert_fusion = bf16[768,384]{1,0:T(8,128)(2,1)} fusion(f32[576,384]{1,0:T(8,128)S(1)} %copy-done.4, f32[384]{0:T(512)S(1)} %copy-done.70, f32[576,768]{1,0:T(8,128)S(1)} %copy-done.1), kind=kOutput, calls=%fused_computation.106 | convolution fusion | flops 344457216 | bytes 3245568 | tf_op jit(solution)/shard_map/dot_general | solution.py:73
  74.6 1.4 reshape.247
  76.1 3.0 %concatenate.8 = bf16[5120,128]{1,0:T(8,128)(2,1)S(1)} concatenate(bf16[144,128]{1,0:T(8,128)(2,1)S(1)} %reshape.243, bf16[147,128]{1,0:T(8,128)(2,1)S(1)} %reshape.244, bf16[3,128]{1,0:T(4,128)(2,1)S(1)} %bitcast.57, bf16[2304,128]{1,0:T(8,128)(2,1)S(1)} %reshape.246, bf16[2304,128]{1,0:T(8,128)(2,1)S(1)} %reshape.247, bf16[3,128]{1,0:T(4,128)(2,1)S(1)} %bitcast.58, ...), dimensions={0} | concatenate | bytes 2621440 | tf_op jit(solution)/shard_map/concatenate | solution.py:133
  79.1 4.6 %all_to_all.30 = bf16[2,2560,128]{2,1,0:T(8,128)(2,1)S(1)} all-to-all(bf16[2,2560,128]{2,1,0:T(8,128)(2,1)S(1)} %bitcast.50), channel_id=1, replica_groups=mesh['x'=4,'zh'=4,'zl'=4,'y'=4,'core'=2] {'core'}, dimensions={0} | all-to-all | bytes 2621440 | tf_op jit(solution)/shard_map/all_to_all | solution.py:147
  85.0 17.2 %all_to_all.31 = bf16[16,160,128]{2,1,0:T(8,128)(2,1)S(1)} all-to-all(bf16[16,160,128]{2,1,0:T(8,128)(2,1)} %bitcast.55), channel_id=1, replica_groups=mesh['x'=4,'zh'=4,'zl'=4,'y'=4,'core'=2] {'x','y'}, dimensions={0} | all-to-all | bytes 1310720 | tf_op jit(solution)/shard_map/all_to_all | solution.py:147
  103.0 4.5 %all-to-all-start.2 = ((bf16[4,160,128]{2,1,0:T(8,128)(2,1)}), bf16[4,160,128]{2,1,0:T(8,128)(2,1)S(1)}, u32[]{:S(2)}, u32[]{:S(2)}) async-start(bf16[4,160,128]{2,1,0:T(8,128)(2,1)} %broadcast_in_dim.96), calls=%async_computation.3 | async-start | bytes 327680 | tf_op jit(solution)/shard_map/all_to_all | solution.py:147
  109.1 3.3 %all-to-all-done.2 = bf16[4,160,128]{2,1,0:T(8,128)(2,1)S(1)} async-done(((bf16[4,160,128]{2,1,0:T(8,128)(2,1)}), bf16[4,160,128]{2,1,0:T(8,128)(2,1)S(1)}, u32[]{:S(2)}, u32[]{:S(2)}) %all-to-all-start.2) | async-done | bytes 163872 | tf_op jit(solution)/shard_map/all_to_all | solution.py:147
  113.1 10.7 %all-to-all-start.3 = ((bf16[4,160,128]{2,1,0:T(8,128)(2,1)}), bf16[4,160,128]{2,1,0:T(8,128)(2,1)S(1)}, u32[]{:S(2)}, u32[]{:S(2)}) async-start(bf16[4,160,128]{2,1,0:T(8,128)(2,1)} %broadcast_in_dim.97), calls=%async_computation.4 | async-start | bytes 327680 | tf_op jit(solution)/shard_map/all_to_all | solution.py:147
  126.0 10.1 %all-to-all-done.3 = bf16[4,160,128]{2,1,0:T(8,128)(2,1)S(1)} async-done(((bf16[4,160,128]{2,1,0:T(8,128)(2,1)}), bf16[4,160,128]{2,1,0:T(8,128)(2,1)S(1)}, u32[]{:S(2)}, u32[]{:S(2)}) %all-to-all-start.3) | async-done | bytes 163872 | tf_op jit(solution)/shard_map/all_to_all | solution.py:147
  136.2 12.9 %all_to_all.32 = bf16[16,160,128]{2,1,0:T(8,128)(2,1)S(1)} all-to-all(bf16[16,160,128]{2,1,0:T(8,128)(2,1)S(1)} %broadcast_in_dim.98), channel_id=1, replica_groups=mesh['x'=4,'zh'=4,'zl'=4,'y'=4,'core'=2] {'x','y'}, dimensions={0} | all-to-all | bytes 1310720 | tf_op jit(solution)/shard_map/all_to_all | solution.py:147
  149.2 11.4 %all_to_all.33 = bf16[2,2560,128]{2,1,0:T(8,128)(2,1)S(1)} all-to-all(bf16[2,2560,128]{2,1,0:T(8,128)(2,1)S(1)} %broadcast_in_dim.100), channel_id=1, replica_groups=mesh['x'=4,'zh'=4,'zl'=4,'y'=4,'core'=2] {'core'}, dimensions={0} | all-to-all | bytes 2621440 | tf_op jit(solution)/shard_map/all_to_all | solution.py:147
  161.9 2.4 %reshape.254 = f32[384,768]{1,0:T(8,128)} reshape(f32[2304,128]{1,0:T(8,128)} %get-tuple-element.116) | data formatting | bytes 2359296 | tf_op jit(solution)/shard_map/reshape | solution.py:141
  (260 shorter events, 25.6 us)
Async XLA Ops:
  7.2 43.3 %copy-start = (bf16[768,384]{1,0:T(8,128)(2,1)S(1)}, bf16[768,384]{1,0:T(8,128)(2,1)}, u32[]{:S(2)}) copy-start(bf16[768,384]{1,0:T(8,128)(2,1)} %param.17) | copy-start | bytes 1769476
  7.2 40.4 %all-gather.4.cloned.1.call-start = ((), (), s32[]{:S(2)}) async-start(), calls=%async_computation.8 | async-start | bytes 1437696 | tf_op jit(solution)/shard_map/all_gather | solution.py:196
  9.0 8.5 %copy-start.28 = (f32[384]{0:T(512)}, f32[384]{0:T(512)S(1)}, u32[]{:S(2)}) copy-start(f32[384]{0:T(512)S(1)} %get-tuple-element.87) | copy-start | bytes 4612
  9.0 8.5 %copy-start.30 = (f32[384]{0:T(512)}, f32[384]{0:T(512)S(1)}, u32[]{:S(2)}) copy-start(f32[384]{0:T(512)S(1)} %get-tuple-element.88) | copy-start | bytes 4612
  9.0 8.5 %copy-start.32 = (f32[384]{0:T(512)}, f32[384]{0:T(512)S(1)}, u32[]{:S(2)}) copy-start(f32[384]{0:T(512)S(1)} %get-tuple-element.89) | copy-start | bytes 4612
  9.0 8.5 %copy-start.34 = (f32[384]{0:T(512)}, f32[384]{0:T(512)S(1)}, u32[]{:S(2)}) copy-start(f32[384]{0:T(512)S(1)} %get-tuple-element.90) | copy-start | bytes 4612
  9.0 8.5 %copy-start.36 = (f32[384]{0:T(512)}, f32[384]{0:T(512)S(1)}, u32[]{:S(2)}) copy-start(f32[384]{0:T(512)S(1)} %get-tuple-element.91) | copy-start | bytes 4612
  9.1 8.5 %copy-start.38 = (f32[384]{0:T(512)}, f32[384]{0:T(512)S(1)}, u32[]{:S(2)}) copy-start(f32[384]{0:T(512)S(1)} %get-tuple-element.92) | copy-start | bytes 4612
  9.1 8.5 %copy-start.40 = (f32[384]{0:T(512)}, f32[384]{0:T(512)S(1)}, u32[]{:S(2)}) copy-start(f32[384]{0:T(512)S(1)} %get-tuple-element.93) | copy-start | bytes 4612
  9.1 8.5 %copy-start.42 = (f32[384]{0:T(512)}, f32[384]{0:T(512)S(1)}, u32[]{:S(2)}) copy-start(f32[384]{0:T(512)S(1)} %get-tuple-element.94) | copy-start | bytes 4612
  9.1 8.5 %copy-start.44 = (f32[384]{0:T(512)}, f32[384]{0:T(512)S(1)}, u32[]{:S(2)}) copy-start(f32[384]{0:T(512)S(1)} %get-tuple-element.95) | copy-start | bytes 4612
  9.2 8.4 %copy-start.48 = (f32[384]{0:T(512)}, f32[384]{0:T(512)S(1)}, u32[]{:S(2)}) copy-start(f32[384]{0:T(512)S(1)} %get-tuple-element.97) | copy-start | bytes 4612
  9.2 8.4 %copy-start.50 = (f32[384]{0:T(512)}, f32[384]{0:T(512)S(1)}, u32[]{:S(2)}) copy-start(f32[384]{0:T(512)S(1)} %get-tuple-element.98) | copy-start | bytes 4612
  9.2 8.4 %copy-start.52 = (f32[384]{0:T(512)}, f32[384]{0:T(512)S(1)}, u32[]{:S(2)}) copy-start(f32[384]{0:T(512)S(1)} %get-tuple-element.99) | copy-start | bytes 4612
  9.2 8.4 %copy-start.54 = (f32[384]{0:T(512)}, f32[384]{0:T(512)S(1)}, u32[]{:S(2)}) copy-start(f32[384]{0:T(512)S(1)} %get-tuple-element.100) | copy-start | bytes 4612
  9.2 8.4 %copy-start.56 = (f32[384]{0:T(512)}, f32[384]{0:T(512)S(1)}, u32[]{:S(2)}) copy-start(f32[384]{0:T(512)S(1)} %get-tuple-element.101) | copy-start | bytes 4612
  9.2 8.4 %copy-start.58 = (f32[384]{0:T(512)}, f32[384]{0:T(512)S(1)}, u32[]{:S(2)}) copy-start(f32[384]{0:T(512)S(1)} %get-tuple-element.102) | copy-start | bytes 4612
  17.1 16.9 %copy-start.9 = (f32[384]{0:T(512)S(1)}, f32[384]{0:T(512)}, u32[]{:S(2)}) copy-start(f32[384]{0:T(512)} %param.15) | copy-start | bytes 4612
  34.1 14.5 %copy-start.71 = (pred[9]{0:T(512)(128)(4,1)S(1)}, pred[9]{0:T(512)(128)(4,1)}, u32[]{:S(2)}) copy-start(pred[9]{0:T(512)(128)(4,1)} %iota_compare_fusion) | copy-start | bytes 31
  83.7 23.8 %copy-start.72 = (pred[9]{0:T(512)(128)(4,1)S(1)}, pred[9]{0:T(512)(128)(4,1)}, u32[]{:S(2)}) copy-start(pred[9]{0:T(512)(128)(4,1)} %iota_compare_fusion) | copy-start | bytes 31
  84.9 22.7 %copy-start.3 = (f32[576,384]{1,0:T(8,128)S(1)}, f32[576,384]{1,0:T(8,128)}, u32[]{:S(2)}) copy-start(f32[576,384]{1,0:T(8,128)} %get-tuple-element.118) | copy-start | bytes 2654212
  103.0 9.4 %all-to-all-start.2 = ((bf16[4,160,128]{2,1,0:T(8,128)(2,1)}), bf16[4,160,128]{2,1,0:T(8,128)(2,1)S(1)}, u32[]{:S(2)}, u32[]{:S(2)}) async-start(bf16[4,160,128]{2,1,0:T(8,128)(2,1)} %broadcast_in_dim.96), calls=%async_computation.3 | async-start | bytes 327680 | tf_op jit(solution)/shard_map/all_to_all | solution.py:147
  113.1 23.0 %all-to-all-start.3 = ((bf16[4,160,128]{2,1,0:T(8,128)(2,1)}), bf16[4,160,128]{2,1,0:T(8,128)(2,1)S(1)}, u32[]{:S(2)}, u32[]{:S(2)}) async-start(bf16[4,160,128]{2,1,0:T(8,128)(2,1)} %broadcast_in_dim.97), calls=%async_computation.4 | async-start | bytes 327680 | tf_op jit(solution)/shard_map/all_to_all | solution.py:147
  123.8 44.6 %reduce-scatter.2.cloned.1.call-start = ((), (), s32[]{:S(2)}) async-start(), calls=%async_computation.7 | async-start | bytes 1437696 | tf_op jit(solution)/shard_map/reduce_scatter | solution.py:204
  (53 other events, 230.1 us)
Sparse Core Ops, SparseCore 0:
  10.1 37.4 all-gather.3
  128.0 40.3 reduce-scatter.1

commit v2 on v1

v2 whole, which is shorter than its diff:
```python
import math

import jax
import jax.numpy as jnp
from jax import lax
from jax.experimental import pallas as pl
from jax.experimental.pallas import tpu as pltpu
from jax.sharding import Mesh
from jax.sharding import PartitionSpec as P

WIDTH = 384
INNER = 768
KERNEL = 7
REACH = KERNEL // 2
PATCH_CH = 48
TILE = 8
MEAN_TILES = 3
SLOTS = 9
FEAT_TILE = 16
N_OWNERS = 512
N_DEC = 8
SHARD = 208
SEQ = N_DEC * SHARD
POSITIONS = SLOTS * TILE * TILE
BLOCK_ROWS = SLOTS * FEAT_TILE
LANES = 128
CHUNKS = WIDTH // LANES
UP_AT = 0
DOWN_AT = UP_AT + (INNER // LANES) * WIDTH
STEM_AT = DOWN_AT + CHUNKS * INNER
SMALL_AT = STEM_AT + CHUNKS * PATCH_CH
SMALL_ROWS = 64
PACK_USED = SMALL_AT + CHUNKS * SMALL_ROWS
PACK_ROWS = 5120
HALF_ROWS = PACK_ROWS // 2
DEC = ("y", "core")
ENC = ("x", "zh", "zl")
PLANE = ("x", "y")
VMEM_BYTES = 50 * 1024 * 1024

epsilon = 1e-06
GELU_A = math.sqrt(2.0 / math.pi)
GELU_B = 0.044715
bf16 = jnp.bfloat16
f32 = jnp.float32


def lanes(chunk):
    return slice(chunk * LANES, (chunk + 1) * LANES)


def column_shift(rows, step):
    if step == 0:
        return rows
    column = lax.broadcasted_iota(jnp.int32, (TILE, LANES), 0) + step
    inside = (column >= 0) & (column < TILE)
    return [jnp.where(inside, pltpu.roll(row, (-step) % TILE, 0), 0.0) for row in rows]


def depthwise(rows, kernel_ref, chunk, sign):
    out = [jnp.zeros((TILE, LANES), f32)] * TILE
    for col_tap in range(KERNEL):
        moved = column_shift(rows, sign * (col_tap - REACH))
        for row_tap in range(KERNEL):
            tap = row_tap * KERNEL + col_tap
            weight = jnp.broadcast_to(kernel_ref[tap : tap + 1, lanes(chunk)], (TILE, LANES))
            for i in range(TILE):
                source = i + sign * (row_tap - REACH)
                if 0 <= source < TILE:
                    out[i] = out[i] + moved[source] * weight
    return out


def forward_kernel(
    count_ref, patches_ref, stem_w_ref, depth_w_ref, gain_ref, up_ref, down_ref, layer_ref,
    stem_ref, centred_ref, inv_ref, hidden_ref, projected_ref, feat_ref,
    taps_ref, field_ref, mixed_ref, normed_ref, act_ref, pool_ref,
):
    taps_ref[...] = depth_w_ref[...].astype(f32)
    stem = jnp.dot(patches_ref[...], stem_w_ref[...], preferred_element_type=f32).astype(bf16)
    stem_ref[...] = stem
    field_ref[...] = stem.astype(f32).reshape(SLOTS * TILE, TILE, WIDTH)
    gain = gain_ref[...]

    def mix(t, carry):
        first = t * TILE
        for chunk in range(CHUNKS):
            rows = [field_ref[first + i, :, lanes(chunk)] for i in range(TILE)]
            out = depthwise(rows, taps_ref, chunk, 1)
            for i in range(TILE):
                mixed_ref[i, :, lanes(chunk)] = out[i]
        for i in range(0, TILE, 2):
            row = mixed_ref[i : i + 2].reshape(2 * TILE, WIDTH)
            deviation = row - jnp.mean(row, axis=1, keepdims=True)
            inv_std = lax.rsqrt(jnp.mean(deviation * deviation, axis=1, keepdims=True) + epsilon)
            centred = deviation * inv_std
            at = pl.ds(pl.multiple_of((first + i) * TILE, 2 * TILE), 2 * TILE)
            centred_ref[at, :] = centred
            inv_ref[at, :] = jnp.broadcast_to(inv_std, (2 * TILE, LANES))
            normed_ref[at, :] = (centred * gain).astype(bf16)
        return carry

    lax.fori_loop(0, SLOTS, mix, 0)
    normed = normed_ref[...]
    for n in range(0, INNER, 256):
        hidden_ref[:, n : n + 256] = jnp.dot(
            normed, up_ref[:, n : n + 256], preferred_element_type=f32
        )

    def activate(r, carry):
        at = pl.ds(pl.multiple_of(r * 16, 16), 16)
        v = hidden_ref[at, :]
        t = jnp.tanh(GELU_A * (v + GELU_B * (v * v * v)))
        act_ref[at, :] = (0.5 * v * (1.0 + t)).astype(bf16)
        return carry

    lax.fori_loop(0, POSITIONS // 16, activate, 0)
    projected_ref[...] = jnp.dot(act_ref[...], down_ref[...], preferred_element_type=f32)
    layer = layer_ref[...]
    count = count_ref[0]

    def pool(t, carry):
        keep = jnp.where(t < count, 0.25, 0.0).astype(f32)
        for pair in range(TILE // 2):
            total = None
            for half in range(2):
                i = t * TILE + 2 * pair + half
                at = pl.ds(pl.multiple_of(i * TILE, TILE), TILE)
                block = field_ref[i] + layer * projected_ref[at, :]
                total = block if total is None else total + block
            total = (total + pltpu.roll(total, TILE - 1, 0)) * keep
            for chunk in range(CHUNKS):
                pool_ref[chunk, pair * TILE : (pair + 1) * TILE, :] = total[:, lanes(chunk)]
        at = pl.ds(pl.multiple_of(t * FEAT_TILE, FEAT_TILE), FEAT_TILE)
        for chunk in range(CHUNKS):
            pooled = pool_ref[chunk, pl.ds(0, FEAT_TILE, stride=2), :].astype(bf16)
            for d in range(N_DEC):
                feat_ref[d, at, lanes(chunk)] = pooled
        return carry

    lax.fori_loop(0, SLOTS, pool, 0)


def forward(count, patches, stem_w, depth_w, gain, up, down, layer):
    vmem = pl.BlockSpec(memory_space=pltpu.VMEM)
    shapes = (
        ((POSITIONS, WIDTH), bf16),
        ((POSITIONS, WIDTH), f32),
        ((POSITIONS, LANES), f32),
        ((POSITIONS, INNER), f32),
        ((POSITIONS, WIDTH), f32),
        ((N_DEC, BLOCK_ROWS, WIDTH), bf16),
    )
    return pl.pallas_call(
        forward_kernel,
        out_shape=[jax.ShapeDtypeStruct(*shape) for shape in shapes],
        in_specs=[pl.BlockSpec(memory_space=pltpu.SMEM)] + [vmem] * 7,
        out_specs=[vmem] * 6,
        scratch_shapes=[
            pltpu.VMEM((KERNEL * KERNEL, WIDTH), f32),
            pltpu.VMEM((SLOTS * TILE, TILE, WIDTH), f32),
            pltpu.VMEM((TILE, TILE, WIDTH), f32),
            pltpu.VMEM((POSITIONS, WIDTH), bf16),
            pltpu.VMEM((POSITIONS, INNER), bf16),
            pltpu.VMEM((CHUNKS, TILE // 2 * TILE, LANES), f32),
        ],
        compiler_params=pltpu.CompilerParams(vmem_limit_bytes=VMEM_BYTES),
        cost_estimate=pl.CostEstimate(
            flops=4 * POSITIONS * WIDTH * INNER, bytes_accessed=8 << 20, transcendentals=0
        ),
        name="block_forward",
    )(count, patches, stem_w, depth_w, gain, up, down, layer)


def rows_times_rows(a, b):
    return lax.dot_general(a, b, (((1,), (1,)), ((), ())), preferred_element_type=f32)


def over_positions(a, b):
    return lax.dot_general(a, b, (((0,), (0,)), ((), ())), preferred_element_type=f32)


def backward_kernel(
    place_ref, count_ref, own_ref, other_ref, patches_ref, stem_ref, centred_ref, inv_ref,
    hidden_ref, projected_ref, depth_w_ref, gain_ref, up_ref, down_ref, layer_ref,
    packed_ref, spans_ref,
    taps_ref, embed_ref, block_ref, proj_ref, act_ref, work_ref, ghid_ref, normed_ref,
    mixed_ref, gstem_ref, taps_sum_ref, rows_sum_ref,
):
    y_here, core_here = place_ref[0], place_ref[1]
    dec_here = 2 * y_here + core_here
    taps_ref[...] = depth_w_ref[...].astype(f32)
    counts, gaps = [None] * N_DEC, [None] * N_DEC
    for y in range(N_DEC // 2):
        embed_ref[pl.ds(pl.multiple_of((2 * y + core_here) * SHARD, 16), SHARD), :] = own_ref[y, :SHARD, :]
        embed_ref[pl.ds(pl.multiple_of((2 * y + 1 - core_here) * SHARD, 16), SHARD), :] = other_ref[y, :SHARD, :]
        mine = own_ref[y, SHARD:, :LANES].astype(f32)
        theirs = other_ref[y, SHARD:, :LANES].astype(f32)
        for core in range(2):
            tail = jnp.where(core_here == core, mine, theirs)
            counts[2 * y + core] = tail[0, 0].astype(jnp.int32)
            gaps[2 * y + core] = tail[0, 1].astype(jnp.int32)
    embed_ref[SEQ:, :] = jnp.zeros((16, WIDTH), bf16)
    at, own_offset = jnp.int32(0), jnp.int32(0)
    for d in range(N_DEC):
        start = at + gaps[d]
        spans_ref[d] = start
        spans_ref[N_DEC + d] = counts[d]
        own_offset = jnp.where(dec_here == d, start, own_offset)
        at = start + FEAT_TILE * counts[d]
    count = count_ref[0]
    layer = layer_ref[...]
    gain = gain_ref[...]
    rows_sum_ref[...] = jnp.zeros((2, TILE, WIDTH), f32)
    taps_sum_ref[...] = jnp.zeros((KERNEL * KERNEL, TILE, WIDTH), f32)

    def spread_tile(t, carry):
        start = own_offset + FEAT_TILE * t
        base = lax.div(start, 16)
        row = lax.broadcasted_iota(jnp.int32, (64, 32), 0)
        col = lax.broadcasted_iota(jnp.int32, (64, 32), 1)
        feat = lax.shift_right_logical(row, 4) * 4 + (lax.shift_right_logical(row, 1) & 3)
        hit = (col == feat + (start - 16 * base)) & (t < count)
        pick = jnp.where(hit, 0.25, 0.0).astype(bf16)
        window = embed_ref[pl.ds(pl.multiple_of(base * 16, 16), 32), :]
        block = jnp.dot(pick, window, preferred_element_type=f32)
        at = pl.ds(pl.multiple_of(t * 64, 64), 64)
        block_ref[at, :] = block
        proj_ref[at, :] = (block * layer).astype(bf16)
        product = block * projected_ref[at, :]
        rows_sum_ref[0] += jnp.sum(product.reshape(TILE, TILE, WIDTH), axis=0)
        normed_ref[at, :] = (centred_ref[at, :] * gain).astype(bf16)
        return carry

    lax.fori_loop(0, SLOTS, spread_tile, 0)
    proj = proj_ref[...]
    for n in range(0, INNER, 256):
        work_ref[:, n : n + 256] = rows_times_rows(proj, down_ref[n : n + 256, :])

    def activate(r, carry):
        at = pl.ds(pl.multiple_of(r * 16, 16), 16)
        v = hidden_ref[at, :]
        square = v * v
        t = jnp.tanh(GELU_A * (v + GELU_B * (square * v)))
        half = 0.5 * (1.0 + t)
        act_ref[at, :] = (v * half).astype(bf16)
        slope = half + (0.5 * GELU_A) * v * (1.0 - t * t) * (1.0 + (3.0 * GELU_B) * square)
        ghid_ref[at, :] = (work_ref[at, :] * slope).astype(bf16)
        return carry

    lax.fori_loop(0, POSITIONS // 16, activate, 0)
    for n in range(0, INNER, 256):
        term = over_positions(act_ref[:, n : n + 256], proj).astype(bf16)
        for chunk in range(CHUNKS):
            to = DOWN_AT + chunk * INNER + n
            packed_ref[to : to + 256, :] = term[:, lanes(chunk)]
    normed = normed_ref[...]
    for n in range(0, INNER, 256):
        term = over_positions(normed, ghid_ref[:, n : n + 256]).astype(bf16)
        for k in range(2):
            to = UP_AT + (n // LANES + k) * WIDTH
            packed_ref[to : to + WIDTH, :] = term[:, lanes(k)]
    work_ref[:, :WIDTH] = rows_times_rows(ghid_ref[...], up_ref[...])

    def unmix(t, carry):
        gain_sum = jnp.zeros((TILE, WIDTH), f32)
        for i in range(0, TILE, 2):
            at = pl.ds(pl.multiple_of((t * TILE + i) * TILE, 2 * TILE), 2 * TILE)
            grad = work_ref[at, :WIDTH]
            centred = centred_ref[at, :]
            gain_sum += jnp.sum((grad * centred).reshape(2, TILE, WIDTH), axis=0)
            scaled = grad * gain
            mean = jnp.mean(scaled, axis=1, keepdims=True)
            mean_c = jnp.mean(scaled * centred, axis=1, keepdims=True)
            mixed = (scaled - mean - centred * mean_c) * inv_ref[at, :1]
            mixed_ref[i : i + 2] = mixed.reshape(2, TILE, WIDTH)
        rows_sum_ref[1] += gain_sum
        for chunk in range(CHUNKS):
            grads = [mixed_ref[i, :, lanes(chunk)] for i in range(TILE)]
            stem = []
            for i in range(0, TILE, 2):
                at = pl.ds(pl.multiple_of((t * TILE + i) * TILE, 2 * TILE), 2 * TILE)
                pair = stem_ref[at, lanes(chunk)].astype(f32)
                stem += [pair[:TILE], pair[TILE:]]
            for col_tap in range(KERNEL):
                moved = column_shift(stem, col_tap - REACH)
                for row_tap in range(KERNEL):
                    total = None
                    for i in range(TILE):
                        source = i + row_tap - REACH
                        if 0 <= source < TILE:
                            part = moved[source] * grads[i]
                            total = part if total is None else total + part
                    taps_sum_ref[row_tap * KERNEL + col_tap, :, lanes(chunk)] += total
            inner = depthwise(grads, taps_ref, chunk, -1)
            for i in range(0, TILE, 2):
                at = pl.ds(pl.multiple_of((t * TILE + i) * TILE, 2 * TILE), 2 * TILE)
                block = block_ref[at, lanes(chunk)]
                pair = jnp.concatenate([inner[i], inner[i + 1]], axis=0)
                gstem_ref[at, lanes(chunk)] = (block + pair).astype(bf16)
        return carry

    lax.fori_loop(0, SLOTS, unmix, 0)
    stem_term = over_positions(patches_ref[...], gstem_ref[...]).astype(bf16)
    small = jnp.concatenate(
        [
            jnp.sum(taps_sum_ref[...], axis=1),
            jnp.sum(rows_sum_ref[...], axis=1),
            jnp.zeros((SMALL_ROWS - KERNEL * KERNEL - 2, WIDTH), f32),
        ],
        axis=0,
    ).astype(bf16)
    for chunk in range(CHUNKS):
        to = STEM_AT + chunk * PATCH_CH
        packed_ref[to : to + PATCH_CH, :] = stem_term[:, lanes(chunk)]
        to = SMALL_AT + chunk * SMALL_ROWS
        packed_ref[to : to + SMALL_ROWS, :] = small[:, lanes(chunk)]
    packed_ref[PACK_USED:, :] = jnp.zeros((PACK_ROWS - PACK_USED, LANES), bf16)


def backward(place, count, own, other, patches, stored, depth_w, gain, up, down, layer):
    vmem = pl.BlockSpec(memory_space=pltpu.VMEM)
    smem = pl.BlockSpec(memory_space=pltpu.SMEM)
    return pl.pallas_call(
        backward_kernel,
        out_shape=[
            jax.ShapeDtypeStruct((PACK_ROWS, LANES), bf16),
            jax.ShapeDtypeStruct((2 * N_DEC,), jnp.int32),
        ],
        in_specs=[smem, smem] + [vmem] * 13,
        out_specs=[vmem, smem],
        scratch_shapes=[
            pltpu.VMEM((KERNEL * KERNEL, WIDTH), f32),
            pltpu.VMEM((SEQ + 16, WIDTH), bf16),
            pltpu.VMEM((POSITIONS, WIDTH), f32),
            pltpu.VMEM((POSITIONS, WIDTH), bf16),
            pltpu.VMEM((POSITIONS, INNER), bf16),
            pltpu.VMEM((POSITIONS, INNER), f32),
            pltpu.VMEM((POSITIONS, INNER), bf16),
            pltpu.VMEM((POSITIONS, WIDTH), bf16),
            pltpu.VMEM((TILE, TILE, WIDTH), f32),
            pltpu.VMEM((POSITIONS, WIDTH), bf16),
            pltpu.VMEM((KERNEL * KERNEL, TILE, WIDTH), f32),
            pltpu.VMEM((2, TILE, WIDTH), f32),
        ],
        compiler_params=pltpu.CompilerParams(vmem_limit_bytes=VMEM_BYTES),
        cost_estimate=pl.CostEstimate(
            flops=8 * POSITIONS * WIDTH * INNER, bytes_accessed=10 << 20, transcendentals=0
        ),
        name="block_backward",
    )(place, count, own, other, patches, *stored, depth_w, gain, up, down, layer)


def place_kernel(place_ref, spans_ref, feat_ref, out_ref, rows_ref):
    base = (2 * place_ref[0] + place_ref[1]) * SHARD
    rows_ref[...] = jnp.zeros((FEAT_TILE + SHARD + FEAT_TILE, WIDTH), f32)

    def one(k, carry):
        d = lax.div(k, SLOTS)
        j = k - d * SLOTS
        to = spans_ref[d] + FEAT_TILE * j - base

        @pl.when((j < spans_ref[N_DEC + d]) & (to > -FEAT_TILE) & (to < SHARD))
        def _():
            at = pl.ds(pl.multiple_of(j * FEAT_TILE, FEAT_TILE), FEAT_TILE)
            chunk = lax.div(to + FEAT_TILE, 16)
            row = lax.broadcasted_iota(jnp.int32, (32, FEAT_TILE), 0)
            col = lax.broadcasted_iota(jnp.int32, (32, FEAT_TILE), 1)
            pick = jnp.where(row == col + (to + FEAT_TILE - 16 * chunk), 1.0, 0.0).astype(bf16)
            window = pl.ds(pl.multiple_of(chunk * 16, 16), 32)
            rows_ref[window, :] += jnp.dot(pick, feat_ref[d, at, :], preferred_element_type=f32)

        return carry

    lax.fori_loop(0, N_DEC * SLOTS, one, 0)
    out_ref[...] = rows_ref[FEAT_TILE : FEAT_TILE + SHARD, :].astype(bf16)


def place_features(place, spans, feat):
    vmem = pl.BlockSpec(memory_space=pltpu.VMEM)
    smem = pl.BlockSpec(memory_space=pltpu.SMEM)
    return pl.pallas_call(
        place_kernel,
        out_shape=jax.ShapeDtypeStruct((SHARD, WIDTH), bf16),
        in_specs=[smem, smem, vmem],
        out_specs=vmem,
        scratch_shapes=[pltpu.VMEM((FEAT_TILE + SHARD + FEAT_TILE, WIDTH), f32)],
        compiler_params=pltpu.CompilerParams(vmem_limit_bytes=VMEM_BYTES),
        name="place_features",
    )(place, spans, feat)


def unpack_kernel(
    place_ref, own_ref, other_ref, stem_ref, depth_ref, gain_ref, up_ref, down_ref, scale_ref, rows_ref
):
    core = place_ref[1]
    factor = 1.0 / math.sqrt(N_OWNERS * MEAN_TILES * FEAT_TILE)
    rows_ref[pl.ds(pl.multiple_of(core * HALF_ROWS, 16), HALF_ROWS), :] = own_ref[...]
    rows_ref[pl.ds(pl.multiple_of((1 - core) * HALF_ROWS, 16), HALF_ROWS), :] = other_ref[...]

    def piece(at, count):
        return rows_ref[at : at + count, :].astype(f32) * factor

    for k in range(INNER // LANES):
        up_ref[:, lanes(k)] = piece(UP_AT + k * WIDTH, WIDTH)
    for chunk in range(CHUNKS):
        down_ref[:, lanes(chunk)] = piece(DOWN_AT + chunk * INNER, INNER)
        stem_ref[:, lanes(chunk)] = piece(STEM_AT + chunk * PATCH_CH, PATCH_CH)
        small = piece(SMALL_AT + chunk * SMALL_ROWS, SMALL_ROWS)
        taps = KERNEL * KERNEL
        depth_ref[:, lanes(chunk)] = small[:taps]
        scale_ref[:, lanes(chunk)] = small[taps : taps + 1]
        gain_ref[:, lanes(chunk)] = small[taps + 1 : taps + 2]


def unpack(place, own, other):
    vmem = pl.BlockSpec(memory_space=pltpu.VMEM)
    smem = pl.BlockSpec(memory_space=pltpu.SMEM)
    shapes = (
        (PATCH_CH, WIDTH),
        (KERNEL * KERNEL, WIDTH),
        (1, WIDTH),
        (WIDTH, INNER),
        (INNER, WIDTH),
        (1, WIDTH),
    )
    return pl.pallas_call(
        unpack_kernel,
        out_shape=[jax.ShapeDtypeStruct(shape, f32) for shape in shapes],
        in_specs=[smem, vmem, vmem],
        out_specs=[vmem] * 6,
        scratch_shapes=[pltpu.VMEM((PACK_ROWS, LANES), bf16)],
        compiler_params=pltpu.CompilerParams(vmem_limit_bytes=VMEM_BYTES),
        name="unpack_terms",
    )(place, own, other)


def swap_blocks(blocks, axes):
    return lax.all_to_all(blocks, axes, 0, 0, tiled=True)


def sum_blocks(blocks):
    return jnp.sum(blocks.astype(f32), axis=0).astype(bf16)


def spread(block, copies):
    return jnp.broadcast_to(block[None], (copies,) + block.shape)


def swap_cores(x):
    return lax.ppermute(x, "core", [(0, 1), (1, 0)])


def sum_all(packed):
    half = sum_blocks(swap_blocks(packed.reshape(2, HALF_ROWS, LANES), "core"))
    part = sum_blocks(swap_blocks(half.reshape(16, PACK_ROWS // 32, LANES), PLANE))
    part = sum_blocks(swap_blocks(spread(part, 4), "zl"))
    part = sum_blocks(swap_blocks(spread(part, 4), "zh"))
    return swap_blocks(spread(part, 16), PLANE).reshape(HALF_ROWS, LANES)


def on_device(
    pixels,
    tile_counts,
    text_gaps,
    stem_weight,
    depth_weight,
    norm_gain,
    up_weight,
    down_weight,
    layer_scale,
    embed_grad,
):
    place = jnp.stack([lax.axis_index("y"), lax.axis_index("core")]).astype(jnp.int32)
    count = tile_counts.reshape(1)
    gain = norm_gain.reshape(1, WIDTH)
    layer = layer_scale.reshape(1, WIDTH)
    patches = pixels.reshape(POSITIONS, PATCH_CH)
    numbers = jnp.concatenate([tile_counts, text_gaps], axis=1).astype(bf16)
    tail = jnp.pad(numbers, ((0, 7), (0, WIDTH - 2)))
    own = swap_blocks(spread(jnp.concatenate([embed_grad[0], tail]), 4), "y")
    *stored, feat = forward(
        count, patches, stem_weight, depth_weight, gain, up_weight, down_weight, layer
    )
    other = swap_cores(own)
    feats = swap_blocks(feat, DEC)
    packed, spans = backward(
        place, count, own, other, patches, stored, depth_weight, gain, up_weight, down_weight, layer
    )
    half = sum_all(packed)
    stem, depth, gain_grad, up, down, scale = unpack(place, half, swap_cores(half))
    sequence = place_features(place, spans, feats)
    return (
        sequence[None],
        stem,
        depth,
        gain_grad.reshape(WIDTH),
        up,
        down,
        scale.reshape(WIDTH),
    )


def solution(mesh):
    fine = Mesh(mesh.devices.reshape(4, 4, 4, 4, 2), ("x", "zh", "zl", "y", "core"))
    return jax.shard_map(
        on_device,
        mesh=fine,
        in_specs=(
            P(DEC, ENC, None),
            P(DEC, ENC),
            P(DEC, ENC),
            P(),
            P(),
            P(),
            P(),
            P(),
            P(),
            P(ENC, DEC, None),
        ),
        out_specs=(P(ENC, DEC, None), P(), P(), P(), P(), P(), P()),
        check_vma=False,
    )
```

time: 178 us -> 149 us (0.84); the launches traced: 175 us -> 149 us
  Pallas kernels: 0 us -> 29.1 us
  blocking collectives: 55.2 us -> 81.2 us
  other arithmetic: 23.2 us -> 3.18 us
  local copies, waits for them, and re-layouts: 22 us -> 2.23 us
  between operations: 19.6 us -> 2.16 us
  matrix products: 14.5 us -> 0 us
  waiting for transfers between devices: 25.6 us -> 11.3 us
  starting transfers between devices: 15.3 us -> 19.5 us
    all_to_all x4 -> x6, blocking collectives: 46.2 us -> 81.2 us  [swap_blocks(): return lax.all_to_all(blocks, axes, 0, 0, tiled=True)]
    pallas_call x0 -> x4, Pallas kernels: none -> 29.1 us  [the longest x1 14.8 us: backward(): pl.pallas_call(backward_kernel, out_shape=[jax.ShapeDtypeStruct((PACK_ROW...]
    dot_general x8 -> x0, matrix products: 14.5 us -> none  [the longest x1 3.22 us: backward_head(): lax.dot_general(grad_proj, down_weight, (((1,), (1,)), ((), ())), preferr...]
    reduce_sum x11 -> x4, other arithmetic: 13.7 us -> 0.81 us  [sum_blocks(): return jnp.sum(blocks.astype(f32), axis=0).astype(bf16)]
    all_gather x1 -> x0, waiting for transfers between devices: 10.6 us -> none  [on_device(): gathered = lax.all_gather(embed_grad[0], DEC, axis=0, tiled=True)]
    ppermute x0 -> x2, starting transfers between devices: none -> 9.53 us  [swap_cores(): return lax.ppermute(x, 'core', [(0, 1), (1, 0)])]
    reshape x12 -> x3, local copies, waits for them, and re-layouts: 9.58 us -> 0.18 us  [the longest x1 0.17 us: on_device(): patches = pixels.reshape(POSITIONS, PATCH_CH)]
    unnamed x1 -> x0, blocking collectives: 9 us -> none
  transfers between devices with their start and end apart: 4 -> 3, of which waited for: 4 -> 1; matrix products, arithmetic and copies ran while one was open for 14% -> 0% of each run, Pallas kernels for 0% -> 8%
where the time goes in v2:
time: 149 us
  blocking collectives  81.2 us (54%)
  Pallas kernels  29.1 us (20%)
  starting transfers between devices  19.5 us (13%)
  waiting for transfers between devices  11.3 us (8%)
  other arithmetic  3.18 us (2%)
  local copies, waits for them, and re-layouts  2.23 us (1%)
  between operations  2.16 us (1%)
    all_to_all x6, blocking collectives, swap_blocks(): return lax.all_to_all(blocks, axes, 0, 0, tiled=True)  81.2 us
    pallas_call x1, Pallas kernels, backward(): pl.pallas_call(backward_kernel, out_shape=[jax.ShapeDtypeStruct((PACK_ROW...  14.8 us
    all_to_all x1, waiting for transfers between devices, swap_blocks(): return lax.all_to_all(blocks, axes, 0, 0, tiled=True)  11.3 us
    all_to_all x1, starting transfers between devices, swap_blocks(): return lax.all_to_all(blocks, axes, 0, 0, tiled=True)  9.92 us
    ppermute x2, starting transfers between devices, swap_cores(): return lax.ppermute(x, 'core', [(0, 1), (1, 0)])  9.53 us
    pallas_call x1, Pallas kernels, forward(): pl.pallas_call(forward_kernel, out_shape=[jax.ShapeDtypeStruct(*shape) fo...  9.07 us
    pallas_call x1, Pallas kernels, place_features(): pl.pallas_call(place_kernel, out_shape=jax.ShapeDtypeStruct((SHARD, WIDTH...  3.02 us
  transfers between devices with their start and end apart: 3, of which 1 were waited for; matrix products, arithmetic and copies ran while one was open for 0% of the time, Pallas kernels for 8%

profile of v2, /device:TPU:1, one launch (start us, length us, event | category | flops | bytes accessed | tf_op | source)
XLA Modules:
  0.0 148.6 jit_solution(10706968677408580878)
XLA Ops:
  2.0 0.1 fusion.5
  2.1 1.0 pad_maximum_fusion
  3.2 12.5 %all_to_all.35.own_ref = bf16[4,216,384]{2,1,0:T(8,128)(2,1)S(1)} all-to-all(bf16[4,216,384]{2,1,0:T(8,128)(2,1)S(1)} %broadcast_in_dim.10), channel_id=1, replica_groups=mesh['x'=4,'zh'=4,'zl'=4,'y'=4,'core'=2] {'y'}, dimensions={0} | all-to-all | bytes 1327104 | tf_op jit(solution)/shard_map/all_to_all | solution.py:439
  15.7 7.5 %collective-permute-start = (bf16[4,216,384]{2,1,0:T(8,128)(2,1)S(1)}, bf16[4,216,384]{2,1,0:T(8,128)(2,1)S(1)}, u32[]{:S(2)}, u32[]{:S(2)}) collective-permute-start(bf16[4,216,384]{2,1,0:T(8,128)(2,1)S(1)} %all_to_all.35.own_ref), channel_id=1, source_target_pairs={{0,1},{1,0},{2,3},{3,2},{4,5},{5,4},{6,7},{7,6},{8,9},{9,8},{10,11... | collective-permute-start | bytes 1990664 | tf_op jit(solution)/shard_map/ppermute | solution.py:451
  23.3 0.2 reshape.74.patches_ref
  23.5 9.1 %block_forward.1 = (bf16[576,384]{1,0:T(8,128)(2,1)S(1)}, f32[576,384]{1,0:T(8,128)S(1)}, f32[576,128]{1,0:T(8,128)S(1)}, f32[576,768]{1,0:T(8,128)}, f32[576,38...) custom-call(s32[1]{0:T(128)} %bitcast.8.count_ref, bf16[576,48]{1,0:T(8,128)(2,1)S(1)} %reshape.74.patches_ref, ...), custom_call_target="tpu_custom_call" | custom-call | flops 679477248 | bytes 8388608 | tf_op jit(solution)/shard_map/block_forward/pallas_call | solution.py:154
  32.6 0.9 copy-done
  33.5 0.9 copy-done.1
  34.5 14.8 %block_backward.1 = (bf16[5120,128]{1,0:T(8,128)(2,1)}, s32[16]{0:T(128)S(1)}) custom-call(s32[2]{0:T(128)S(1)} %pad_add_fusion.place_ref, s32[1]{0:T(128)} %bitcast.9.count_ref, bf16[4,216,384]{2,1,0:T(8,128)(2,1)S(1)} %all_to_all.35.own_ref, bf16[4,216,384]{2,1,0:T(8,128)(2,1)S(1)} %collective-permute-done.other_ref, ...), custom_call_target="tpu_custom_call" | custom-call | flops 1358954496 | bytes 10485760 | tf_op jit(solution)/shard_map/block_backward/pallas_call | solution.py:324
  49.3 5.6 %all_to_all.36 = bf16[2,2560,128]{2,1,0:T(8,128)(2,1)S(1)} all-to-all(bf16[2,2560,128]{2,1,0:T(8,128)(2,1)} %bitcast.13), channel_id=1, replica_groups=mesh['x'=4,'zh'=4,'zl'=4,'y'=4,'core'=2] {'core'}, dimensions={0} | all-to-all | bytes 2621440 | tf_op jit(solution)/shard_map/all_to_all | solution.py:439
  54.9 0.7 reduce_sum.48
  55.5 15.1 %all_to_all.37 = bf16[16,160,128]{2,1,0:T(8,128)(2,1)S(1)} all-to-all(bf16[16,160,128]{2,1,0:T(8,128)(2,1)S(1)} %bitcast.12), channel_id=1, replica_groups=mesh['x'=4,'zh'=4,'zl'=4,'y'=4,'core'=2] {'x','y'}, dimensions={0} | all-to-all | bytes 1310720 | tf_op jit(solution)/shard_map/all_to_all | solution.py:439
  70.7 0.1 reduce_sum.49
  70.8 11.0 %all_to_all.38 = bf16[4,160,128]{2,1,0:T(8,128)(2,1)S(1)} all-to-all(bf16[4,160,128]{2,1,0:T(8,128)(2,1)S(1)} %broadcast_in_dim.12), channel_id=1, replica_groups=mesh['x'=4,'zh'=4,'zl'=4,'y'=4,'core'=2] {'zl'}, dimensions={0} | all-to-all | bytes 327680 | tf_op jit(solution)/shard_map/all_to_all | solution.py:439
  81.9 24.2 %all_to_all.39 = bf16[4,160,128]{2,1,0:T(8,128)(2,1)S(1)} all-to-all(bf16[4,160,128]{2,1,0:T(8,128)(2,1)S(1)} %broadcast_in_dim.13), channel_id=1, replica_groups=mesh['x'=4,'zh'=4,'zl'=4,'y'=4,'core'=2] {'zh'}, dimensions={0} | all-to-all | bytes 327680 | tf_op jit(solution)/shard_map/all_to_all | solution.py:439
  106.1 0.1 broadcast_in_dim.14
  106.2 12.8 %all_to_all.40 = bf16[16,160,128]{2,1,0:T(8,128)(2,1)S(1)} all-to-all(bf16[16,160,128]{2,1,0:T(8,128)(2,1)S(1)} %broadcast_in_dim.14), channel_id=1, replica_groups=mesh['x'=4,'zh'=4,'zl'=4,'y'=4,'core'=2] {'x','y'}, dimensions={0} | all-to-all | bytes 1310720 | tf_op jit(solution)/shard_map/all_to_all | solution.py:439
  119.0 9.9 %all-to-all-start.1 = ((bf16[8,144,384]{2,1,0:T(8,128)(2,1)}), bf16[8,144,384]{2,1,0:T(8,128)(2,1)S(1)}, u32[]{:S(2)}, u32[]{:S(2)}) async-start(bf16[8,144,384]{2,1,0:T(8,128)(2,1)} %get-tuple-element.27), calls=%async_computation.1 | async-start | bytes 1769472 | tf_op jit(solution)/shard_map/all_to_all | solution.py:439
  128.9 2.0 %collective-permute-start.1 = (bf16[2560,128]{1,0:T(8,128)(2,1)S(1)}, bf16[2560,128]{1,0:T(8,128)(2,1)S(1)}, u32[]{:S(2)}, u32[]{:S(2)}) collective-permute-start(bf16[2560,128]{1,0:T(8,128)(2,1)S(1)} %bitcast.10), channel_id=1, source_target_pairs={{0,1},{1,0},{2,3},{3,2},{4,5},{5,4},{6,7},{7,6},{8,9},{9,8},{10,11... | collective-permute-start | bytes 1966088 | tf_op jit(solution)/shard_map/ppermute | solution.py:451
  130.9 11.3 %all-to-all-done.1.feat_ref = bf16[8,144,384]{2,1,0:T(8,128)(2,1)S(1)} async-done(((bf16[8,144,384]{2,1,0:T(8,128)(2,1)}), bf16[8,144,384]{2,1,0:T(8,128)(2,1)S(1)}, u32[]{:S(2)}, u32[]{:S(2)}) %all-to-all-start.1) | async-done | bytes 884768 | tf_op jit(solution)/shard_map/all_to_all | solution.py:439
  142.3 3.0 %place_features.1 = bf16[208,384]{1,0:T(8,128)(2,1)} custom-call(s32[2]{0:T(128)S(1)} %pad_add_fusion.place_ref, s32[16]{0:T(128)S(1)} %get-tuple-element.26.spans_ref, bf16[8,144,384]{2,1,0:T(8,128)(2,1)S(1)} %all-to-all-done.1.feat_ref), custom_call_target="tpu_custom_call" | custom-call | tf_op jit(solution)/shard_map/place_features/pallas_call | solution.py:382
  145.3 2.1 %unpack_terms.1 = (f32[48,384]{1,0:T(8,128)}, f32[49,384]{1,0:T(8,128)}, f32[1,384]{1,0:T(1,128)S(1)}, f32[384,768]{1,0:T(8,128)}, f32[768,384]{1,0:T(8,128)}, /*index=5*/f32[1,384]{1,0:T(1,128)S(1)}) custom-call(s32[2]{0:T(128)S(1)} %pad_add_fusion.place_ref, bf16[2560,128]{1,0:T(8,128)(2,1)S(1)} %bitcast.11, ...), custom_call_target="tpu_custom_call" | custom-call | tf_op jit(solution)/shard_map/unpack_terms/pallas_call | solution.py:427
  147.4 0.6 reduce.4
  148.0 0.6 reduce.5
  (26 shorter events, 0.3 us)
Async XLA Ops:
  0.6 22.6 %copy-start.7 = (f32[384]{0:T(512)S(1)}, f32[384]{0:T(512)}, u32[]{:S(2)}) copy-start(f32[384]{0:T(512)} %param.15) | copy-start | bytes 4612
  0.6 22.6 %copy-start.8 = (f32[384]{0:T(512)S(1)}, f32[384]{0:T(512)}, u32[]{:S(2)}) copy-start(f32[384]{0:T(512)} %param.18) | copy-start | bytes 4612
  0.7 22.6 %copy-start.6 = (bf16[1,9,3072]{2,1,0:T(8,128)(2,1)S(1)}, bf16[1,9,3072]{2,1,0:T(8,128)(2,1)}, u32[]{:S(2)}) copy-start(bf16[1,9,3072]{2,1,0:T(8,128)(2,1)} %param.10) | copy-start | bytes 165892
  2.1 21.4 %copy-start.2 = (bf16[384,768]{1,0:T(8,128)(2,1)S(1)}, bf16[384,768]{1,0:T(8,128)(2,1)}, u32[]{:S(2)}) copy-start(bf16[384,768]{1,0:T(8,128)(2,1)} %up_ref.3) | copy-start | bytes 1769476
  2.1 21.4 %copy-start.3 = (bf16[768,384]{1,0:T(8,128)(2,1)S(1)}, bf16[768,384]{1,0:T(8,128)(2,1)}, u32[]{:S(2)}) copy-start(bf16[768,384]{1,0:T(8,128)(2,1)} %down_ref.3) | copy-start | bytes 1769476
  2.1 21.4 %copy-start.4 = (bf16[49,384]{1,0:T(8,128)(2,1)S(1)}, bf16[49,384]{1,0:T(8,128)(2,1)}, u32[]{:S(2)}) copy-start(bf16[49,384]{1,0:T(8,128)(2,1)} %depth_w_ref.3) | copy-start | bytes 112900
  2.1 21.4 %copy-start.5 = (bf16[48,384]{1,0:T(8,128)(2,1)S(1)}, bf16[48,384]{1,0:T(8,128)(2,1)}, u32[]{:S(2)}) copy-start(bf16[48,384]{1,0:T(8,128)(2,1)} %stem_w_ref.1) | copy-start | bytes 110596
  15.7 18.8 %collective-permute-start = (bf16[4,216,384]{2,1,0:T(8,128)(2,1)S(1)}, bf16[4,216,384]{2,1,0:T(8,128)(2,1)S(1)}, u32[]{:S(2)}, u32[]{:S(2)}) collective-permute-start(bf16[4,216,384]{2,1,0:T(8,128)(2,1)S(1)} %all_to_all.35.own_ref), channel_id=1, source_target_pairs={{0,1},{1,0},{2,3},{3,2},{4,5},{5,4},{6,7},{7,6},{8,9},{9,8},{10,11... | collective-permute-start | bytes 1990664 | tf_op jit(solution)/shard_map/ppermute | solution.py:451
  32.6 0.9 copy-start
  33.5 0.9 copy-start.1
  119.0 23.3 %all-to-all-start.1 = ((bf16[8,144,384]{2,1,0:T(8,128)(2,1)}), bf16[8,144,384]{2,1,0:T(8,128)(2,1)S(1)}, u32[]{:S(2)}, u32[]{:S(2)}) async-start(bf16[8,144,384]{2,1,0:T(8,128)(2,1)} %get-tuple-element.27), calls=%async_computation.1 | async-start | bytes 1769472 | tf_op jit(solution)/shard_map/all_to_all | solution.py:439
  128.9 16.4 %collective-permute-start.1 = (bf16[2560,128]{1,0:T(8,128)(2,1)S(1)}, bf16[2560,128]{1,0:T(8,128)(2,1)S(1)}, u32[]{:S(2)}, u32[]{:S(2)}) collective-permute-start(bf16[2560,128]{1,0:T(8,128)(2,1)S(1)} %bitcast.10), channel_id=1, source_target_pairs={{0,1},{1,0},{2,3},{3,2},{4,5},{5,4},{6,7},{7,6},{8,9},{9,8},{10,11... | collective-permute-start | bytes 1966088 | tf_op jit(solution)/shard_map/ppermute | solution.py:451

commit v3 on v2

--- a/solution.py
+++ b/solution.py
@@ -36,7 +36,7 @@
 DEC = ("y", "core")
 ENC = ("x", "zh", "zl")
 PLANE = ("x", "y")
-VMEM_BYTES = 50 * 1024 * 1024
+VMEM_BYTES = 24 * 1024 * 1024
 
 epsilon = 1e-06
 GELU_A = math.sqrt(2.0 / math.pi)
@@ -71,15 +71,40 @@
     return out
 
 
+def in_hbm(x):
+    return pltpu.with_memory_space_constraint(x, pltpu.HBM)
+
+
+class Copies:
+    def __init__(self, sems):
+        self.sems, self.made = sems, []
+
+    def start(self, source, target):
+        copy = pltpu.make_async_copy(source, target, self.sems.at[len(self.made)])
+        self.made.append(copy)
+        copy.start()
+        return copy
+
+
 def forward_kernel(
-    count_ref, patches_ref, stem_w_ref, depth_w_ref, gain_ref, up_ref, down_ref, layer_ref,
-    stem_ref, centred_ref, inv_ref, hidden_ref, projected_ref, feat_ref,
-    taps_ref, field_ref, mixed_ref, normed_ref, act_ref, pool_ref,
+    count_ref, patches_ref, stem_w_hbm, depth_w_hbm, gain_ref, up_hbm, down_hbm, layer_ref,
+    stem_hbm, centred_hbm, inv_hbm, hidden_hbm, feat_hbm,
+    stem_w_ref, depth_w_ref, up_ref, down_ref, stem_ref, centred_ref, inv_ref, hidden_ref,
+    projected_ref, feat_ref, taps_ref, field_ref, mixed_ref, normed_ref, act_ref, pool_ref, sems,
 ):
-    taps_ref[...] = depth_w_ref[...].astype(f32)
+    copies = Copies(sems)
+    stem_w_in = copies.start(stem_w_hbm, stem_w_ref)
+    depth_w_in = copies.start(depth_w_hbm, depth_w_ref)
+    up_in = copies.start(up_hbm, up_ref)
+    down_in = copies.start(down_hbm, down_ref)
+    outs = []
+    stem_w_in.wait()
     stem = jnp.dot(patches_ref[...], stem_w_ref[...], preferred_element_type=f32).astype(bf16)
     stem_ref[...] = stem
+    outs.append(copies.start(stem_ref, stem_hbm))
     field_ref[...] = stem.astype(f32).reshape(SLOTS * TILE, TILE, WIDTH)
+    depth_w_in.wait()
+    taps_ref[...] = depth_w_ref[...].astype(f32)
     gain = gain_ref[...]
 
     def mix(t, carry):
@@ -100,12 +125,16 @@
             normed_ref[at, :] = (centred * gain).astype(bf16)
         return carry
 
-    lax.fori_loop(0, SLOTS, mix, 0)
+    lax.fori_loop(0, SLOTS, mix, 0, unroll=True)
+    outs.append(copies.start(centred_ref, centred_hbm))
+    outs.append(copies.start(inv_ref, inv_hbm))
+    up_in.wait()
     normed = normed_ref[...]
     for n in range(0, INNER, 256):
         hidden_ref[:, n : n + 256] = jnp.dot(
             normed, up_ref[:, n : n + 256], preferred_element_type=f32
         )
+    outs.append(copies.start(hidden_ref, hidden_hbm))
 
     def activate(r, carry):
         at = pl.ds(pl.multiple_of(r * 16, 16), 16)
@@ -114,7 +143,8 @@
         act_ref[at, :] = (0.5 * v * (1.0 + t)).astype(bf16)
         return carry
 
-    lax.fori_loop(0, POSITIONS // 16, activate, 0)
+    lax.fori_loop(0, POSITIONS // 16, activate, 0, unroll=4)
+    down_in.wait()
     projected_ref[...] = jnp.dot(act_ref[...], down_ref[...], preferred_element_type=f32)
     layer = layer_ref[...]
     count = count_ref[0]
@@ -133,43 +163,54 @@
                 pool_ref[chunk, pair * TILE : (pair + 1) * TILE, :] = total[:, lanes(chunk)]
         at = pl.ds(pl.multiple_of(t * FEAT_TILE, FEAT_TILE), FEAT_TILE)
         for chunk in range(CHUNKS):
-            pooled = pool_ref[chunk, pl.ds(0, FEAT_TILE, stride=2), :].astype(bf16)
-            for d in range(N_DEC):
-                feat_ref[d, at, lanes(chunk)] = pooled
+            feat_ref[at, lanes(chunk)] = pool_ref[chunk, pl.ds(0, FEAT_TILE, stride=2), :].astype(bf16)
         return carry
 
     lax.fori_loop(0, SLOTS, pool, 0)
+    for d in range(N_DEC):
+        outs.append(copies.start(feat_ref, feat_hbm.at[d]))
+    for out in outs:
+        out.wait()
 
 
 def forward(count, patches, stem_w, depth_w, gain, up, down, layer):
     vmem = pl.BlockSpec(memory_space=pltpu.VMEM)
-    shapes = (
+    smem = pl.BlockSpec(memory_space=pltpu.SMEM)
+    hbm = pl.BlockSpec(memory_space=pltpu.HBM)
+    stored = (
         ((POSITIONS, WIDTH), bf16),
         ((POSITIONS, WIDTH), f32),
         ((POSITIONS, LANES), f32),
         ((POSITIONS, INNER), f32),
-        ((POSITIONS, WIDTH), f32),
-        ((N_DEC, BLOCK_ROWS, WIDTH), bf16),
     )
+    shapes = stored + (((N_DEC, BLOCK_ROWS, WIDTH), bf16),)
     return pl.pallas_call(
         forward_kernel,
-        out_shape=[jax.ShapeDtypeStruct(*shape) for shape in shapes],
-        in_specs=[pl.BlockSpec(memory_space=pltpu.SMEM)] + [vmem] * 7,
-        out_specs=[vmem] * 6,
+        out_shape=[pltpu.HBM(*shape) for shape in shapes],
+        in_specs=[smem, vmem, hbm, hbm, vmem, hbm, hbm, vmem],
+        out_specs=[hbm] * 5,
         scratch_shapes=[
+            pltpu.VMEM((PATCH_CH, WIDTH), bf16),
+            pltpu.VMEM((KERNEL * KERNEL, WIDTH), bf16),
+            pltpu.VMEM((WIDTH, INNER), bf16),
+            pltpu.VMEM((INNER, WIDTH), bf16),
+            *[pltpu.VMEM(*shape) for shape in stored],
+            pltpu.VMEM((POSITIONS, WIDTH), f32),
+            pltpu.VMEM((BLOCK_ROWS, WIDTH), bf16),
             pltpu.VMEM((KERNEL * KERNEL, WIDTH), f32),
             pltpu.VMEM((SLOTS * TILE, TILE, WIDTH), f32),
             pltpu.VMEM((TILE, TILE, WIDTH), f32),
             pltpu.VMEM((POSITIONS, WIDTH), bf16),
             pltpu.VMEM((POSITIONS, INNER), bf16),
             pltpu.VMEM((CHUNKS, TILE // 2 * TILE, LANES), f32),
+            pltpu.SemaphoreType.DMA((16,)),
         ],
         compiler_params=pltpu.CompilerParams(vmem_limit_bytes=VMEM_BYTES),
         cost_estimate=pl.CostEstimate(
             flops=4 * POSITIONS * WIDTH * INNER, bytes_accessed=8 << 20, transcendentals=0
         ),
         name="block_forward",
-    )(count, patches, stem_w, depth_w, gain, up, down, layer)
+    )(count, patches, in_hbm(stem_w), in_hbm(depth_w), gain, in_hbm(up), in_hbm(down), layer)
 
 
 def rows_times_rows(a, b):
@@ -180,16 +221,29 @@
     return lax.dot_general(a, b, (((0,), (0,)), ((), ())), preferred_element_type=f32)
 
 
+def rows_sum(x):
+    return jnp.sum(x.reshape(-1, TILE, WIDTH), axis=0)
+
+
 def backward_kernel(
-    place_ref, count_ref, own_ref, other_ref, patches_ref, stem_ref, centred_ref, inv_ref,
-    hidden_ref, projected_ref, depth_w_ref, gain_ref, up_ref, down_ref, layer_ref,
-    packed_ref, spans_ref,
+    place_ref, count_ref, own_ref, other_ref, patches_ref, stem_hbm, centred_hbm, inv_hbm,
+    hidden_hbm, depth_w_hbm, gain_ref, up_hbm, down_hbm, layer_ref,
+    packed_hbm, spans_ref,
+    stem_ref, centred_ref, inv_ref, hidden_ref, depth_w_ref, up_ref, down_ref, packed_ref,
     taps_ref, embed_ref, block_ref, proj_ref, act_ref, work_ref, ghid_ref, normed_ref,
-    mixed_ref, gstem_ref, taps_sum_ref, rows_sum_ref,
+    mixed_ref, gstem_ref, taps_sum_ref, gain_sum_ref, scale_sum_ref, sems,
 ):
+    copies = Copies(sems)
+    down_in = copies.start(down_hbm, down_ref)
+    hidden_in = copies.start(hidden_hbm, hidden_ref)
+    centred_in = copies.start(centred_hbm, centred_ref)
+    up_in = copies.start(up_hbm, up_ref)
+    depth_w_in = copies.start(depth_w_hbm, depth_w_ref)
+    inv_in = copies.start(inv_hbm, inv_ref)
+    stem_in = copies.start(stem_hbm, stem_ref)
+    outs = []
     y_here, core_here = place_ref[0], place_ref[1]
     dec_here = 2 * y_here + core_here
-    taps_ref[...] = depth_w_ref[...].astype(f32)
     counts, gaps = [None] * N_DEC, [None] * N_DEC
     for y in range(N_DEC // 2):
         embed_ref[pl.ds(pl.multiple_of((2 * y + core_here) * SHARD, 16), SHARD), :] = own_ref[y, :SHARD, :]
@@ -211,7 +265,8 @@
     count = count_ref[0]
     layer = layer_ref[...]
     gain = gain_ref[...]
-    rows_sum_ref[...] = jnp.zeros((2, TILE, WIDTH), f32)
+    gain_sum_ref[...] = jnp.zeros((TILE, WIDTH), f32)
+    scale_sum_ref[...] = jnp.zeros((TILE, WIDTH), f32)
     taps_sum_ref[...] = jnp.zeros((KERNEL * KERNEL, TILE, WIDTH), f32)
 
     def spread_tile(t, carry):
@@ -227,15 +282,14 @@
         at = pl.ds(pl.multiple_of(t * 64, 64), 64)
         block_ref[at, :] = block
         proj_ref[at, :] = (block * layer).astype(bf16)
-        product = block * projected_ref[at, :]
-        rows_sum_ref[0] += jnp.sum(product.reshape(TILE, TILE, WIDTH), axis=0)
-        normed_ref[at, :] = (centred_ref[at, :] * gain).astype(bf16)
         return carry
 
-    lax.fori_loop(0, SLOTS, spread_tile, 0)
+    lax.fori_loop(0, SLOTS, spread_tile, 0, unroll=True)
     proj = proj_ref[...]
+    down_in.wait()
     for n in range(0, INNER, 256):
         work_ref[:, n : n + 256] = rows_times_rows(proj, down_ref[n : n + 256, :])
+    hidden_in.wait()
 
     def activate(r, carry):
         at = pl.ds(pl.multiple_of(r * 16, 16), 16)
@@ -248,38 +302,48 @@
         ghid_ref[at, :] = (work_ref[at, :] * slope).astype(bf16)
         return carry
 
-    lax.fori_loop(0, POSITIONS // 16, activate, 0)
-    for n in range(0, INNER, 256):
-        term = over_positions(act_ref[:, n : n + 256], proj).astype(bf16)
+    lax.fori_loop(0, POSITIONS // 16, activate, 0, unroll=4)
+    up_in.wait()
+    work_ref[:, :WIDTH] = rows_times_rows(ghid_ref[...], up_ref[...])
+    centred_in.wait()
+    inv_in.wait()
+    stem_in.wait()
+    depth_w_in.wait()
+    taps_ref[...] = depth_w_ref[...].astype(f32)
+    normed_ref[...] = (centred_ref[...] * gain).astype(bf16)
+
+    def down_part(n):
+        term = over_positions(act_ref[:, n : n + 256], proj)
+        scale_sum_ref[...] += rows_sum(term * down_ref[n : n + 256, :].astype(f32))
+        term = term.astype(bf16)
         for chunk in range(CHUNKS):
             to = DOWN_AT + chunk * INNER + n
             packed_ref[to : to + 256, :] = term[:, lanes(chunk)]
-    normed = normed_ref[...]
-    for n in range(0, INNER, 256):
-        term = over_positions(normed, ghid_ref[:, n : n + 256]).astype(bf16)
+
+    def up_part(n):
+        term = over_positions(normed_ref[...], ghid_ref[:, n : n + 256]).astype(bf16)
         for k in range(2):
             to = UP_AT + (n // LANES + k) * WIDTH
             packed_ref[to : to + WIDTH, :] = term[:, lanes(k)]
-    work_ref[:, :WIDTH] = rows_times_rows(ghid_ref[...], up_ref[...])
-
-    def unmix(t, carry):
+
+    def unmix(t):
         gain_sum = jnp.zeros((TILE, WIDTH), f32)
         for i in range(0, TILE, 2):
-            at = pl.ds(pl.multiple_of((t * TILE + i) * TILE, 2 * TILE), 2 * TILE)
+            at = slice((t * TILE + i) * TILE, (t * TILE + i + 2) * TILE)
             grad = work_ref[at, :WIDTH]
             centred = centred_ref[at, :]
-            gain_sum += jnp.sum((grad * centred).reshape(2, TILE, WIDTH), axis=0)
+            gain_sum += rows_sum(grad * centred)
             scaled = grad * gain
             mean = jnp.mean(scaled, axis=1, keepdims=True)
             mean_c = jnp.mean(scaled * centred, axis=1, keepdims=True)
             mixed = (scaled - mean - centred * mean_c) * inv_ref[at, :1]
-            mixed_ref[i : i + 2] = mixed.reshape(2, TILE, WIDTH)
-        rows_sum_ref[1] += gain_sum
+            mixed_ref[t % 2, i : i + 2] = mixed.reshape(2, TILE, WIDTH)
+        gain_sum_ref[...] += gain_sum
         for chunk in range(CHUNKS):
-            grads = [mixed_ref[i, :, lanes(chunk)] for i in range(TILE)]
+            grads = [mixed_ref[t % 2, i, :, lanes(chunk)] for i in range(TILE)]
             stem = []
             for i in range(0, TILE, 2):
-                at = pl.ds(pl.multiple_of((t * TILE + i) * TILE, 2 * TILE), 2 * TILE)
+                at = slice((t * TILE + i) * TILE, (t * TILE + i + 2) * TILE)
                 pair = stem_ref[at, lanes(chunk)].astype(f32)
                 stem += [pair[:TILE], pair[TILE:]]
             for col_tap in range(KERNEL):
@@ -294,18 +358,24 @@
                     taps_sum_ref[row_tap * KERNEL + col_tap, :, lanes(chunk)] += total
             inner = depthwise(grads, taps_ref, chunk, -1)
             for i in range(0, TILE, 2):
-                at = pl.ds(pl.multiple_of((t * TILE + i) * TILE, 2 * TILE), 2 * TILE)
+                at = slice((t * TILE + i) * TILE, (t * TILE + i + 2) * TILE)
                 block = block_ref[at, lanes(chunk)]
                 pair = jnp.concatenate([inner[i], inner[i + 1]], axis=0)
                 gstem_ref[at, lanes(chunk)] = (block + pair).astype(bf16)
-        return carry
-
-    lax.fori_loop(0, SLOTS, unmix, 0)
+
+    parts = [(up_part, n) for n in range(0, INNER, 256)] + [(down_part, n) for n in range(0, INNER, 256)]
+    for t in range(SLOTS):
+        if t < len(parts):
+            parts[t][0](parts[t][1])
+        unmix(t)
+    outs.append(copies.start(packed_ref.at[:STEM_AT], packed_hbm.at[:STEM_AT]))
     stem_term = over_positions(patches_ref[...], gstem_ref[...]).astype(bf16)
+    scale_row = jnp.sum(scale_sum_ref[...], axis=0, keepdims=True) / layer
     small = jnp.concatenate(
         [
             jnp.sum(taps_sum_ref[...], axis=1),
-            jnp.sum(rows_sum_ref[...], axis=1),
+            scale_row,
+            jnp.sum(gain_sum_ref[...], axis=0, keepdims=True),
             jnp.zeros((SMALL_ROWS - KERNEL * KERNEL - 2, WIDTH), f32),
         ],
         axis=0,
@@ -316,20 +386,32 @@
         to = SMALL_AT + chunk * SMALL_ROWS
         packed_ref[to : to + SMALL_ROWS, :] = small[:, lanes(chunk)]
     packed_ref[PACK_USED:, :] = jnp.zeros((PACK_ROWS - PACK_USED, LANES), bf16)
+    outs.append(copies.start(packed_ref.at[STEM_AT:], packed_hbm.at[STEM_AT:]))
+    for out in outs:
+        out.wait()
 
 
 def backward(place, count, own, other, patches, stored, depth_w, gain, up, down, layer):
     vmem = pl.BlockSpec(memory_space=pltpu.VMEM)
     smem = pl.BlockSpec(memory_space=pltpu.SMEM)
+    hbm = pl.BlockSpec(memory_space=pltpu.HBM)
     return pl.pallas_call(
         backward_kernel,
         out_shape=[
-            jax.ShapeDtypeStruct((PACK_ROWS, LANES), bf16),
+            pltpu.HBM((PACK_ROWS, LANES), bf16),
             jax.ShapeDtypeStruct((2 * N_DEC,), jnp.int32),
         ],
-        in_specs=[smem, smem] + [vmem] * 13,
-        out_specs=[vmem, smem],
+        in_specs=[smem, smem, vmem, vmem, vmem, hbm, hbm, hbm, hbm, hbm, vmem, hbm, hbm, vmem],
+        out_specs=[hbm, smem],
         scratch_shapes=[
+            pltpu.VMEM((POSITIONS, WIDTH), bf16),
+            pltpu.VMEM((POSITIONS, WIDTH), f32),
+            pltpu.VMEM((POSITIONS, LANES), f32),
+            pltpu.VMEM((POSITIONS, INNER), f32),
+            pltpu.VMEM((KERNEL * KERNEL, WIDTH), bf16),
+            pltpu.VMEM((WIDTH, INNER), bf16),
+            pltpu.VMEM((INNER, WIDTH), bf16),
+            pltpu.VMEM((PACK_ROWS, LANES), bf16),
             pltpu.VMEM((KERNEL * KERNEL, WIDTH), f32),
             pltpu.VMEM((SEQ + 16, WIDTH), bf16),
             pltpu.VMEM((POSITIONS, WIDTH), f32),
@@ -338,17 +420,22 @@
             pltpu.VMEM((POSITIONS, INNER), f32),
             pltpu.VMEM((POSITIONS, INNER), bf16),
             pltpu.VMEM((POSITIONS, WIDTH), bf16),
-            pltpu.VMEM((TILE, TILE, WIDTH), f32),
+            pltpu.VMEM((2, TILE, TILE, WIDTH), f32),
             pltpu.VMEM((POSITIONS, WIDTH), bf16),
             pltpu.VMEM((KERNEL * KERNEL, TILE, WIDTH), f32),
-            pltpu.VMEM((2, TILE, WIDTH), f32),
+            pltpu.VMEM((TILE, WIDTH), f32),
+            pltpu.VMEM((TILE, WIDTH), f32),
+            pltpu.SemaphoreType.DMA((16,)),
         ],
         compiler_params=pltpu.CompilerParams(vmem_limit_bytes=VMEM_BYTES),
         cost_estimate=pl.CostEstimate(
             flops=8 * POSITIONS * WIDTH * INNER, bytes_accessed=10 << 20, transcendentals=0
         ),
         name="block_backward",
-    )(place, count, own, other, patches, *stored, depth_w, gain, up, down, layer)
+    )(
+        place, count, own, other, patches, *map(in_hbm, stored), in_hbm(depth_w), gain,
+        in_hbm(up), in_hbm(down), layer,
+    )
 
 
 def place_kernel(place_ref, spans_ref, feat_ref, out_ref, rows_ref):
@@ -409,8 +496,8 @@
         small = piece(SMALL_AT + chunk * SMALL_ROWS, SMALL_ROWS)
         taps = KERNEL * KERNEL
         depth_ref[:, lanes(chunk)] = small[:taps]
-        scale_ref[:, lanes(chunk)] = small[taps : taps + 1]
-        gain_ref[:, lanes(chunk)] = small[taps + 1 : taps + 2]
+        scale_ref[lanes(chunk)] = small[taps]
+        gain_ref[lanes(chunk)] = small[taps + 1]
 
 
 def unpack(place, own, other):
@@ -419,10 +506,10 @@
     shapes = (
         (PATCH_CH, WIDTH),
         (KERNEL * KERNEL, WIDTH),
-        (1, WIDTH),
+        (WIDTH,),
         (WIDTH, INNER),
         (INNER, WIDTH),
-        (1, WIDTH),
+        (WIDTH,),
     )
     return pl.pallas_call(
         unpack_kernel,
@@ -435,6 +522,32 @@
     )(place, own, other)
 
 
+def prepare_kernel(count_ref, gap_ref, embed_hbm, out_hbm, rows_ref, sems):
+    copies = Copies(sems)
+    rows_in = copies.start(embed_hbm.at[0], rows_ref.at[:SHARD])
+    lane = lax.broadcasted_iota(jnp.int32, (16, WIDTH), 1)
+    count, gap = count_ref[0, 0].astype(f32), gap_ref[0, 0].astype(f32)
+    rows_ref[SHARD:, :] = jnp.where(lane == 0, count, jnp.where(lane == 1, gap, 0.0)).astype(bf16)
+    rows_in.wait()
+    outs = [copies.start(rows_ref, out_hbm.at[y]) for y in range(N_DEC // 2)]
+    for out in outs:
+        out.wait()
+
+
+def prepare(tile_counts, text_gaps, embed_grad):
+    smem = pl.BlockSpec(memory_space=pltpu.SMEM)
+    hbm = pl.BlockSpec(memory_space=pltpu.HBM)
+    return pl.pallas_call(
+        prepare_kernel,
+        out_shape=pltpu.HBM((N_DEC // 2, SHARD + 16, WIDTH), bf16),
+        in_specs=[smem, smem, hbm],
+        out_specs=hbm,
+        scratch_shapes=[pltpu.VMEM((SHARD + 16, WIDTH), bf16), pltpu.SemaphoreType.DMA((8,))],
+        compiler_params=pltpu.CompilerParams(vmem_limit_bytes=VMEM_BYTES),
+        name="prepare_rows",
+    )(tile_counts, text_gaps, in_hbm(embed_grad))
+
+
 def swap_blocks(blocks, axes):
     return lax.all_to_all(blocks, axes, 0, 0, tiled=True)
 
@@ -451,12 +564,13 @@
     return lax.ppermute(x, "core", [(0, 1), (1, 0)])
 
 
-def sum_all(packed):
+def sum_all(packed, beside):
     half = sum_blocks(swap_blocks(packed.reshape(2, HALF_ROWS, LANES), "core"))
     part = sum_blocks(swap_blocks(half.reshape(16, PACK_ROWS // 32, LANES), PLANE))
     part = sum_blocks(swap_blocks(spread(part, 4), "zl"))
     part = sum_blocks(swap_blocks(spread(part, 4), "zh"))
-    return swap_blocks(spread(part, 16), PLANE).reshape(HALF_ROWS, LANES)
+    part, beside = lax.optimization_barrier((part, beside))
+    return swap_blocks(spread(part, 16), PLANE).reshape(HALF_ROWS, LANES), beside
 
 
 def on_device(
@@ -476,29 +590,21 @@
     gain = norm_gain.reshape(1, WIDTH)
     layer = layer_scale.reshape(1, WIDTH)
     patches = pixels.reshape(POSITIONS, PATCH_CH)
-    numbers = jnp.concatenate([tile_counts, text_gaps], axis=1).astype(bf16)
-    tail = jnp.pad(numbers, ((0, 7), (0, WIDTH - 2)))
-    own = swap_blocks(spread(jnp.concatenate([embed_grad[0], tail]), 4), "y")
+    own = swap_blocks(prepare(tile_counts, text_gaps, embed_grad), "y")
     *stored, feat = forward(
         count, patches, stem_weight, depth_weight, gain, up_weight, down_weight, layer
     )
+    own, feat, place = lax.optimization_barrier((own, feat, place))
     other = swap_cores(own)
     feats = swap_blocks(feat, DEC)
     packed, spans = backward(
         place, count, own, other, patches, stored, depth_weight, gain, up_weight, down_weight, layer
     )
-    half = sum_all(packed)
+    packed, feats = lax.optimization_barrier((packed, feats))
+    sequence = place_features(place, spans, feats)
+    half, sequence = sum_all(packed, sequence)
     stem, depth, gain_grad, up, down, scale = unpack(place, half, swap_cores(half))
-    sequence = place_features(place, spans, feats)
-    return (
-        sequence[None],
-        stem,
-        depth,
-        gain_grad.reshape(WIDTH),
-        up,
-        down,
-        scale.reshape(WIDTH),
-    )
+    return sequence[None], stem, depth, gain_grad, up, down, scale
 
 
 def solution(mesh):

time: 149 us -> 127 us (0.85)
  blocking collectives: 81.2 us -> 45.2 us
  starting transfers between devices: 19.5 us -> 37.7 us
  other arithmetic: 3.18 us -> 0.89 us
    all_to_all x6 -> x4, blocking collectives: 81.2 us -> 45.2 us  [swap_blocks(): return lax.all_to_all(blocks, axes, 0, 0, tiled=True)]
    all_to_all x1 -> x3, starting transfers between devices: 9.92 us -> 21.1 us  [swap_blocks(): return lax.all_to_all(blocks, axes, 0, 0, tiled=True)]
    ppermute x2, starting transfers between devices: 9.53 us -> 16.6 us  [swap_cores(): return lax.ppermute(x, 'core', [(0, 1), (1, 0)])]
    unnamed x18 -> x6, local copies, waits for them, and re-layouts: 1.86 us -> 0.01 us
    ppermute x2, waiting for transfers between devices: 0.01 us -> 1.7 us  [swap_cores(): return lax.ppermute(x, 'core', [(0, 1), (1, 0)])]
    all_to_all x1 -> x3, waiting for transfers between devices: 11.3 us -> 9.66 us  [swap_blocks(): return lax.all_to_all(blocks, axes, 0, 0, tiled=True)]
    pallas_call x2 -> x3, Pallas kernels: 23.9 us -> 22.5 us  [the longest x1 12.9 us: backward(): pl.pallas_call(backward_kernel, out_shape=[pltpu.HBM((PACK_ROWS, LANES),...]
  transfers between devices with their start and end apart: 3 -> 5, of which waited for: 1 -> 3; matrix products, arithmetic and copies ran while one was open for 0% -> 0% of each run, Pallas kernels for 8% -> 19%
where the time goes in v3:
time: 127 us; the launch traced here: 126 us
  blocking collectives  45.2 us (36%)
  starting transfers between devices  37.7 us (30%)
  Pallas kernels  27.7 us (22%)
  waiting for transfers between devices  11.4 us (9%)
  between operations  2.09 us (2%)
    all_to_all x4, blocking collectives, swap_blocks(): return lax.all_to_all(blocks, axes, 0, 0, tiled=True)  45.2 us
    all_to_all x3, starting transfers between devices, swap_blocks(): return lax.all_to_all(blocks, axes, 0, 0, tiled=True)  21.1 us
    ppermute x2, starting transfers between devices, swap_cores(): return lax.ppermute(x, 'core', [(0, 1), (1, 0)])  16.6 us
    pallas_call x1, Pallas kernels, backward(): pl.pallas_call(backward_kernel, out_shape=[pltpu.HBM((PACK_ROWS, LANES),...  12.9 us
    all_to_all x3, waiting for transfers between devices, swap_blocks(): return lax.all_to_all(blocks, axes, 0, 0, tiled=True)  9.66 us
    pallas_call x1, Pallas kernels, forward(): pl.pallas_call(forward_kernel, out_shape=[pltpu.HBM(*shape) for shape in...  7.72 us
    pallas_call x1, Pallas kernels, place_features(): pl.pallas_call(place_kernel, out_shape=jax.ShapeDtypeStruct((SHARD, WIDTH...  3.02 us
  transfers between devices with their start and end apart: 5, of which 3 were waited for; matrix products, arithmetic and copies ran while one was open for 0% of the time, Pallas kernels for 19%

profile of v3, /device:TPU:1, one launch (start us, length us, event | category | flops | bytes accessed | tf_op | source)
XLA Modules:
  0.0 125.9 jit_solution(3234940703463179130)
XLA Ops:
  2.0 1.8 %prepare_rows.1 = bf16[4,224,384]{2,1,0:T(8,128)(2,1)} custom-call(s32[1,1]{1,0:T(1,128)} %copy.17.count_ref, s32[1,1]{1,0:T(1,128)S(6)} %copy.18.gap_ref, bf16[1,208,384]{2,1,0:T(8,128)(2,1)} %embed_hbm.1), custom_call_target="tpu_custom_call" | custom-call | tf_op jit(solution)/shard_map/prepare_rows/pallas_call | solution.py:540
  3.8 5.0 %all-to-all-start = ((bf16[4,224,384]{2,1,0:T(8,128)(2,1)}), bf16[4,224,384]{2,1,0:T(8,128)(2,1)S(1)}, u32[]{:S(2)}, u32[]{:S(2)}) async-start(bf16[4,224,384]{2,1,0:T(8,128)(2,1)} %prepare_rows.1), calls=%async_computation | async-start | bytes 1376256 | tf_op jit(solution)/shard_map/all_to_all | solution.py:552
  8.9 0.2 reshape.39.patches_ref
  9.1 7.7 %block_forward.1 = (bf16[576,384]{1,0:T(8,128)(2,1)}, f32[576,384]{1,0:T(8,128)}, f32[576,128]{1,0:T(8,128)}, f32[576,768]{1,0:T(8,128)}, bf16[8,144,384]{2,1,0:T(8,128)(2,1)}) custom-call(s32[1]{0:T(128)} %bitcast.7.count_ref, bf16[576,48]{1,0:T(8,128)(2,1)S(1)} %reshape.39.patches_ref, bf16[48,384]{1,0:T(8,128)(2,1)} %stem_w_hbm.1, ...), custom_call_target="tpu_custom_call" | custom-call | flops 679477248 | bytes 8388608 | tf_op jit(solution)/shard_map/block_forward/pallas_call | solution.py:187
  16.8 0.1 pad_add_fusion.place_ref
  16.9 0.0 all-to-all-done.own_ref
  16.9 8.2 %collective-permute-start = (bf16[4,224,384]{2,1,0:T(8,128)(2,1)S(1)}, bf16[4,224,384]{2,1,0:T(8,128)(2,1)S(1)}, u32[]{:S(2)}, u32[]{:S(2)}) collective-permute-start(bf16[4,224,384]{2,1,0:T(8,128)(2,1)S(1)} %all-to-all-done.own_ref), channel_id=1, source_target_pairs={{0,1},{1,0},{2,3},{3,2},{4,5},{5,4},{6,7},{7,6},{8,9},{9,8},{10,11... | collective-permute-start | bytes 2064392 | tf_op jit(solution)/shard_map/ppermute | solution.py:564
  25.0 4.0 %all-to-all-start.1 = ((bf16[8,144,384]{2,1,0:T(8,128)(2,1)}), bf16[8,144,384]{2,1,0:T(8,128)(2,1)S(1)}, u32[]{:S(2)}, u32[]{:S(2)}) async-start(bf16[8,144,384]{2,1,0:T(8,128)(2,1)} %get-tuple-element.35), calls=%async_computation.1 | async-start | bytes 1769472 | tf_op jit(solution)/shard_map/all_to_all | solution.py:552
  29.0 12.9 %block_backward.1 = (bf16[5120,128]{1,0:T(8,128)(2,1)}, s32[16]{0:T(128)S(1)}) custom-call(s32[2]{0:T(128)S(1)} %pad_add_fusion.place_ref, s32[1]{0:T(128)} %bitcast.8.count_ref, bf16[4,224,384]{2,1,0:T(8,128)(2,1)S(1)} %all-to-all-done.own_ref, bf16[4,224,384]{2,1,0:T(8,128)(2,1)S(1)} %collective-permute-done.other_ref, ...), custom_call_target="tpu_custom_call" | custom-call | flops 1358954496 | bytes 10485760 | tf_op jit(solution)/shard_map/block_backward/pallas_call | solution.py:398
  42.0 0.4 all-to-all-done.1.feat_ref
  42.4 6.4 %all_to_all.35 = bf16[2,2560,128]{2,1,0:T(8,128)(2,1)S(1)} all-to-all(bf16[2,2560,128]{2,1,0:T(8,128)(2,1)} %bitcast.12), channel_id=1, replica_groups=mesh['x'=4,'zh'=4,'zl'=4,'y'=4,'core'=2] {'core'}, dimensions={0} | all-to-all | bytes 2621440 | tf_op jit(solution)/shard_map/all_to_all | solution.py:552
  48.8 0.7 reduce_sum.48
  49.5 15.1 %all_to_all.36 = bf16[16,160,128]{2,1,0:T(8,128)(2,1)S(1)} all-to-all(bf16[16,160,128]{2,1,0:T(8,128)(2,1)S(1)} %bitcast.11), channel_id=1, replica_groups=mesh['x'=4,'zh'=4,'zl'=4,'y'=4,'core'=2] {'x','y'}, dimensions={0} | all-to-all | bytes 1310720 | tf_op jit(solution)/shard_map/all_to_all | solution.py:552
  64.6 0.1 reduce_sum.49
  64.7 10.9 %all_to_all.37 = bf16[4,160,128]{2,1,0:T(8,128)(2,1)S(1)} all-to-all(bf16[4,160,128]{2,1,0:T(8,128)(2,1)S(1)} %broadcast_in_dim.8), channel_id=1, replica_groups=mesh['x'=4,'zh'=4,'zl'=4,'y'=4,'core'=2] {'zl'}, dimensions={0} | all-to-all | bytes 327680 | tf_op jit(solution)/shard_map/all_to_all | solution.py:552
  75.7 0.7 broadcast_in_dim.9
  76.4 12.1 %all-to-all-start.5 = ((bf16[4,160,128]{2,1,0:T(8,128)(2,1)}), bf16[4,160,128]{2,1,0:T(8,128)(2,1)S(1)}, u32[]{:S(2)}, u32[]{:S(2)}) async-start(bf16[4,160,128]{2,1,0:T(8,128)(2,1)} %broadcast_in_dim.9), calls=%async_computation.5 | async-start | bytes 327680 | tf_op jit(solution)/shard_map/all_to_all | solution.py:552
  88.5 3.0 %place_features.1 = bf16[208,384]{1,0:T(8,128)(2,1)} custom-call(s32[2]{0:T(128)S(1)} %pad_add_fusion.place_ref, s32[16]{0:T(128)S(1)} %get-tuple-element.37.spans_ref, bf16[8,144,384]{2,1,0:T(8,128)(2,1)S(1)} %all-to-all-done.1.feat_ref), custom_call_target="tpu_custom_call" | custom-call | tf_op jit(solution)/shard_map/place_features/pallas_call | solution.py:469
  91.5 9.2 %all-to-all-done.5 = bf16[4,160,128]{2,1,0:T(8,128)(2,1)S(1)} async-done(((bf16[4,160,128]{2,1,0:T(8,128)(2,1)}), bf16[4,160,128]{2,1,0:T(8,128)(2,1)S(1)}, u32[]{:S(2)}, u32[]{:S(2)}) %all-to-all-start.5) | async-done | bytes 163872 | tf_op jit(solution)/shard_map/all_to_all | solution.py:552
  100.8 0.1 broadcast_in_dim.11
  100.8 12.8 %all_to_all.38 = bf16[16,160,128]{2,1,0:T(8,128)(2,1)S(1)} all-to-all(bf16[16,160,128]{2,1,0:T(8,128)(2,1)S(1)} %broadcast_in_dim.11), channel_id=1, replica_groups=mesh['x'=4,'zh'=4,'zl'=4,'y'=4,'core'=2] {'x','y'}, dimensions={0} | all-to-all | bytes 1310720 | tf_op jit(solution)/shard_map/all_to_all | solution.py:552
  113.6 8.4 %collective-permute-start.1 = (bf16[2560,128]{1,0:T(8,128)(2,1)S(1)}, bf16[2560,128]{1,0:T(8,128)(2,1)S(1)}, u32[]{:S(2)}, u32[]{:S(2)}) collective-permute-start(bf16[2560,128]{1,0:T(8,128)(2,1)S(1)} %bitcast.9), channel_id=1, source_target_pairs={{0,1},{1,0},{2,3},{3,2},{4,5},{5,4},{6,7},{7,6},{8,9},{9,8},{10,11... | collective-permute-start | bytes 1966088 | tf_op jit(solution)/shard_map/ppermute | solution.py:564
  122.0 1.7 %collective-permute-done.1.other_ref = bf16[2560,128]{1,0:T(8,128)(2,1)S(1)} collective-permute-done((bf16[2560,128]{1,0:T(8,128)(2,1)S(1)}, bf16[2560,128]{1,0:T(8,128)(2,1)S(1)}, u32[]{:S(2)}, u32[]{:S(2)}) %collective-permute-start.1) | collective-permute-done | bytes 655392 | tf_op jit(solution)/shard_map/ppermute | solution.py:564
  123.7 2.2 %unpack_terms.1 = (f32[48,384]{1,0:T(8,128)}, f32[49,384]{1,0:T(8,128)}, f32[384]{0:T(512)}, f32[384,768]{1,0:T(8,128)}, f32[768,384]{1,0:T(8,128)}, /*index=5*/f32[384]{0:T(512)}) custom-call(s32[2]{0:T(128)S(1)} %pad_add_fusion.place_ref, bf16[2560,128]{1,0:T(8,128)(2,1)S(1)} %bitcast.10, bf16[2560,128]{1,0:T(8,128)(2,1)S(1)} %collective-permute-done.1.other_ref), custom_call_target="tpu_custom_call" | custom-call | tf_op jit(solution)/shard_map/unpack_terms/pallas_call | solution.py:514
  (12 shorter events, 0.1 us)
Async XLA Ops:
  0.6 8.2 %copy-start.1 = (f32[384]{0:T(512)S(1)}, f32[384]{0:T(512)}, u32[]{:S(2)}) copy-start(f32[384]{0:T(512)} %param.15) | copy-start | bytes 4612
  0.6 8.2 %copy-start.2 = (f32[384]{0:T(512)S(1)}, f32[384]{0:T(512)}, u32[]{:S(2)}) copy-start(f32[384]{0:T(512)} %param.18) | copy-start | bytes 4612
  0.7 8.2 %copy-start = (bf16[1,9,3072]{2,1,0:T(8,128)(2,1)S(1)}, bf16[1,9,3072]{2,1,0:T(8,128)(2,1)}, u32[]{:S(2)}) copy-start(bf16[1,9,3072]{2,1,0:T(8,128)(2,1)} %param.10) | copy-start | bytes 165892
  3.8 13.0 %all-to-all-start = ((bf16[4,224,384]{2,1,0:T(8,128)(2,1)}), bf16[4,224,384]{2,1,0:T(8,128)(2,1)S(1)}, u32[]{:S(2)}, u32[]{:S(2)}) async-start(bf16[4,224,384]{2,1,0:T(8,128)(2,1)} %prepare_rows.1), calls=%async_computation | async-start | bytes 1376256 | tf_op jit(solution)/shard_map/all_to_all | solution.py:552
  16.9 12.2 %collective-permute-start = (bf16[4,224,384]{2,1,0:T(8,128)(2,1)S(1)}, bf16[4,224,384]{2,1,0:T(8,128)(2,1)S(1)}, u32[]{:S(2)}, u32[]{:S(2)}) collective-permute-start(bf16[4,224,384]{2,1,0:T(8,128)(2,1)S(1)} %all-to-all-done.own_ref), channel_id=1, source_target_pairs={{0,1},{1,0},{2,3},{3,2},{4,5},{5,4},{6,7},{7,6},{8,9},{9,8},{10,11... | collective-permute-start | bytes 2064392 | tf_op jit(solution)/shard_map/ppermute | solution.py:564
  25.0 17.3 %all-to-all-start.1 = ((bf16[8,144,384]{2,1,0:T(8,128)(2,1)}), bf16[8,144,384]{2,1,0:T(8,128)(2,1)S(1)}, u32[]{:S(2)}, u32[]{:S(2)}) async-start(bf16[8,144,384]{2,1,0:T(8,128)(2,1)} %get-tuple-element.35), calls=%async_computation.1 | async-start | bytes 1769472 | tf_op jit(solution)/shard_map/all_to_all | solution.py:552
  76.4 24.4 %all-to-all-start.5 = ((bf16[4,160,128]{2,1,0:T(8,128)(2,1)}), bf16[4,160,128]{2,1,0:T(8,128)(2,1)S(1)}, u32[]{:S(2)}, u32[]{:S(2)}) async-start(bf16[4,160,128]{2,1,0:T(8,128)(2,1)} %broadcast_in_dim.9), calls=%async_computation.5 | async-start | bytes 327680 | tf_op jit(solution)/shard_map/all_to_all | solution.py:552
  113.6 10.1 %collective-permute-start.1 = (bf16[2560,128]{1,0:T(8,128)(2,1)S(1)}, bf16[2560,128]{1,0:T(8,128)(2,1)S(1)}, u32[]{:S(2)}, u32[]{:S(2)}) collective-permute-start(bf16[2560,128]{1,0:T(8,128)(2,1)S(1)} %bitcast.9), channel_id=1, source_target_pairs={{0,1},{1,0},{2,3},{3,2},{4,5},{5,4},{6,7},{7,6},{8,9},{9,8},{10,11... | collective-permute-start | bytes 1966088 | tf_op jit(solution)/shard_map/ppermute | solution.py:564

commit v4 on v3

v4 whole, which is shorter than its diff:
```python
import math

import jax
import jax.numpy as jnp
from jax import lax
from jax.experimental import pallas as pl
from jax.experimental.pallas import tpu as pltpu
from jax.sharding import Mesh
from jax.sharding import PartitionSpec as P

WIDTH = 384
INNER = 768
KERNEL = 7
REACH = KERNEL // 2
PATCH_CH = 48
TILE = 8
MEAN_TILES = 3
SLOTS = 9
FEAT_TILE = 16
N_OWNERS = 512
N_DEC = 8
SHARD = 208
SEQ = N_DEC * SHARD
POSITIONS = SLOTS * TILE * TILE
BLOCK_ROWS = SLOTS * FEAT_TILE
LANES = 128
LEAD = 8
LEAD_ROWS = LEAD * TILE * TILE
CHUNKS = WIDTH // LANES
PACK_ROWS = 5120
HALF_ROWS = PACK_ROWS // 2
UP_AT = 0
DOWN_AT = HALF_ROWS
LATE_AT = (INNER // LANES) * WIDTH
STEM_AT = LATE_AT
SMALL_AT = HALF_ROWS + LATE_AT
SMALL_ROWS = 64
DEC = ("y", "core")
ENC = ("x", "zh", "zl")
PLANE = ("x", "y")
VMEM_BYTES = 24 * 1024 * 1024

epsilon = 1e-06
GELU_A = math.sqrt(2.0 / math.pi)
GELU_B = 0.044715
bf16 = jnp.bfloat16
f32 = jnp.float32


def lanes(chunk):
    return slice(chunk * LANES, (chunk + 1) * LANES)


def column_shift(rows, step):
    if step == 0:
        return rows
    column = lax.broadcasted_iota(jnp.int32, (TILE, LANES), 0) + step
    inside = (column >= 0) & (column < TILE)
    return [jnp.where(inside, pltpu.roll(row, (-step) % TILE, 0), 0.0) for row in rows]


def depthwise(rows, taps_ref, chunk, sign):
    out = [jnp.zeros((TILE, LANES), f32)] * TILE
    for col_tap in range(KERNEL):
        moved = column_shift(rows, sign * (col_tap - REACH))
        for row_tap in range(KERNEL):
            weight = taps_ref[row_tap * KERNEL + col_tap, :, lanes(chunk)]
            for i in range(TILE):
                source = i + sign * (row_tap - REACH)
                if 0 <= source < TILE:
                    out[i] = out[i] + moved[source] * weight
    return out


def place_rows(i, j):
    return slice((i * TILE + j) * LEAD, (i * TILE + j + 1) * LEAD)


def last_rows(i):
    return slice(LEAD_ROWS + i * TILE, LEAD_ROWS + (i + 1) * TILE)


def depthwise_row(field_ref, taps_ref, chunk, sign, i):
    out = [jnp.zeros((LEAD, LANES), f32)] * TILE
    for row_tap in range(KERNEL):
        source = i + sign * (row_tap - REACH)
        if 0 <= source < TILE:
            row = [field_ref[place_rows(source, j), lanes(chunk)] for j in range(TILE)]
            for col_tap in range(KERNEL):
                weight = taps_ref[row_tap * KERNEL + col_tap, :, lanes(chunk)]
                for j in range(TILE):
                    column = j + sign * (col_tap - REACH)
                    if 0 <= column < TILE:
                        out[j] = out[j] + row[column] * weight
    return out


def set_taps(taps_ref, depth_w_ref):
    taps = depth_w_ref[...].astype(f32)
    for k in range(KERNEL * KERNEL):
        taps_ref[k] = jnp.broadcast_to(taps[k : k + 1], (TILE, WIDTH))


def in_hbm(x):
    return pltpu.with_memory_space_constraint(x, pltpu.HBM)


class Copies:
    def __init__(self, sems):
        self.sems, self.made = sems, []

    def start(self, source, target):
        copy = pltpu.make_async_copy(source, target, self.sems.at[len(self.made)])
        self.made.append(copy)
        copy.start()
        return copy


def forward_kernel(
    count_ref, patches_ref, stem_w_hbm, depth_w_hbm, gain_ref, up_hbm, down_hbm, layer_ref,
    stem_hbm, centred_hbm, hidden_hbm, inv_ref, feat_hbm,
    stem_w_ref, depth_w_ref, up_ref, down_ref, stem_ref, centred_ref, half_ref, hidden_ref,
    projected_ref, feat_ref, taps_ref, field_ref, mixed_ref, normed_ref, act_ref, pool_ref, last_ref,
    sems,
):
    copies = Copies(sems)
    stem_w_in = copies.start(stem_w_hbm, stem_w_ref)
    depth_w_in = copies.start(depth_w_hbm, depth_w_ref)
    up_in = copies.start(up_hbm, up_ref)
    down_in = copies.start(down_hbm, down_ref)
    outs = []
    stem_w_in.wait()
    stem = jnp.dot(patches_ref[...], stem_w_ref[...], preferred_element_type=f32).astype(bf16)
    stem_ref[...] = stem
    outs.append(copies.start(stem_ref, stem_hbm))
    field_ref[...] = stem.astype(f32)
    depth_w_in.wait()
    set_taps(taps_ref, depth_w_ref)
    gain = gain_ref[...]

    def norm(at):
        row = mixed_ref[at, :]
        deviation = row - jnp.mean(row, axis=1, keepdims=True)
        inv_std = lax.rsqrt(jnp.mean(deviation * deviation, axis=1, keepdims=True) + epsilon)
        centred = deviation * inv_std
        centred_ref[at, :] = centred
        inv_ref[at, :] = jnp.broadcast_to(inv_std, (2 * TILE, LANES))
        normed_ref[at, :] = (centred * gain).astype(bf16)

    for i in range(TILE):
        for chunk in range(CHUNKS):
            out = depthwise_row(field_ref, taps_ref, chunk, 1, i)
            for j in range(TILE):
                mixed_ref[place_rows(i, j), lanes(chunk)] = out[j]
        for at in range(i * 64, i * 64 + 64, 16):
            norm(slice(at, at + 16))
    for chunk in range(CHUNKS):
        out = depthwise([field_ref[last_rows(i), lanes(chunk)] for i in range(TILE)], taps_ref, chunk, 1)
        for i in range(TILE):
            mixed_ref[last_rows(i), lanes(chunk)] = out[i]
    for at in range(LEAD_ROWS, POSITIONS, 16):
        norm(slice(at, at + 16))
    outs.append(copies.start(centred_ref, centred_hbm))
    up_in.wait()
    normed = normed_ref[...]
    for n in range(0, INNER, 256):
        hidden_ref[:, n : n + 256] = jnp.dot(
            normed, up_ref[:, n : n + 256], preferred_element_type=f32
        )

    def activate(r, carry):
        at = pl.ds(pl.multiple_of(r * 16, 16), 16)
        v = hidden_ref[at, :]
        half_ref[at, :] = v.astype(bf16)
        t = jnp.tanh(GELU_A * (v + GELU_B * (v * v * v)))
        act_ref[at, :] = (0.5 * v * (1.0 + t)).astype(bf16)
        return carry

    lax.fori_loop(0, POSITIONS // 16, activate, 0, unroll=4)
    outs.append(copies.start(half_ref, hidden_hbm))
    down_in.wait()
    projected_ref[...] = jnp.dot(act_ref[...], down_ref[...], preferred_element_type=f32)
    layer = layer_ref[...]
    count = count_ref[0, 0]

    keep = jnp.where(lax.broadcasted_iota(jnp.int32, (LEAD, WIDTH), 0) < count, 0.25, 0.0)

    def block(at):
        return field_ref[at, :] + layer * projected_ref[at, :]

    for f in range(FEAT_TILE):
        i, j = 2 * (f // 4), 2 * (f % 4)
        total = block(place_rows(i, j)) + block(place_rows(i, j + 1))
        total += block(place_rows(i + 1, j)) + block(place_rows(i + 1, j + 1))
        pool_ref[f * LEAD : (f + 1) * LEAD, :] = total * keep
    keep_last = jnp.where(count == SLOTS, 0.25, 0.0).astype(f32)
    for pair in range(TILE // 2):
        total = block(last_rows(2 * pair)) + block(last_rows(2 * pair + 1))
        total = (total + pltpu.roll(total, TILE - 1, 0)) * keep_last
        for chunk in range(CHUNKS):
            last_ref[chunk, pair * TILE : (pair + 1) * TILE, :] = total[:, lanes(chunk)]
    for chunk in range(CHUNKS):
        pool_ref[LEAD * FEAT_TILE :, lanes(chunk)] = last_ref[chunk, pl.ds(0, FEAT_TILE, stride=2), :]
    row = lax.broadcasted_iota(jnp.int32, (BLOCK_ROWS, BLOCK_ROWS), 0)
    col = lax.broadcasted_iota(jnp.int32, (BLOCK_ROWS, BLOCK_ROWS), 1)
    tile, f = lax.shift_right_logical(row, 4), row & 15
    order = jnp.where(col == jnp.where(tile < LEAD, f * LEAD + tile, LEAD * FEAT_TILE + f), 1.0, 0.0)
    feat_ref[...] = jnp.dot(
        order.astype(bf16), pool_ref[...].astype(bf16), preferred_element_type=f32
    ).astype(bf16)
    for d in range(N_DEC):
        outs.append(copies.start(feat_ref, feat_hbm.at[d]))
    for out in outs:
        out.wait()


def forward(count, patches, stem_w, depth_w, gain, up, down, layer):
    vmem = pl.BlockSpec(memory_space=pltpu.VMEM)
    smem = pl.BlockSpec(memory_space=pltpu.SMEM)
    hbm = pl.BlockSpec(memory_space=pltpu.HBM)
    stored = (
        ((POSITIONS, WIDTH), bf16),
        ((POSITIONS, WIDTH), f32),
        ((POSITIONS, INNER), bf16),
    )
    inv = jax.ShapeDtypeStruct((POSITIONS, LANES), f32)
    return pl.pallas_call(
        forward_kernel,
        out_shape=[pltpu.HBM(*shape) for shape in stored] + [inv, pltpu.HBM((N_DEC, BLOCK_ROWS, WIDTH), bf16)],
        in_specs=[smem, vmem, hbm, hbm, vmem, hbm, hbm, vmem],
        out_specs=[hbm, hbm, hbm, vmem, hbm],
        scratch_shapes=[
            pltpu.VMEM((PATCH_CH, WIDTH), bf16),
            pltpu.VMEM((KERNEL * KERNEL, WIDTH), bf16),
            pltpu.VMEM((WIDTH, INNER), bf16),
            pltpu.VMEM((INNER, WIDTH), bf16),
            *[pltpu.VMEM(*shape) for shape in stored],
            pltpu.VMEM((POSITIONS, INNER), f32),
            pltpu.VMEM((POSITIONS, WIDTH), f32),
            pltpu.VMEM((BLOCK_ROWS, WIDTH), bf16),
            pltpu.VMEM((KERNEL * KERNEL, TILE, WIDTH), f32),
            pltpu.VMEM((POSITIONS, WIDTH), f32),
            pltpu.VMEM((POSITIONS, WIDTH), f32),
            pltpu.VMEM((POSITIONS, WIDTH), bf16),
            pltpu.VMEM((POSITIONS, INNER), bf16),
            pltpu.VMEM((BLOCK_ROWS, WIDTH), f32),
            pltpu.VMEM((CHUNKS, TILE // 2 * TILE, LANES), f32),
            pltpu.SemaphoreType.DMA((18,)),
        ],
        compiler_params=pltpu.CompilerParams(vmem_limit_bytes=VMEM_BYTES),
        cost_estimate=pl.CostEstimate(
            flops=4 * POSITIONS * WIDTH * INNER, bytes_accessed=8 << 20, transcendentals=0
        ),
        name="block_forward",
    )(count, patches, in_hbm(stem_w), in_hbm(depth_w), gain, in_hbm(up), in_hbm(down), layer)


def rows_times_rows(a, b):
    return lax.dot_general(a, b, (((1,), (1,)), ((), ())), preferred_element_type=f32)


def over_positions(a, b):
    return lax.dot_general(a, b, (((0,), (0,)), ((), ())), preferred_element_type=f32)


def rows_sum(x):
    return jnp.sum(x.reshape(-1, TILE, WIDTH), axis=0)


def backward_kernel(
    place_ref, own_ref, other_ref, patches_ref, stem_hbm, centred_hbm, hidden_hbm,
    inv_ref, depth_w_hbm, gain_ref, up_hbm, down_hbm, layer_ref,
    mine_hbm, theirs_hbm, spans_ref,
    stem_ref, centred_ref, hidden_ref, depth_w_ref, up_ref, down_ref, packed_ref,
    taps_ref, embed_ref, block_ref, proj_ref, act_ref, work_ref, ghid_ref, normed_ref, field_ref,
    mixed_ref, gstem_ref, taps_sum_ref, scale_sum_ref, tails_ref, sems,
):
    copies = Copies(sems)
    y_here, core_here = place_ref[0], place_ref[1]
    dec_here = 2 * y_here + core_here
    down_in = copies.start(down_hbm, down_ref)
    hidden_in = copies.start(hidden_hbm, hidden_ref)
    up_in = copies.start(up_hbm, up_ref)
    centred_in = copies.start(centred_hbm, centred_ref)
    depth_w_in = copies.start(depth_w_hbm, depth_w_ref)
    stem_in = copies.start(stem_hbm, stem_ref)
    outs = []
    layer = layer_ref[...]
    gain = gain_ref[...]
    scale_sum_ref[...] = jnp.zeros((TILE, WIDTH), f32)
    embed_ref[SEQ:, :] = jnp.zeros((16, WIDTH), bf16)
    for used in (STEM_AT + CHUNKS * PATCH_CH, SMALL_AT + CHUNKS * SMALL_ROWS):
        end = HALF_ROWS if used < HALF_ROWS else PACK_ROWS
        packed_ref[used:end, :] = jnp.zeros((end - used, LANES), bf16)
    counts, gaps = [None] * N_DEC, [None] * N_DEC
    for y in range(N_DEC // 2):
        for k, source in ((core_here, own_ref), (1 - core_here, other_ref)):
            to = pl.ds(pl.multiple_of((2 * y + k) * SHARD, 16), SHARD)
            embed_ref[to, :] = source[y, :SHARD, :]
            tails_ref[k, y] = source[y, SHARD:, :]
        for core in range(2):
            tail = tails_ref[core, y, :, :LANES].astype(f32)
            counts[2 * y + core] = tail[0, 0].astype(jnp.int32)
            gaps[2 * y + core] = tail[0, 1].astype(jnp.int32)
    at, own_offset, count = jnp.int32(0), jnp.int32(0), jnp.int32(0)
    for d in range(N_DEC):
        start = at + gaps[d]
        spans_ref[d] = start
        spans_ref[N_DEC + d] = counts[d]
        own_offset = jnp.where(dec_here == d, start, own_offset)
        count = jnp.where(dec_here == d, counts[d], count)
        at = start + FEAT_TILE * counts[d]

    base = lax.div(own_offset, 16)
    row = lax.broadcasted_iota(jnp.int32, (POSITIONS, BLOCK_ROWS + 16), 0)
    col = lax.broadcasted_iota(jnp.int32, (POSITIONS, BLOCK_ROWS + 16), 1)
    tile = jnp.where(row < LEAD_ROWS, row & (LEAD - 1), LEAD)
    spot = jnp.where(row < LEAD_ROWS, lax.shift_right_logical(row, 3), row - LEAD_ROWS)
    feat = lax.shift_right_logical(spot, 4) * 4 + (lax.shift_right_logical(spot, 1) & 3)
    hit = (col == tile * FEAT_TILE + feat + (own_offset - 16 * base)) & (tile < count)
    pick = jnp.where(hit, 0.25, 0.0).astype(bf16)
    window = embed_ref[pl.ds(pl.multiple_of(base * 16, 16), BLOCK_ROWS + 16), :]
    block = jnp.dot(pick, window, preferred_element_type=f32)
    block_ref[...] = block
    proj_ref[...] = (block * layer).astype(bf16)
    proj = proj_ref[...]
    down_in.wait()
    for n in range(0, INNER, 256):
        work_ref[:, n : n + 256] = rows_times_rows(proj, down_ref[n : n + 256, :])

    hidden_in.wait()

    def activate(r, carry):
        at = pl.ds(pl.multiple_of(r * 16, 16), 16)
        v = hidden_ref[at, :].astype(f32)
        square = v * v
        t = jnp.tanh(GELU_A * (v + GELU_B * (square * v)))
        half = 0.5 * (1.0 + t)
        act_ref[at, :] = (v * half).astype(bf16)
        slope = half + (0.5 * GELU_A) * v * (1.0 - t * t) * (1.0 + (3.0 * GELU_B) * square)
        ghid_ref[at, :] = (work_ref[at, :] * slope).astype(bf16)
        return carry

    lax.fori_loop(0, POSITIONS // 16, activate, 0, unroll=4)
    up_in.wait()
    work_ref[:, :WIDTH] = rows_times_rows(ghid_ref[...], up_ref[...])
    centred_in.wait()
    stem_in.wait()
    depth_w_in.wait()
    set_taps(taps_ref, depth_w_ref)
    field_ref[...] = stem_ref[...].astype(f32)

    def unnorm(r, carry):
        at = pl.ds(pl.multiple_of(r * 16, 16), 16)
        grad = work_ref[at, :WIDTH]
        centred = centred_ref[at, :]
        normed_ref[at, :] = (centred * gain).astype(bf16)
        scaled = grad * gain
        mean = jnp.mean(scaled, axis=1, keepdims=True)
        mean_c = jnp.mean(scaled * centred, axis=1, keepdims=True)
        mixed_ref[at, :] = (scaled - mean - centred * mean_c) * inv_ref[at, :1]
        return carry + rows_sum(grad * centred)

    gain_sum = lax.fori_loop(0, POSITIONS // 16, unnorm, jnp.zeros((TILE, WIDTH), f32), unroll=6)

    def down_part(n):
        term = over_positions(act_ref[:, n : n + 256], proj)
        scale_sum_ref[...] += rows_sum(term * down_ref[n : n + 256, :].astype(f32))
        term = term.astype(bf16)
        for chunk in range(CHUNKS):
            to = DOWN_AT + chunk * INNER + n
            packed_ref[to : to + 256, :] = term[:, lanes(chunk)]

    def up_part(n):
        term = over_positions(normed_ref[...], ghid_ref[:, n : n + 256]).astype(bf16)
        for k in range(2):
            to = UP_AT + (n // LANES + k) * WIDTH
            packed_ref[to : to + WIDTH, :] = term[:, lanes(k)]

    def taps_term(chunk, row_tap):
        sums = [jnp.zeros((LEAD, LANES), f32)] * KERNEL
        for i in range(TILE):
            source = i + row_tap - REACH
            if 0 <= source < TILE:
                row = [field_ref[place_rows(source, j), lanes(chunk)] for j in range(TILE)]
                for j in range(TILE):
                    grad = mixed_ref[place_rows(i, j), lanes(chunk)]
                    for col_tap in range(KERNEL):
                        column = j + col_tap - REACH
                        if 0 <= column < TILE:
                            sums[col_tap] = sums[col_tap] + row[column] * grad
        for col_tap in range(KERNEL):
            taps_sum_ref[row_tap * KERNEL + col_tap, :, lanes(chunk)] = sums[col_tap]

    def unmix_row(chunk, i):
        inner = depthwise_row(mixed_ref, taps_ref, chunk, -1, i)
        for j in range(0, TILE, 2):
            at = slice((i * TILE + j) * LEAD, (i * TILE + j + 2) * LEAD)
            pair = jnp.concatenate([inner[j], inner[j + 1]], axis=0)
            gstem_ref[at, lanes(chunk)] = (block_ref[at, lanes(chunk)] + pair).astype(bf16)

    def unmix_last(chunk):
        grads = [mixed_ref[last_rows(i), lanes(chunk)] for i in range(TILE)]
        stem = [field_ref[last_rows(i), lanes(chunk)] for i in range(TILE)]
        for col_tap in range(KERNEL):
            moved = column_shift(stem, col_tap - REACH)
            for row_tap in range(KERNEL):
                total = None
                for i in range(TILE):
                    source = i + row_tap - REACH
                    if 0 <= source < TILE:
                        part = moved[source] * grads[i]
                        total = part if total is None else total + part
                taps_sum_ref[row_tap * KERNEL + col_tap, :, lanes(chunk)] += total
        inner = depthwise(grads, taps_ref, chunk, -1)
        for i in range(0, TILE, 2):
            at = slice(LEAD_ROWS + i * TILE, LEAD_ROWS + (i + 2) * TILE)
            pair = jnp.concatenate([inner[i], inner[i + 1]], axis=0)
            gstem_ref[at, lanes(chunk)] = (block_ref[at, lanes(chunk)] + pair).astype(bf16)

    for n in range(0, INNER, 256):
        up_part(n)
        down_part(n)
    for core, target in ((core_here, mine_hbm), (1 - core_here, theirs_hbm)):
        at = pl.ds(pl.multiple_of(core * HALF_ROWS, 16), LATE_AT)
        outs.append(copies.start(packed_ref.at[at], target.at[:LATE_AT]))
    for chunk in range(CHUNKS):
        for row_tap in range(KERNEL):
            taps_term(chunk, row_tap)
        for i in range(TILE):
            unmix_row(chunk, i)
    for chunk in range(CHUNKS):
        unmix_last(chunk)
    stem_term = over_positions(patches_ref[...], gstem_ref[...]).astype(bf16)
    scale_row = jnp.sum(scale_sum_ref[...], axis=0, keepdims=True) / layer
    small = jnp.concatenate(
        [
            jnp.sum(taps_sum_ref[...], axis=1),
            scale_row,
            jnp.sum(gain_sum, axis=0, keepdims=True),
            jnp.zeros((SMALL_ROWS - KERNEL * KERNEL - 2, WIDTH), f32),
        ],
        axis=0,
    ).astype(bf16)
    for chunk in range(CHUNKS):
        to = STEM_AT + chunk * PATCH_CH
        packed_ref[to : to + PATCH_CH, :] = stem_term[:, lanes(chunk)]
        to = SMALL_AT + chunk * SMALL_ROWS
        packed_ref[to : to + SMALL_ROWS, :] = small[:, lanes(chunk)]
    for k, target in ((core_here, mine_hbm), (1 - core_here, theirs_hbm)):
        at = pl.ds(pl.multiple_of(k * HALF_ROWS + LATE_AT, 16), HALF_ROWS - LATE_AT)
        outs.append(copies.start(packed_ref.at[at], target.at[LATE_AT:]))
    for out in outs:
        out.wait()


def backward(place, own, other, patches, stored, depth_w, gain, up, down, layer):
    vmem = pl.BlockSpec(memory_space=pltpu.VMEM)
    smem = pl.BlockSpec(memory_space=pltpu.SMEM)
    hbm = pl.BlockSpec(memory_space=pltpu.HBM)
    return pl.pallas_call(
        backward_kernel,
        out_shape=[
            pltpu.HBM((HALF_ROWS, LANES), bf16),
            pltpu.HBM((HALF_ROWS, LANES), bf16),
            jax.ShapeDtypeStruct((2 * N_DEC,), jnp.int32),
        ],
        in_specs=[smem, vmem, vmem, vmem, hbm, hbm, hbm, vmem, hbm, vmem, hbm, hbm, vmem],
        out_specs=[hbm, hbm, smem],
        scratch_shapes=[
            pltpu.VMEM((POSITIONS, WIDTH), bf16),
            pltpu.VMEM((POSITIONS, WIDTH), f32),
            pltpu.VMEM((POSITIONS, INNER), bf16),
            pltpu.VMEM((KERNEL * KERNEL, WIDTH), bf16),
            pltpu.VMEM((WIDTH, INNER), bf16),
            pltpu.VMEM((INNER, WIDTH), bf16),
            pltpu.VMEM((PACK_ROWS, LANES), bf16),
            pltpu.VMEM((KERNEL * KERNEL, TILE, WIDTH), f32),
            pltpu.VMEM((SEQ + 16, WIDTH), bf16),
            pltpu.VMEM((POSITIONS, WIDTH), f32),
            pltpu.VMEM((POSITIONS, WIDTH), bf16),
            pltpu.VMEM((POSITIONS, INNER), bf16),
            pltpu.VMEM((POSITIONS, INNER), f32),
            pltpu.VMEM((POSITIONS, INNER), bf16),
            pltpu.VMEM((POSITIONS, WIDTH), bf16),
            pltpu.VMEM((POSITIONS, WIDTH), f32),
            pltpu.VMEM((POSITIONS, WIDTH), f32),
            pltpu.VMEM((POSITIONS, WIDTH), bf16),
            pltpu.VMEM((KERNEL * KERNEL, TILE, WIDTH), f32),
            pltpu.VMEM((TILE, WIDTH), f32),
            pltpu.VMEM((2, N_DEC // 2, 16, WIDTH), bf16),
            pltpu.SemaphoreType.DMA((24,)),
        ],
        compiler_params=pltpu.CompilerParams(vmem_limit_bytes=VMEM_BYTES),
        cost_estimate=pl.CostEstimate(
            flops=8 * POSITIONS * WIDTH * INNER, bytes_accessed=10 << 20, transcendentals=0
        ),
        name="block_backward",
    )(
        place, own, other, patches, *map(in_hbm, stored[:3]), stored[3], in_hbm(depth_w), gain,
        in_hbm(up), in_hbm(down), layer,
    )


def place_kernel(place_ref, spans_ref, feat_ref, out_ref, rows_ref):
    base = (2 * place_ref[0] + place_ref[1]) * SHARD
    rows_ref[...] = jnp.zeros((FEAT_TILE + SHARD + FEAT_TILE, WIDTH), f32)

    def one(k, carry):
        d = lax.div(k, SLOTS)
        j = k - d * SLOTS
        to = spans_ref[d] + FEAT_TILE * j - base

        @pl.when((j < spans_ref[N_DEC + d]) & (to > -FEAT_TILE) & (to < SHARD))
        def _():
            at = pl.ds(pl.multiple_of(j * FEAT_TILE, FEAT_TILE), FEAT_TILE)
            chunk = lax.div(to + FEAT_TILE, 16)
            row = lax.broadcasted_iota(jnp.int32, (32, FEAT_TILE), 0)
            col = lax.broadcasted_iota(jnp.int32, (32, FEAT_TILE), 1)
            pick = jnp.where(row == col + (to + FEAT_TILE - 16 * chunk), 1.0, 0.0).astype(bf16)
            window = pl.ds(pl.multiple_of(chunk * 16, 16), 32)
            rows_ref[window, :] += jnp.dot(pick, feat_ref[d, at, :], preferred_element_type=f32)

        return carry

    lax.fori_loop(0, N_DEC * SLOTS, one, 0)
    out_ref[...] = rows_ref[FEAT_TILE : FEAT_TILE + SHARD, :].astype(bf16)


def place_features(place, spans, feat):
    vmem = pl.BlockSpec(memory_space=pltpu.VMEM)
    smem = pl.BlockSpec(memory_space=pltpu.SMEM)
    return pl.pallas_call(
        place_kernel,
        out_shape=jax.ShapeDtypeStruct((SHARD, WIDTH), bf16),
        in_specs=[smem, smem, vmem],
        out_specs=vmem,
        scratch_shapes=[pltpu.VMEM((FEAT_TILE + SHARD + FEAT_TILE, WIDTH), f32)],
        compiler_params=pltpu.CompilerParams(vmem_limit_bytes=VMEM_BYTES),
        name="place_features",
    )(place, spans, feat)


def unpack_kernel(
    place_ref, own_ref, other_ref, stem_ref, depth_ref, gain_ref, up_ref, down_ref, scale_ref, rows_ref
):
    core = place_ref[1]
    factor = 1.0 / math.sqrt(N_OWNERS * MEAN_TILES * FEAT_TILE)
    rows_ref[pl.ds(pl.multiple_of(core * HALF_ROWS, 16), HALF_ROWS), :] = own_ref[...]
    rows_ref[pl.ds(pl.multiple_of((1 - core) * HALF_ROWS, 16), HALF_ROWS), :] = other_ref[...]

    def piece(at, count):
        return rows_ref[at : at + count, :].astype(f32) * factor

    for k in range(INNER // LANES):
        up_ref[:, lanes(k)] = piece(UP_AT + k * WIDTH, WIDTH)
    for chunk in range(CHUNKS):
        down_ref[:, lanes(chunk)] = piece(DOWN_AT + chunk * INNER, INNER)
        stem_ref[:, lanes(chunk)] = piece(STEM_AT + chunk * PATCH_CH, PATCH_CH)
        small = piece(SMALL_AT + chunk * SMALL_ROWS, SMALL_ROWS)
        taps = KERNEL * KERNEL
        depth_ref[:, lanes(chunk)] = small[:taps]
        scale_ref[lanes(chunk)] = small[taps]
        gain_ref[lanes(chunk)] = small[taps + 1]


def unpack(place, own, other):
    vmem = pl.BlockSpec(memory_space=pltpu.VMEM)
    smem = pl.BlockSpec(memory_space=pltpu.SMEM)
    shapes = (
        (PATCH_CH, WIDTH),
        (KERNEL * KERNEL, WIDTH),
        (WIDTH,),
        (WIDTH, INNER),
        (INNER, WIDTH),
        (WIDTH,),
    )
    return pl.pallas_call(
        unpack_kernel,
        out_shape=[jax.ShapeDtypeStruct(shape, f32) for shape in shapes],
        in_specs=[smem, vmem, vmem],
        out_specs=[vmem] * 6,
        scratch_shapes=[pltpu.VMEM((PACK_ROWS, LANES), bf16)],
        compiler_params=pltpu.CompilerParams(vmem_limit_bytes=VMEM_BYTES),
        name="unpack_terms",
    )(place, own, other)


def prepare_kernel(count_hbm, gap_hbm, embed_hbm, out_hbm, rows_ref, count_ref, gap_ref, sems):
    copies = Copies(sems)
    count_in = copies.start(count_hbm, count_ref)
    gap_in = copies.start(gap_hbm, gap_ref)
    rows_in = copies.start(embed_hbm.at[0], rows_ref.at[:SHARD])
    count_in.wait()
    gap_in.wait()
    lane = lax.broadcasted_iota(jnp.int32, (16, WIDTH), 1)
    count, gap = count_ref[0, 0].astype(f32), gap_ref[0, 0].astype(f32)
    rows_ref[SHARD:, :] = jnp.where(lane == 0, count, jnp.where(lane == 1, gap, 0.0)).astype(bf16)
    rows_in.wait()
    outs = [copies.start(rows_ref, out_hbm.at[y]) for y in range(N_DEC // 2)]
    for out in outs:
        out.wait()


def prepare(tile_counts, text_gaps, embed_grad):
    hbm = pl.BlockSpec(memory_space=pltpu.HBM)
    return pl.pallas_call(
        prepare_kernel,
        out_shape=pltpu.HBM((N_DEC // 2, SHARD + 16, WIDTH), bf16),
        in_specs=[pl.BlockSpec(memory_space=pl.ANY)] * 2 + [hbm],
        out_specs=hbm,
        scratch_shapes=[
            pltpu.VMEM((SHARD + 16, WIDTH), bf16),
            pltpu.SMEM((1, 1), jnp.int32),
            pltpu.SMEM((1, 1), jnp.int32),
            pltpu.SemaphoreType.DMA((8,)),
        ],
        compiler_params=pltpu.CompilerParams(vmem_limit_bytes=VMEM_BYTES),
        name="prepare_rows",
    )(tile_counts, text_gaps, in_hbm(embed_grad))


def swap_blocks(blocks, axes):
    return lax.all_to_all(blocks, axes, 0, 0, tiled=True)


def sum_blocks(blocks):
    return jnp.sum(blocks.astype(f32), axis=0).astype(bf16)


def spread(block, copies):
    return jnp.broadcast_to(block[None], (copies,) + block.shape)


def swap_cores(x):
    return lax.ppermute(x, "core", [(0, 1), (1, 0)])


def sum_all(half, beside):
    part = sum_blocks(swap_blocks(half.reshape(16, PACK_ROWS // 32, LANES), PLANE))
    part = sum_blocks(swap_blocks(spread(part, 4), "zl"))
    part = sum_blocks(swap_blocks(spread(part, 4), "zh"))
    part, beside = lax.optimization_barrier((part, beside))
    return swap_blocks(spread(part, 16), PLANE).reshape(HALF_ROWS, LANES), beside


def order_patches(tiles):
    patches = tiles.reshape(SLOTS, TILE * TILE, PATCH_CH)
    lead = patches[:LEAD].transpose(1, 0, 2).reshape(LEAD_ROWS, PATCH_CH)
    return jnp.concatenate([lead, patches[LEAD]])


def on_device(
    pixels,
    tile_counts,
    text_gaps,
    stem_weight,
    depth_weight,
    norm_gain,
    up_weight,
    down_weight,
    layer_scale,
    embed_grad,
):
    place = jnp.stack([lax.axis_index("y"), lax.axis_index("core")]).astype(jnp.int32)
    gain = norm_gain.reshape(1, WIDTH)
    layer = layer_scale.reshape(1, WIDTH)
    patches = order_patches(pixels[0])
    own = swap_blocks(prepare(tile_counts, text_gaps, embed_grad), "y")
    *stored, feat = forward(
        tile_counts, patches, stem_weight, depth_weight, gain, up_weight, down_weight, layer
    )
    own, feat, place = lax.optimization_barrier((own, feat, place))
    other = swap_cores(own)
    feats = swap_blocks(feat, DEC)
    mine, theirs, spans = backward(
        place, own, other, patches, stored, depth_weight, gain, up_weight, down_weight, layer
    )
    theirs, feats = lax.optimization_barrier((theirs, feats))
    half = (mine.astype(f32) + swap_cores(theirs).astype(f32)).astype(bf16)
    sequence = place_features(place, spans, feats)
    half, sequence = sum_all(half, sequence)
    stem, depth, gain_grad, up, down, scale = unpack(place, half, swap_cores(half))
    return sequence[None], stem, depth, gain_grad, up, down, scale


def solution(mesh):
    fine = Mesh(mesh.devices.reshape(4, 4, 4, 4, 2), ("x", "zh", "zl", "y", "core"))
    return jax.shard_map(
        on_device,
        mesh=fine,
        in_specs=(
            P(DEC, ENC, None),
            P(DEC, ENC),
            P(DEC, ENC),
            P(),
            P(),
            P(),
            P(),
            P(),
            P(),
            P(ENC, DEC, None),
        ),
        out_specs=(P(ENC, DEC, None), P(), P(), P(), P(), P(), P()),
        check_vma=False,
    )
```

time: 127 us -> 125 us (0.984)
  blocking collectives: 45.2 us -> 38.7 us
  waiting for transfers between devices: 11.4 us -> 14.4 us
  starting transfers between devices: 37.7 us -> 40.2 us
  Pallas kernels: 27.7 us -> 26.1 us
    all_to_all x4 -> x3, blocking collectives: 45.2 us -> 38.7 us  [swap_blocks(): return lax.all_to_all(blocks, axes, 0, 0, tiled=True)]
    ppermute x2 -> x3, starting transfers between devices: 16.6 us -> 19.5 us  [swap_cores(): return lax.ppermute(x, 'core', [(0, 1), (1, 0)])]
    ppermute x2 -> x3, waiting for transfers between devices: 1.7 us -> 3.62 us  [swap_cores(): return lax.ppermute(x, 'core', [(0, 1), (1, 0)])]
    convert_element_type x0 -> x1, other arithmetic: none -> 1.29 us  [on_device(): half = (mine.astype(f32) + swap_cores(theirs).astype(f32)).astype(bf16)]
  transfers between devices with their start and end apart: 5 -> 6, of which waited for: 3 -> 5; matrix products, arithmetic and copies ran while one was open for 0% -> 0% of each run, Pallas kernels for 19% -> 18%
where the time goes in v4:
time: 125 us; the launch traced here: 124 us
  starting transfers between devices  40.2 us (32%)
  blocking collectives  38.7 us (31%)
  Pallas kernels  26.1 us (21%)
  waiting for transfers between devices  14.4 us (12%)
  between operations  2.14 us (2%)
  other arithmetic  1.55 us (1%)
    all_to_all x3, blocking collectives, swap_blocks(): return lax.all_to_all(blocks, axes, 0, 0, tiled=True)  38.7 us
    all_to_all x3, starting transfers between devices, swap_blocks(): return lax.all_to_all(blocks, axes, 0, 0, tiled=True)  20.6 us
    ppermute x3, starting transfers between devices, swap_cores(): return lax.ppermute(x, 'core', [(0, 1), (1, 0)])  19.5 us
    pallas_call x1, Pallas kernels, backward(): pl.pallas_call(backward_kernel, out_shape=[pltpu.HBM((HALF_ROWS, LANES),...  12.2 us
    all_to_all x3, waiting for transfers between devices, swap_blocks(): return lax.all_to_all(blocks, axes, 0, 0, tiled=True)  10.7 us
    pallas_call x1, Pallas kernels, forward(): pl.pallas_call(forward_kernel, out_shape=[pltpu.HBM(*shape) for shape in...  6.59 us
    ppermute x3, waiting for transfers between devices, swap_cores(): return lax.ppermute(x, 'core', [(0, 1), (1, 0)])  3.62 us
    pallas_call x1, Pallas kernels, place_features(): pl.pallas_call(place_kernel, out_shape=jax.ShapeDtypeStruct((SHARD, WIDTH...  3.23 us
  transfers between devices with their start and end apart: 6, of which 5 were waited for; matrix products, arithmetic and copies ran while one was open for 0% of the time, Pallas kernels for 18%

profile of v4, /device:TPU:1, one launch (start us, length us, event | category | flops | bytes accessed | tf_op | source)
XLA Modules:
  0.0 124.2 jit_solution(5920119578793779791)
XLA Ops:
  2.0 1.9 %prepare_rows.1 = bf16[4,224,384]{2,1,0:T(8,128)(2,1)} custom-call(s32[1,1]{1,0:T(1,128)S(6)} %copy.30.count_hbm.count_ref, s32[1,1]{1,0:T(1,128)S(6)} %copy.31.gap_hbm, bf16[1,208,384]{2,1,0:T(8,128)(2,1)} %embed_hbm.1), custom_call_target="tpu_custom_call" | custom-call | tf_op jit(solution)/shard_map/prepare_rows/pallas_call | solution.py:607
  3.9 5.0 %all-to-all-start = ((bf16[4,224,384]{2,1,0:T(8,128)(2,1)}), bf16[4,224,384]{2,1,0:T(8,128)(2,1)S(1)}, u32[]{:S(2)}, u32[]{:S(2)}) async-start(bf16[4,224,384]{2,1,0:T(8,128)(2,1)} %prepare_rows.1), calls=%async_computation | async-start | bytes 1376256 | tf_op jit(solution)/shard_map/all_to_all | solution.py:624
  9.1 0.2 slice.11
  9.2 0.1 copy.29
  9.4 6.6 %block_forward.1 = (bf16[576,384]{1,0:T(8,128)(2,1)}, f32[576,384]{1,0:T(8,128)}, bf16[576,768]{1,0:T(8,128)(2,1)}, f32[576,128]{1,0:T(8,128)S(1)}, bf16[8,144,384]{2,1,0:T(8,128)(2,1)}) custom-call(s32[1,1]{1,0:T(1,128)S(6)} %copy.30.count_hbm.count_ref, bf16[576,48]{1,0:T(8,128)(2,1)S(1)} %pad_maximum_fusion.patches_ref, bf16[48,384]{1,0:T(8,128)(2,1)} %stem_w_hbm.1, ...), custom_call_target="tpu_custom_call" | custom-call | flops 679477248 | bytes 8388608 | tf_op jit(solution)/shard_map/block_forward/pallas_call | solution.py:227
  16.1 0.6 all-to-all-done.own_ref
  16.7 8.4 %collective-permute-start = (bf16[4,224,384]{2,1,0:T(8,128)(2,1)S(1)}, bf16[4,224,384]{2,1,0:T(8,128)(2,1)S(1)}, u32[]{:S(2)}, u32[]{:S(2)}) collective-permute-start(bf16[4,224,384]{2,1,0:T(8,128)(2,1)S(1)} %all-to-all-done.own_ref), channel_id=1, source_target_pairs={{0,1},{1,0},{2,3},{3,2},{4,5},{5,4},{6,7},{7,6},{8,9},{9,8},{10,11... | collective-permute-start | bytes 2064392 | tf_op jit(solution)/shard_map/ppermute | solution.py:636
  25.1 3.5 %all-to-all-start.1 = ((bf16[8,144,384]{2,1,0:T(8,128)(2,1)}), bf16[8,144,384]{2,1,0:T(8,128)(2,1)S(1)}, u32[]{:S(2)}, u32[]{:S(2)}) async-start(bf16[8,144,384]{2,1,0:T(8,128)(2,1)} %get-tuple-element.37), calls=%async_computation.1 | async-start | bytes 1769472 | tf_op jit(solution)/shard_map/all_to_all | solution.py:624
  28.6 12.2 %block_backward.1 = (bf16[2560,128]{1,0:T(8,128)(2,1)}, bf16[2560,128]{1,0:T(8,128)(2,1)}, s32[16]{0:T(128)S(1)}) custom-call(s32[2]{0:T(128)S(1)} %pad_add_fusion.place_ref, bf16[4,224,384]{2,1,0:T(8,128)(2,1)S(1)} %all-to-all-done.own_ref, bf16[4,224,384]{2,1,0:T(8,128)(2,1)S(1)} %collective-permute-done.other_ref, ...), custom_call_target="tpu_custom_call" | custom-call | flops 1358954496 | bytes 10485760 | tf_op jit(solution)/shard_map/block_backward/pallas_call | solution.py:461
  40.9 1.1 all-to-all-done.1.feat_ref
  41.9 2.8 %collective-permute-start.1 = (bf16[2560,128]{1,0:T(8,128)(2,1)}, bf16[2560,128]{1,0:T(8,128)(2,1)S(1)}, u32[]{:S(2)}, u32[]{:S(2)}) collective-permute-start(bf16[2560,128]{1,0:T(8,128)(2,1)} %get-tuple-element.38), channel_id=1, source_target_pairs={{0,1},{1,0},{2,3},{3,2},{4,5},{5,4},{6,7},{7,6},{8,9},{9,8},{10,11... | collective-permute-start | bytes 1966088 | tf_op jit(solution)/shard_map/ppermute | solution.py:636
  44.7 1.9 %collective-permute-done.1 = bf16[2560,128]{1,0:T(8,128)(2,1)S(1)} collective-permute-done((bf16[2560,128]{1,0:T(8,128)(2,1)}, bf16[2560,128]{1,0:T(8,128)(2,1)S(1)}, u32[]{:S(2)}, u32[]{:S(2)}) %collective-permute-start.1) | collective-permute-done | bytes 655392 | tf_op jit(solution)/shard_map/ppermute | solution.py:636
  46.6 1.3 %add_convert_fusion = bf16[2560,128]{1,0:T(8,128)(2,1)S(1)} fusion(bf16[2560,128]{1,0:T(8,128)(2,1)S(1)} %collective-permute-done.1, bf16[2560,128]{1,0:T(8,128)(2,1)} %get-tuple-element.35), kind=kLoop, calls=%fused_computation | loop fusion | flops 1310720 | bytes 1966080 | tf_op jit(solution)/shard_map/convert_element_type | solution.py:680
  47.9 14.9 %all_to_all.30 = bf16[16,160,128]{2,1,0:T(8,128)(2,1)S(1)} all-to-all(bf16[16,160,128]{2,1,0:T(8,128)(2,1)S(1)} %bitcast.11), channel_id=1, replica_groups=mesh['x'=4,'zh'=4,'zl'=4,'y'=4,'core'=2] {'x','y'}, dimensions={0} | all-to-all | bytes 1310720 | tf_op jit(solution)/shard_map/all_to_all | solution.py:624
  62.8 0.1 reduce_sum.36
  62.9 11.0 %all_to_all.31 = bf16[4,160,128]{2,1,0:T(8,128)(2,1)S(1)} all-to-all(bf16[4,160,128]{2,1,0:T(8,128)(2,1)S(1)} %broadcast_in_dim.8), channel_id=1, replica_groups=mesh['x'=4,'zh'=4,'zl'=4,'y'=4,'core'=2] {'zl'}, dimensions={0} | all-to-all | bytes 327680 | tf_op jit(solution)/shard_map/all_to_all | solution.py:624
  73.9 0.7 broadcast_in_dim.9
  74.6 12.1 %all-to-all-start.4 = ((bf16[4,160,128]{2,1,0:T(8,128)(2,1)}), bf16[4,160,128]{2,1,0:T(8,128)(2,1)S(1)}, u32[]{:S(2)}, u32[]{:S(2)}) async-start(bf16[4,160,128]{2,1,0:T(8,128)(2,1)} %broadcast_in_dim.9), calls=%async_computation.4 | async-start | bytes 327680 | tf_op jit(solution)/shard_map/all_to_all | solution.py:624
  86.7 3.2 %place_features.1 = bf16[208,384]{1,0:T(8,128)(2,1)} custom-call(s32[2]{0:T(128)S(1)} %pad_add_fusion.place_ref, s32[16]{0:T(128)S(1)} %get-tuple-element.39.spans_ref, bf16[8,144,384]{2,1,0:T(8,128)(2,1)S(1)} %all-to-all-done.1.feat_ref), custom_call_target="tpu_custom_call" | custom-call | tf_op jit(solution)/shard_map/place_features/pallas_call | solution.py:533
  90.0 9.0 %all-to-all-done.4 = bf16[4,160,128]{2,1,0:T(8,128)(2,1)S(1)} async-done(((bf16[4,160,128]{2,1,0:T(8,128)(2,1)}), bf16[4,160,128]{2,1,0:T(8,128)(2,1)S(1)}, u32[]{:S(2)}, u32[]{:S(2)}) %all-to-all-start.4) | async-done | bytes 163872 | tf_op jit(solution)/shard_map/all_to_all | solution.py:624
  99.1 12.8 %all_to_all.32 = bf16[16,160,128]{2,1,0:T(8,128)(2,1)S(1)} all-to-all(bf16[16,160,128]{2,1,0:T(8,128)(2,1)S(1)} %broadcast_in_dim.11), channel_id=1, replica_groups=mesh['x'=4,'zh'=4,'zl'=4,'y'=4,'core'=2] {'x','y'}, dimensions={0} | all-to-all | bytes 1310720 | tf_op jit(solution)/shard_map/all_to_all | solution.py:624
  111.9 8.4 %collective-permute-start.2 = (bf16[2560,128]{1,0:T(8,128)(2,1)S(1)}, bf16[2560,128]{1,0:T(8,128)(2,1)S(1)}, u32[]{:S(2)}, u32[]{:S(2)}) collective-permute-start(bf16[2560,128]{1,0:T(8,128)(2,1)S(1)} %bitcast.9), channel_id=1, source_target_pairs={{0,1},{1,0},{2,3},{3,2},{4,5},{5,4},{6,7},{7,6},{8,9},{9,8},{10,11... | collective-permute-start | bytes 1966088 | tf_op jit(solution)/shard_map/ppermute | solution.py:636
  120.3 1.7 %collective-permute-done.2.other_ref = bf16[2560,128]{1,0:T(8,128)(2,1)S(1)} collective-permute-done((bf16[2560,128]{1,0:T(8,128)(2,1)S(1)}, bf16[2560,128]{1,0:T(8,128)(2,1)S(1)}, u32[]{:S(2)}, u32[]{:S(2)}) %collective-permute-start.2) | collective-permute-done | bytes 655392 | tf_op jit(solution)/shard_map/ppermute | solution.py:636
  122.0 2.2 %unpack_terms.1 = (f32[48,384]{1,0:T(8,128)}, f32[49,384]{1,0:T(8,128)}, f32[384]{0:T(512)}, f32[384,768]{1,0:T(8,128)}, f32[768,384]{1,0:T(8,128)}, /*index=5*/f32[384]{0:T(512)}) custom-call(s32[2]{0:T(128)S(1)} %pad_add_fusion.place_ref, bf16[2560,128]{1,0:T(8,128)(2,1)S(1)} %bitcast.10, bf16[2560,128]{1,0:T(8,128)(2,1)S(1)} %collective-permute-done.2.other_ref), custom_call_target="tpu_custom_call" | custom-call | tf_op jit(solution)/shard_map/unpack_terms/pallas_call | solution.py:578
  (19 shorter events, 0.4 us)
Async XLA Ops:
  0.6 8.3 %copy-start.1 = (f32[384]{0:T(512)S(1)}, f32[384]{0:T(512)}, u32[]{:S(2)}) copy-start(f32[384]{0:T(512)} %param.15) | copy-start | bytes 4612
  0.6 8.3 %copy-start.2 = (f32[384]{0:T(512)S(1)}, f32[384]{0:T(512)}, u32[]{:S(2)}) copy-start(f32[384]{0:T(512)} %param.18) | copy-start | bytes 4612
  0.7 8.3 %copy-start = (bf16[1,9,3072]{2,1,0:T(8,128)(2,1)S(1)}, bf16[1,9,3072]{2,1,0:T(8,128)(2,1)}, u32[]{:S(2)}) copy-start(bf16[1,9,3072]{2,1,0:T(8,128)(2,1)} %param.10) | copy-start | bytes 165892
  2.0 7.1 %slice-start = ((bf16[1,9,3072]{2,1,0:T(8,128)(2,1)}), bf16[1,8,3072]{2,1,0:T(8,128)(2,1)S(1)}, s32[]{:S(2)}) async-start(bf16[1,9,3072]{2,1,0:T(8,128)(2,1)} %param.10), calls=%async_computation.6 | async-start | bytes 98304 | tf_op jit(solution)/shard_map/slice | solution.py:649
  3.9 12.8 %all-to-all-start = ((bf16[4,224,384]{2,1,0:T(8,128)(2,1)}), bf16[4,224,384]{2,1,0:T(8,128)(2,1)S(1)}, u32[]{:S(2)}, u32[]{:S(2)}) async-start(bf16[4,224,384]{2,1,0:T(8,128)(2,1)} %prepare_rows.1), calls=%async_computation | async-start | bytes 1376256 | tf_op jit(solution)/shard_map/all_to_all | solution.py:624
  16.7 11.9 %collective-permute-start = (bf16[4,224,384]{2,1,0:T(8,128)(2,1)S(1)}, bf16[4,224,384]{2,1,0:T(8,128)(2,1)S(1)}, u32[]{:S(2)}, u32[]{:S(2)}) collective-permute-start(bf16[4,224,384]{2,1,0:T(8,128)(2,1)S(1)} %all-to-all-done.own_ref), channel_id=1, source_target_pairs={{0,1},{1,0},{2,3},{3,2},{4,5},{5,4},{6,7},{7,6},{8,9},{9,8},{10,11... | collective-permute-start | bytes 2064392 | tf_op jit(solution)/shard_map/ppermute | solution.py:636
  25.1 16.8 %all-to-all-start.1 = ((bf16[8,144,384]{2,1,0:T(8,128)(2,1)}), bf16[8,144,384]{2,1,0:T(8,128)(2,1)S(1)}, u32[]{:S(2)}, u32[]{:S(2)}) async-start(bf16[8,144,384]{2,1,0:T(8,128)(2,1)} %get-tuple-element.37), calls=%async_computation.1 | async-start | bytes 1769472 | tf_op jit(solution)/shard_map/all_to_all | solution.py:624
  41.9 4.7 %collective-permute-start.1 = (bf16[2560,128]{1,0:T(8,128)(2,1)}, bf16[2560,128]{1,0:T(8,128)(2,1)S(1)}, u32[]{:S(2)}, u32[]{:S(2)}) collective-permute-start(bf16[2560,128]{1,0:T(8,128)(2,1)} %get-tuple-element.38), channel_id=1, source_target_pairs={{0,1},{1,0},{2,3},{3,2},{4,5},{5,4},{6,7},{7,6},{8,9},{9,8},{10,11... | collective-permute-start | bytes 1966088 | tf_op jit(solution)/shard_map/ppermute | solution.py:636
  74.6 24.4 %all-to-all-start.4 = ((bf16[4,160,128]{2,1,0:T(8,128)(2,1)}), bf16[4,160,128]{2,1,0:T(8,128)(2,1)S(1)}, u32[]{:S(2)}, u32[]{:S(2)}) async-start(bf16[4,160,128]{2,1,0:T(8,128)(2,1)} %broadcast_in_dim.9), calls=%async_computation.4 | async-start | bytes 327680 | tf_op jit(solution)/shard_map/all_to_all | solution.py:624
  111.9 10.1 %collective-permute-start.2 = (bf16[2560,128]{1,0:T(8,128)(2,1)S(1)}, bf16[2560,128]{1,0:T(8,128)(2,1)S(1)}, u32[]{:S(2)}, u32[]{:S(2)}) collective-permute-start(bf16[2560,128]{1,0:T(8,128)(2,1)S(1)} %bitcast.9), channel_id=1, source_target_pairs={{0,1},{1,0},{2,3},{3,2},{4,5},{5,4},{6,7},{7,6},{8,9},{9,8},{10,11... | collective-permute-start | bytes 1966088 | tf_op jit(solution)/shard_map/ppermute | solution.py:636

commit v5 on v4

--- a/solution.py
+++ b/solution.py
@@ -36,7 +36,9 @@
 SMALL_AT = HALF_ROWS + LATE_AT
 SMALL_ROWS = 64
 DEC = ("y", "core")
-ENC = ("x", "zh", "zl")
+ENC = ("x", "z")
+RUNS = [[4 * g + k for k in range(4)] for g in range(4)]
+ACROSS = [[0, 6, 10, 12], [1, 7, 11, 13], [2, 4, 8, 14], [3, 5, 9, 15]]
 PLANE = ("x", "y")
 VMEM_BYTES = 24 * 1024 * 1024
 
@@ -620,8 +622,8 @@
     )(tile_counts, text_gaps, in_hbm(embed_grad))
 
 
-def swap_blocks(blocks, axes):
-    return lax.all_to_all(blocks, axes, 0, 0, tiled=True)
+def swap_blocks(blocks, axes, groups=None):
+    return lax.all_to_all(blocks, axes, 0, 0, axis_index_groups=groups, tiled=True)
 
 
 def sum_blocks(blocks):
@@ -638,8 +640,8 @@
 
 def sum_all(half, beside):
     part = sum_blocks(swap_blocks(half.reshape(16, PACK_ROWS // 32, LANES), PLANE))
-    part = sum_blocks(swap_blocks(spread(part, 4), "zl"))
-    part = sum_blocks(swap_blocks(spread(part, 4), "zh"))
+    part = sum_blocks(swap_blocks(spread(part, 4), "z", RUNS))
+    part = sum_blocks(swap_blocks(spread(part, 4), "z", ACROSS))
     part, beside = lax.optimization_barrier((part, beside))
     return swap_blocks(spread(part, 16), PLANE).reshape(HALF_ROWS, LANES), beside
 
@@ -685,7 +687,7 @@
 
 
 def solution(mesh):
-    fine = Mesh(mesh.devices.reshape(4, 4, 4, 4, 2), ("x", "zh", "zl", "y", "core"))
+    fine = Mesh(mesh.devices.reshape(4, 16, 4, 2), ("x", "z", "y", "core"))
     return jax.shard_map(
         on_device,
         mesh=fine,

time: 125 us -> 123 us (0.984)
  waiting for transfers between devices: 14.4 us -> 12.3 us
    all_to_all x3, waiting for transfers between devices: 10.7 us -> 8.73 us  [swap_blocks(): lax.all_to_all(blocks, axes, 0, 0, axis_index_groups=groups, tiled=True)]
    all_to_all x3, starting transfers between devices: 20.6 us -> 18.9 us  [swap_blocks(): lax.all_to_all(blocks, axes, 0, 0, axis_index_groups=groups, tiled=True)]
where the time goes in v5:
time: 123 us; the launch traced here: 122 us
  starting transfers between devices  39.5 us (32%)
  blocking collectives  38.7 us (31%)
  Pallas kernels  26.5 us (22%)
  waiting for transfers between devices  12.3 us (10%)
  between operations  2.14 us (2%)
  other arithmetic  1.55 us (1%)
    all_to_all x3, blocking collectives, swap_blocks(): lax.all_to_all(blocks, axes, 0, 0, axis_index_groups=groups, tiled=True)  38.7 us
    ppermute x3, starting transfers between devices, swap_cores(): return lax.ppermute(x, 'core', [(0, 1), (1, 0)])  20.6 us
    all_to_all x3, starting transfers between devices, swap_blocks(): lax.all_to_all(blocks, axes, 0, 0, axis_index_groups=groups, tiled=True)  18.9 us
    pallas_call x1, Pallas kernels, backward(): pl.pallas_call(backward_kernel, out_shape=[pltpu.HBM((HALF_ROWS, LANES),...  12.2 us
    all_to_all x3, waiting for transfers between devices, swap_blocks(): lax.all_to_all(blocks, axes, 0, 0, axis_index_groups=groups, tiled=True)  8.73 us
    pallas_call x1, Pallas kernels, forward(): pl.pallas_call(forward_kernel, out_shape=[pltpu.HBM(*shape) for shape in...  6.59 us
    pallas_call x1, Pallas kernels, place_features(): pl.pallas_call(place_kernel, out_shape=jax.ShapeDtypeStruct((SHARD, WIDTH...  3.63 us
    ppermute x3, waiting for transfers between devices, swap_cores(): return lax.ppermute(x, 'core', [(0, 1), (1, 0)])  3.62 us
  transfers between devices with their start and end apart: 6, of which 5 were waited for; matrix products, arithmetic and copies ran while one was open for 0% of the time, Pallas kernels for 18%

profile of v5, /device:TPU:1, one launch (start us, length us, event | category | flops | bytes accessed | tf_op | source)
XLA Modules:
  0.0 121.9 jit_solution(5262715473799974116)
XLA Ops:
  2.0 1.9 %prepare_rows.1 = bf16[4,224,384]{2,1,0:T(8,128)(2,1)} custom-call(s32[1,1]{1,0:T(1,128)S(6)} %copy.30.count_hbm.count_ref, s32[1,1]{1,0:T(1,128)S(6)} %copy.31.gap_hbm, bf16[1,208,384]{2,1,0:T(8,128)(2,1)} %embed_hbm.1), custom_call_target="tpu_custom_call" | custom-call | tf_op jit(solution)/shard_map/prepare_rows/pallas_call | solution.py:609
  3.9 5.0 %all-to-all-start = ((bf16[4,224,384]{2,1,0:T(8,128)(2,1)}), bf16[4,224,384]{2,1,0:T(8,128)(2,1)S(1)}, u32[]{:S(2)}, u32[]{:S(2)}) async-start(bf16[4,224,384]{2,1,0:T(8,128)(2,1)} %prepare_rows.1), calls=%async_computation | async-start | bytes 1376256 | tf_op jit(solution)/shard_map/all_to_all | solution.py:626
  9.1 0.2 slice.11
  9.2 0.1 copy.29
  9.4 6.6 %block_forward.1 = (bf16[576,384]{1,0:T(8,128)(2,1)}, f32[576,384]{1,0:T(8,128)}, bf16[576,768]{1,0:T(8,128)(2,1)}, f32[576,128]{1,0:T(8,128)S(1)}, bf16[8,144,384]{2,1,0:T(8,128)(2,1)}) custom-call(s32[1,1]{1,0:T(1,128)S(6)} %copy.30.count_hbm.count_ref, bf16[576,48]{1,0:T(8,128)(2,1)S(1)} %pad_maximum_fusion.patches_ref, bf16[48,384]{1,0:T(8,128)(2,1)} %stem_w_hbm.1, ...), custom_call_target="tpu_custom_call" | custom-call | flops 679477248 | bytes 8388608 | tf_op jit(solution)/shard_map/block_forward/pallas_call | solution.py:229
  16.1 0.6 all-to-all-done.own_ref
  16.7 8.4 %collective-permute-start = (bf16[4,224,384]{2,1,0:T(8,128)(2,1)S(1)}, bf16[4,224,384]{2,1,0:T(8,128)(2,1)S(1)}, u32[]{:S(2)}, u32[]{:S(2)}) collective-permute-start(bf16[4,224,384]{2,1,0:T(8,128)(2,1)S(1)} %all-to-all-done.own_ref), channel_id=1, source_target_pairs={{0,1},{1,0},{2,3},{3,2},{4,5},{5,4},{6,7},{7,6},{8,9},{9,8},{10,11... | collective-permute-start | bytes 2064392 | tf_op jit(solution)/shard_map/ppermute | solution.py:638
  25.1 3.5 %all-to-all-start.1 = ((bf16[8,144,384]{2,1,0:T(8,128)(2,1)}), bf16[8,144,384]{2,1,0:T(8,128)(2,1)S(1)}, u32[]{:S(2)}, u32[]{:S(2)}) async-start(bf16[8,144,384]{2,1,0:T(8,128)(2,1)} %get-tuple-element.37), calls=%async_computation.1 | async-start | bytes 1769472 | tf_op jit(solution)/shard_map/all_to_all | solution.py:626
  28.6 12.2 %block_backward.1 = (bf16[2560,128]{1,0:T(8,128)(2,1)}, bf16[2560,128]{1,0:T(8,128)(2,1)}, s32[16]{0:T(128)S(1)}) custom-call(s32[2]{0:T(128)S(1)} %pad_add_fusion.place_ref, bf16[4,224,384]{2,1,0:T(8,128)(2,1)S(1)} %all-to-all-done.own_ref, bf16[4,224,384]{2,1,0:T(8,128)(2,1)S(1)} %collective-permute-done.other_ref, ...), custom_call_target="tpu_custom_call" | custom-call | flops 1358954496 | bytes 10485760 | tf_op jit(solution)/shard_map/block_backward/pallas_call | solution.py:463
  40.9 1.1 all-to-all-done.1.feat_ref
  41.9 2.8 %collective-permute-start.1 = (bf16[2560,128]{1,0:T(8,128)(2,1)}, bf16[2560,128]{1,0:T(8,128)(2,1)S(1)}, u32[]{:S(2)}, u32[]{:S(2)}) collective-permute-start(bf16[2560,128]{1,0:T(8,128)(2,1)} %get-tuple-element.38), channel_id=1, source_target_pairs={{0,1},{1,0},{2,3},{3,2},{4,5},{5,4},{6,7},{7,6},{8,9},{9,8},{10,11... | collective-permute-start | bytes 1966088 | tf_op jit(solution)/shard_map/ppermute | solution.py:638
  44.7 1.9 %collective-permute-done.1 = bf16[2560,128]{1,0:T(8,128)(2,1)S(1)} collective-permute-done((bf16[2560,128]{1,0:T(8,128)(2,1)}, bf16[2560,128]{1,0:T(8,128)(2,1)S(1)}, u32[]{:S(2)}, u32[]{:S(2)}) %collective-permute-start.1) | collective-permute-done | bytes 655392 | tf_op jit(solution)/shard_map/ppermute | solution.py:638
  46.6 1.3 %add_convert_fusion = bf16[2560,128]{1,0:T(8,128)(2,1)S(1)} fusion(bf16[2560,128]{1,0:T(8,128)(2,1)S(1)} %collective-permute-done.1, bf16[2560,128]{1,0:T(8,128)(2,1)} %get-tuple-element.35), kind=kLoop, calls=%fused_computation | loop fusion | flops 1310720 | bytes 1966080 | tf_op jit(solution)/shard_map/convert_element_type | solution.py:682
  47.9 14.9 %all_to_all.30 = bf16[16,160,128]{2,1,0:T(8,128)(2,1)S(1)} all-to-all(bf16[16,160,128]{2,1,0:T(8,128)(2,1)S(1)} %bitcast.11), channel_id=1, replica_groups=mesh['x'=4,'z'=16,'y'=4,'core'=2] {'x','y'}, dimensions={0} | all-to-all | bytes 1310720 | tf_op jit(solution)/shard_map/all_to_all | solution.py:626
  62.8 0.1 reduce_sum.36
  62.9 11.0 %all_to_all.31 = bf16[4,160,128]{2,1,0:T(8,128)(2,1)S(1)} all-to-all(bf16[4,160,128]{2,1,0:T(8,128)(2,1)S(1)} %broadcast_in_dim.8), channel_id=1, replica_groups={{0,8,16,24},{32,40,48,56},{64,72,80,88},{96,104,112,120},{1,9,17,25},{3..., dimensions={0} | all-to-all | bytes 327680 | tf_op jit(solution)/shard_map/all_to_all | solution.py:626
  73.9 0.7 broadcast_in_dim.9
  74.6 10.4 %all-to-all-start.4 = ((bf16[4,160,128]{2,1,0:T(8,128)(2,1)}), bf16[4,160,128]{2,1,0:T(8,128)(2,1)S(1)}, u32[]{:S(2)}, u32[]{:S(2)}) async-start(bf16[4,160,128]{2,1,0:T(8,128)(2,1)} %broadcast_in_dim.9), calls=%async_computation.4 | async-start | bytes 327680 | tf_op jit(solution)/shard_map/all_to_all | solution.py:626
  85.0 3.6 %place_features.1 = bf16[208,384]{1,0:T(8,128)(2,1)} custom-call(s32[2]{0:T(128)S(1)} %pad_add_fusion.place_ref, s32[16]{0:T(128)S(1)} %get-tuple-element.39.spans_ref, bf16[8,144,384]{2,1,0:T(8,128)(2,1)S(1)} %all-to-all-done.1.feat_ref), custom_call_target="tpu_custom_call" | custom-call | tf_op jit(solution)/shard_map/place_features/pallas_call | solution.py:535
  88.6 7.0 %all-to-all-done.4 = bf16[4,160,128]{2,1,0:T(8,128)(2,1)S(1)} async-done(((bf16[4,160,128]{2,1,0:T(8,128)(2,1)}), bf16[4,160,128]{2,1,0:T(8,128)(2,1)S(1)}, u32[]{:S(2)}, u32[]{:S(2)}) %all-to-all-start.4) | async-done | bytes 163872 | tf_op jit(solution)/shard_map/all_to_all | solution.py:626
  95.7 12.9 %all_to_all.32 = bf16[16,160,128]{2,1,0:T(8,128)(2,1)S(1)} all-to-all(bf16[16,160,128]{2,1,0:T(8,128)(2,1)S(1)} %broadcast_in_dim.11), channel_id=1, replica_groups=mesh['x'=4,'z'=16,'y'=4,'core'=2] {'x','y'}, dimensions={0} | all-to-all | bytes 1310720 | tf_op jit(solution)/shard_map/all_to_all | solution.py:626
  108.6 9.5 %collective-permute-start.2 = (bf16[2560,128]{1,0:T(8,128)(2,1)S(1)}, bf16[2560,128]{1,0:T(8,128)(2,1)S(1)}, u32[]{:S(2)}, u32[]{:S(2)}) collective-permute-start(bf16[2560,128]{1,0:T(8,128)(2,1)S(1)} %bitcast.9), channel_id=1, source_target_pairs={{0,1},{1,0},{2,3},{3,2},{4,5},{5,4},{6,7},{7,6},{8,9},{9,8},{10,11... | collective-permute-start | bytes 1966088 | tf_op jit(solution)/shard_map/ppermute | solution.py:638
  118.1 1.7 %collective-permute-done.2.other_ref = bf16[2560,128]{1,0:T(8,128)(2,1)S(1)} collective-permute-done((bf16[2560,128]{1,0:T(8,128)(2,1)S(1)}, bf16[2560,128]{1,0:T(8,128)(2,1)S(1)}, u32[]{:S(2)}, u32[]{:S(2)}) %collective-permute-start.2) | collective-permute-done | bytes 655392 | tf_op jit(solution)/shard_map/ppermute | solution.py:638
  119.8 2.2 %unpack_terms.1 = (f32[48,384]{1,0:T(8,128)}, f32[49,384]{1,0:T(8,128)}, f32[384]{0:T(512)}, f32[384,768]{1,0:T(8,128)}, f32[768,384]{1,0:T(8,128)}, /*index=5*/f32[384]{0:T(512)}) custom-call(s32[2]{0:T(128)S(1)} %pad_add_fusion.place_ref, bf16[2560,128]{1,0:T(8,128)(2,1)S(1)} %bitcast.10, bf16[2560,128]{1,0:T(8,128)(2,1)S(1)} %collective-permute-done.2.other_ref), custom_call_target="tpu_custom_call" | custom-call | tf_op jit(solution)/shard_map/unpack_terms/pallas_call | solution.py:580
  (19 shorter events, 0.4 us)
Async XLA Ops:
  0.6 8.3 %copy-start.1 = (f32[384]{0:T(512)S(1)}, f32[384]{0:T(512)}, u32[]{:S(2)}) copy-start(f32[384]{0:T(512)} %param.15) | copy-start | bytes 4612
  0.6 8.3 %copy-start.2 = (f32[384]{0:T(512)S(1)}, f32[384]{0:T(512)}, u32[]{:S(2)}) copy-start(f32[384]{0:T(512)} %param.18) | copy-start | bytes 4612
  0.7 8.3 %copy-start = (bf16[1,9,3072]{2,1,0:T(8,128)(2,1)S(1)}, bf16[1,9,3072]{2,1,0:T(8,128)(2,1)}, u32[]{:S(2)}) copy-start(bf16[1,9,3072]{2,1,0:T(8,128)(2,1)} %param.10) | copy-start | bytes 165892
  2.0 7.1 %slice-start = ((bf16[1,9,3072]{2,1,0:T(8,128)(2,1)}), bf16[1,8,3072]{2,1,0:T(8,128)(2,1)S(1)}, s32[]{:S(2)}) async-start(bf16[1,9,3072]{2,1,0:T(8,128)(2,1)} %param.10), calls=%async_computation.6 | async-start | bytes 98304 | tf_op jit(solution)/shard_map/slice | solution.py:651
  3.9 12.8 %all-to-all-start = ((bf16[4,224,384]{2,1,0:T(8,128)(2,1)}), bf16[4,224,384]{2,1,0:T(8,128)(2,1)S(1)}, u32[]{:S(2)}, u32[]{:S(2)}) async-start(bf16[4,224,384]{2,1,0:T(8,128)(2,1)} %prepare_rows.1), calls=%async_computation | async-start | bytes 1376256 | tf_op jit(solution)/shard_map/all_to_all | solution.py:626
  16.7 11.9 %collective-permute-start = (bf16[4,224,384]{2,1,0:T(8,128)(2,1)S(1)}, bf16[4,224,384]{2,1,0:T(8,128)(2,1)S(1)}, u32[]{:S(2)}, u32[]{:S(2)}) collective-permute-start(bf16[4,224,384]{2,1,0:T(8,128)(2,1)S(1)} %all-to-all-done.own_ref), channel_id=1, source_target_pairs={{0,1},{1,0},{2,3},{3,2},{4,5},{5,4},{6,7},{7,6},{8,9},{9,8},{10,11... | collective-permute-start | bytes 2064392 | tf_op jit(solution)/shard_map/ppermute | solution.py:638
  25.1 16.8 %all-to-all-start.1 = ((bf16[8,144,384]{2,1,0:T(8,128)(2,1)}), bf16[8,144,384]{2,1,0:T(8,128)(2,1)S(1)}, u32[]{:S(2)}, u32[]{:S(2)}) async-start(bf16[8,144,384]{2,1,0:T(8,128)(2,1)} %get-tuple-element.37), calls=%async_computation.1 | async-start | bytes 1769472 | tf_op jit(solution)/shard_map/all_to_all | solution.py:626
  41.9 4.7 %collective-permute-start.1 = (bf16[2560,128]{1,0:T(8,128)(2,1)}, bf16[2560,128]{1,0:T(8,128)(2,1)S(1)}, u32[]{:S(2)}, u32[]{:S(2)}) collective-permute-start(bf16[2560,128]{1,0:T(8,128)(2,1)} %get-tuple-element.38), channel_id=1, source_target_pairs={{0,1},{1,0},{2,3},{3,2},{4,5},{5,4},{6,7},{7,6},{8,9},{9,8},{10,11... | collective-permute-start | bytes 1966088 | tf_op jit(solution)/shard_map/ppermute | solution.py:638
  74.6 21.0 %all-to-all-start.4 = ((bf16[4,160,128]{2,1,0:T(8,128)(2,1)}), bf16[4,160,128]{2,1,0:T(8,128)(2,1)S(1)}, u32[]{:S(2)}, u32[]{:S(2)}) async-start(bf16[4,160,128]{2,1,0:T(8,128)(2,1)} %broadcast_in_dim.9), calls=%async_computation.4 | async-start | bytes 327680 | tf_op jit(solution)/shard_map/all_to_all | solution.py:626
  108.6 11.2 %collective-permute-start.2 = (bf16[2560,128]{1,0:T(8,128)(2,1)S(1)}, bf16[2560,128]{1,0:T(8,128)(2,1)S(1)}, u32[]{:S(2)}, u32[]{:S(2)}) collective-permute-start(bf16[2560,128]{1,0:T(8,128)(2,1)S(1)} %bitcast.9), channel_id=1, source_target_pairs={{0,1},{1,0},{2,3},{3,2},{4,5},{5,4},{6,7},{7,6},{8,9},{9,8},{10,11... | collective-permute-start | bytes 1966088 | tf_op jit(solution)/shard_map/ppermute | solution.py:638

commit v6 on v5

--- a/solution.py
+++ b/solution.py
@@ -36,10 +36,13 @@
 SMALL_AT = HALF_ROWS + LATE_AT
 SMALL_ROWS = 64
 DEC = ("y", "core")
-ENC = ("x", "z")
-RUNS = [[4 * g + k for k in range(4)] for g in range(4)]
-ACROSS = [[0, 6, 10, 12], [1, 7, 11, 13], [2, 4, 8, 14], [3, 5, 9, 15]]
-PLANE = ("x", "y")
+ENC = ("x", "pair", "side")
+BLOCK = ("x", "pair", "side", "y")
+BLOCKS = [
+    [((x * 8 + pair) * 2 + (side if pair < 4 else 1 - side)) * 4 + y for x in range(4) for y in range(4) for side in range(2)]
+    for pair in range(8)
+]
+ACROSS = [[0, 2, 4, 6, 9, 11, 13, 15], [1, 3, 5, 7, 8, 10, 12, 14]]
 VMEM_BYTES = 24 * 1024 * 1024
 
 epsilon = 1e-06
@@ -639,11 +642,10 @@
 
 
 def sum_all(half, beside):
-    part = sum_blocks(swap_blocks(half.reshape(16, PACK_ROWS // 32, LANES), PLANE))
-    part = sum_blocks(swap_blocks(spread(part, 4), "z", RUNS))
-    part = sum_blocks(swap_blocks(spread(part, 4), "z", ACROSS))
+    part = sum_blocks(swap_blocks(half.reshape(32, HALF_ROWS // 32, LANES), BLOCK, BLOCKS))
+    part = sum_blocks(swap_blocks(spread(part, 8), ("pair", "side"), ACROSS))
     part, beside = lax.optimization_barrier((part, beside))
-    return swap_blocks(spread(part, 16), PLANE).reshape(HALF_ROWS, LANES), beside
+    return swap_blocks(spread(part, 32), BLOCK, BLOCKS).reshape(HALF_ROWS, LANES), beside
 
 
 def order_patches(tiles):
@@ -687,7 +689,7 @@
 
 
 def solution(mesh):
-    fine = Mesh(mesh.devices.reshape(4, 16, 4, 2), ("x", "z", "y", "core"))
+    fine = Mesh(mesh.devices.reshape(4, 8, 2, 4, 2), ("x", "pair", "side", "y", "core"))
     return jax.shard_map(
         on_device,
         mesh=fine,

time: 123 us -> 120 us (0.976)
  blocking collectives: 38.7 us -> 34.1 us
  waiting for transfers between devices: 12.3 us -> 15.7 us
  starting transfers between devices: 39.5 us -> 37.8 us
    ppermute x3, starting transfers between devices: 20.6 us -> 15.8 us  [swap_cores(): return lax.ppermute(x, 'core', [(0, 1), (1, 0)])]
    all_to_all x3 -> x2, blocking collectives: 38.7 us -> 34.1 us  [swap_blocks(): lax.all_to_all(blocks, axes, 0, 0, axis_index_groups=groups, tiled=True)]
    all_to_all x3, waiting for transfers between devices: 8.73 us -> 12.1 us  [swap_blocks(): lax.all_to_all(blocks, axes, 0, 0, axis_index_groups=groups, tiled=True)]
    all_to_all x3, starting transfers between devices: 18.9 us -> 22 us  [swap_blocks(): lax.all_to_all(blocks, axes, 0, 0, axis_index_groups=groups, tiled=True)]
  transfers between devices with their start and end apart: 6 -> 6, of which waited for: 5 -> 5; matrix products, arithmetic and copies ran while one was open for 0% -> 0% of each run, Pallas kernels for 18% -> 19%
where the time goes in v6:
time: 120 us; the launch traced here: 119 us
  starting transfers between devices  37.8 us (31%)
  blocking collectives  34.1 us (28%)
  Pallas kernels  26.5 us (22%)
  waiting for transfers between devices  15.7 us (13%)
  between operations  2.13 us (2%)
  other arithmetic  1.53 us (1%)
    all_to_all x2, blocking collectives, swap_blocks(): lax.all_to_all(blocks, axes, 0, 0, axis_index_groups=groups, tiled=True)  34.1 us
    all_to_all x3, starting transfers between devices, swap_blocks(): lax.all_to_all(blocks, axes, 0, 0, axis_index_groups=groups, tiled=True)  22 us
    ppermute x3, starting transfers between devices, swap_cores(): return lax.ppermute(x, 'core', [(0, 1), (1, 0)])  15.8 us
    pallas_call x1, Pallas kernels, backward(): pl.pallas_call(backward_kernel, out_shape=[pltpu.HBM((HALF_ROWS, LANES),...  12.3 us
    all_to_all x3, waiting for transfers between devices, swap_blocks(): lax.all_to_all(blocks, axes, 0, 0, axis_index_groups=groups, tiled=True)  12.1 us
    pallas_call x1, Pallas kernels, forward(): pl.pallas_call(forward_kernel, out_shape=[pltpu.HBM(*shape) for shape in...  6.61 us
    pallas_call x1, Pallas kernels, place_features(): pl.pallas_call(place_kernel, out_shape=jax.ShapeDtypeStruct((SHARD, WIDTH...  3.65 us
    ppermute x3, waiting for transfers between devices, swap_cores(): return lax.ppermute(x, 'core', [(0, 1), (1, 0)])  3.62 us
  transfers between devices with their start and end apart: 6, of which 5 were waited for; matrix products, arithmetic and copies ran while one was open for 0% of the time, Pallas kernels for 19%

profile of v6, /device:TPU:1, one launch (start us, length us, event | category | flops | bytes accessed | tf_op | source)
XLA Modules:
  0.0 119.0 jit_solution(12372791594208233648)
XLA Ops:
  2.0 1.9 %prepare_rows.1 = bf16[4,224,384]{2,1,0:T(8,128)(2,1)} custom-call(s32[1,1]{1,0:T(1,128)S(6)} %copy.30.count_hbm.count_ref, s32[1,1]{1,0:T(1,128)S(6)} %copy.31.gap_hbm, bf16[1,208,384]{2,1,0:T(8,128)(2,1)} %embed_hbm.1), custom_call_target="tpu_custom_call" | custom-call | tf_op jit(solution)/shard_map/prepare_rows/pallas_call | solution.py:612
  3.9 5.0 %all-to-all-start = ((bf16[4,224,384]{2,1,0:T(8,128)(2,1)}), bf16[4,224,384]{2,1,0:T(8,128)(2,1)S(1)}, u32[]{:S(2)}, u32[]{:S(2)}) async-start(bf16[4,224,384]{2,1,0:T(8,128)(2,1)} %prepare_rows.1), calls=%async_computation | async-start | bytes 1376256 | tf_op jit(solution)/shard_map/all_to_all | solution.py:629
  9.0 0.1 squeeze.3
  9.1 0.2 slice.11
  9.2 0.1 copy.29
  9.4 6.6 %block_forward.1 = (bf16[576,384]{1,0:T(8,128)(2,1)}, f32[576,384]{1,0:T(8,128)}, bf16[576,768]{1,0:T(8,128)(2,1)}, f32[576,128]{1,0:T(8,128)S(1)}, bf16[8,144,384]{2,1,0:T(8,128)(2,1)}) custom-call(s32[1,1]{1,0:T(1,128)S(6)} %copy.30.count_hbm.count_ref, bf16[576,48]{1,0:T(8,128)(2,1)S(1)} %pad_maximum_fusion.patches_ref, bf16[48,384]{1,0:T(8,128)(2,1)} %stem_w_hbm.1, ...), custom_call_target="tpu_custom_call" | custom-call | flops 679477248 | bytes 8388608 | tf_op jit(solution)/shard_map/block_forward/pallas_call | solution.py:232
  16.1 0.6 all-to-all-done.own_ref
  16.7 8.4 %collective-permute-start = (bf16[4,224,384]{2,1,0:T(8,128)(2,1)S(1)}, bf16[4,224,384]{2,1,0:T(8,128)(2,1)S(1)}, u32[]{:S(2)}, u32[]{:S(2)}) collective-permute-start(bf16[4,224,384]{2,1,0:T(8,128)(2,1)S(1)} %all-to-all-done.own_ref), channel_id=1, source_target_pairs={{0,1},{1,0},{2,3},{3,2},{4,5},{5,4},{6,7},{7,6},{8,9},{9,8},{10,11... | collective-permute-start | bytes 2064392 | tf_op jit(solution)/shard_map/ppermute | solution.py:641
  25.1 3.5 %all-to-all-start.1 = ((bf16[8,144,384]{2,1,0:T(8,128)(2,1)}), bf16[8,144,384]{2,1,0:T(8,128)(2,1)S(1)}, u32[]{:S(2)}, u32[]{:S(2)}) async-start(bf16[8,144,384]{2,1,0:T(8,128)(2,1)} %get-tuple-element.37), calls=%async_computation.1 | async-start | bytes 1769472 | tf_op jit(solution)/shard_map/all_to_all | solution.py:629
  28.6 12.3 %block_backward.1 = (bf16[2560,128]{1,0:T(8,128)(2,1)}, bf16[2560,128]{1,0:T(8,128)(2,1)}, s32[16]{0:T(128)S(1)}) custom-call(s32[2]{0:T(128)S(1)} %pad_add_fusion.place_ref, bf16[4,224,384]{2,1,0:T(8,128)(2,1)S(1)} %all-to-all-done.own_ref, bf16[4,224,384]{2,1,0:T(8,128)(2,1)S(1)} %collective-permute-done.other_ref, ...), custom_call_target="tpu_custom_call" | custom-call | flops 1358954496 | bytes 10485760 | tf_op jit(solution)/shard_map/block_backward/pallas_call | solution.py:466
  40.9 1.0 all-to-all-done.1.feat_ref
  41.9 2.8 %collective-permute-start.1 = (bf16[2560,128]{1,0:T(8,128)(2,1)}, bf16[2560,128]{1,0:T(8,128)(2,1)S(1)}, u32[]{:S(2)}, u32[]{:S(2)}) collective-permute-start(bf16[2560,128]{1,0:T(8,128)(2,1)} %get-tuple-element.38), channel_id=1, source_target_pairs={{0,1},{1,0},{2,3},{3,2},{4,5},{5,4},{6,7},{7,6},{8,9},{9,8},{10,11... | collective-permute-start | bytes 1966088 | tf_op jit(solution)/shard_map/ppermute | solution.py:641
  44.7 1.9 %collective-permute-done.1 = bf16[2560,128]{1,0:T(8,128)(2,1)S(1)} collective-permute-done((bf16[2560,128]{1,0:T(8,128)(2,1)}, bf16[2560,128]{1,0:T(8,128)(2,1)S(1)}, u32[]{:S(2)}, u32[]{:S(2)}) %collective-permute-start.1) | collective-permute-done | bytes 655392 | tf_op jit(solution)/shard_map/ppermute | solution.py:641
  46.6 1.3 %add_convert_fusion = bf16[2560,128]{1,0:T(8,128)(2,1)S(1)} fusion(bf16[2560,128]{1,0:T(8,128)(2,1)S(1)} %collective-permute-done.1, bf16[2560,128]{1,0:T(8,128)(2,1)} %get-tuple-element.35), kind=kLoop, calls=%fused_computation | loop fusion | flops 1310720 | bytes 1966080 | tf_op jit(solution)/shard_map/convert_element_type | solution.py:684
  47.9 17.3 %all_to_all.25 = bf16[32,80,128]{2,1,0:T(8,128)(2,1)S(1)} all-to-all(bf16[32,80,128]{2,1,0:T(8,128)(2,1)S(1)} %bitcast.11), channel_id=1, replica_groups={{0,8,2,10,4,12,6,14,128,136,130,138,132,140,134,142,256,264,258,266,260..., dimensions={0} | all-to-all | bytes 1310720 | tf_op jit(solution)/shard_map/all_to_all | solution.py:629
  65.2 0.1 reduce_sum.24
  65.3 0.7 broadcast_in_dim.6
  66.0 13.5 %all-to-all-start.3 = ((bf16[8,80,128]{2,1,0:T(8,128)(2,1)}), bf16[8,80,128]{2,1,0:T(8,128)(2,1)S(1)}, u32[]{:S(2)}, u32[]{:S(2)}) async-start(bf16[8,80,128]{2,1,0:T(8,128)(2,1)} %broadcast_in_dim.6), calls=%async_computation.3 | async-start | bytes 327680 | tf_op jit(solution)/shard_map/all_to_all | solution.py:629
  79.4 3.6 %place_features.1 = bf16[208,384]{1,0:T(8,128)(2,1)} custom-call(s32[2]{0:T(128)S(1)} %pad_add_fusion.place_ref, s32[16]{0:T(128)S(1)} %get-tuple-element.39.spans_ref, bf16[8,144,384]{2,1,0:T(8,128)(2,1)S(1)} %all-to-all-done.1.feat_ref), custom_call_target="tpu_custom_call" | custom-call | tf_op jit(solution)/shard_map/place_features/pallas_call | solution.py:538
  83.1 10.4 %all-to-all-done.3 = bf16[8,80,128]{2,1,0:T(8,128)(2,1)S(1)} async-done(((bf16[8,80,128]{2,1,0:T(8,128)(2,1)}), bf16[8,80,128]{2,1,0:T(8,128)(2,1)S(1)}, u32[]{:S(2)}, u32[]{:S(2)}) %all-to-all-start.3) | async-done | bytes 163872 | tf_op jit(solution)/shard_map/all_to_all | solution.py:629
  93.6 16.8 %all_to_all.26 = bf16[32,80,128]{2,1,0:T(8,128)(2,1)S(1)} all-to-all(bf16[32,80,128]{2,1,0:T(8,128)(2,1)S(1)} %broadcast_in_dim.8), channel_id=1, replica_groups={{0,8,2,10,4,12,6,14,128,136,130,138,132,140,134,142,256,264,258,266,260..., dimensions={0} | all-to-all | bytes 1310720 | tf_op jit(solution)/shard_map/all_to_all | solution.py:629
  110.5 4.7 %collective-permute-start.2 = (bf16[2560,128]{1,0:T(8,128)(2,1)S(1)}, bf16[2560,128]{1,0:T(8,128)(2,1)S(1)}, u32[]{:S(2)}, u32[]{:S(2)}) collective-permute-start(bf16[2560,128]{1,0:T(8,128)(2,1)S(1)} %bitcast.9), channel_id=1, source_target_pairs={{0,1},{1,0},{2,3},{3,2},{4,5},{5,4},{6,7},{7,6},{8,9},{9,8},{10,11... | collective-permute-start | bytes 1966088 | tf_op jit(solution)/shard_map/ppermute | solution.py:641
  115.2 1.7 %collective-permute-done.2.other_ref = bf16[2560,128]{1,0:T(8,128)(2,1)S(1)} collective-permute-done((bf16[2560,128]{1,0:T(8,128)(2,1)S(1)}, bf16[2560,128]{1,0:T(8,128)(2,1)S(1)}, u32[]{:S(2)}, u32[]{:S(2)}) %collective-permute-start.2) | collective-permute-done | bytes 655392 | tf_op jit(solution)/shard_map/ppermute | solution.py:641
  116.9 2.2 %unpack_terms.1 = (f32[48,384]{1,0:T(8,128)}, f32[49,384]{1,0:T(8,128)}, f32[384]{0:T(512)}, f32[384,768]{1,0:T(8,128)}, f32[768,384]{1,0:T(8,128)}, /*index=5*/f32[384]{0:T(512)}) custom-call(s32[2]{0:T(128)S(1)} %pad_add_fusion.place_ref, bf16[2560,128]{1,0:T(8,128)(2,1)S(1)} %bitcast.10, bf16[2560,128]{1,0:T(8,128)(2,1)S(1)} %collective-permute-done.2.other_ref), custom_call_target="tpu_custom_call" | custom-call | tf_op jit(solution)/shard_map/unpack_terms/pallas_call | solution.py:583
  (16 shorter events, 0.3 us)
Async XLA Ops:
  0.6 8.3 %copy-start.1 = (f32[384]{0:T(512)S(1)}, f32[384]{0:T(512)}, u32[]{:S(2)}) copy-start(f32[384]{0:T(512)} %param.15) | copy-start | bytes 4612
  0.6 8.3 %copy-start.2 = (f32[384]{0:T(512)S(1)}, f32[384]{0:T(512)}, u32[]{:S(2)}) copy-start(f32[384]{0:T(512)} %param.18) | copy-start | bytes 4612
  0.7 8.3 %copy-start = (bf16[1,9,3072]{2,1,0:T(8,128)(2,1)S(1)}, bf16[1,9,3072]{2,1,0:T(8,128)(2,1)}, u32[]{:S(2)}) copy-start(bf16[1,9,3072]{2,1,0:T(8,128)(2,1)} %param.10) | copy-start | bytes 165892
  2.0 7.1 %slice-start = ((bf16[1,9,3072]{2,1,0:T(8,128)(2,1)}), bf16[1,8,3072]{2,1,0:T(8,128)(2,1)S(1)}, s32[]{:S(2)}) async-start(bf16[1,9,3072]{2,1,0:T(8,128)(2,1)} %param.10), calls=%async_computation.5 | async-start | bytes 98304 | tf_op jit(solution)/shard_map/slice | solution.py:653
  3.9 12.8 %all-to-all-start = ((bf16[4,224,384]{2,1,0:T(8,128)(2,1)}), bf16[4,224,384]{2,1,0:T(8,128)(2,1)S(1)}, u32[]{:S(2)}, u32[]{:S(2)}) async-start(bf16[4,224,384]{2,1,0:T(8,128)(2,1)} %prepare_rows.1), calls=%async_computation | async-start | bytes 1376256 | tf_op jit(solution)/shard_map/all_to_all | solution.py:629
  16.7 11.9 %collective-permute-start = (bf16[4,224,384]{2,1,0:T(8,128)(2,1)S(1)}, bf16[4,224,384]{2,1,0:T(8,128)(2,1)S(1)}, u32[]{:S(2)}, u32[]{:S(2)}) collective-permute-start(bf16[4,224,384]{2,1,0:T(8,128)(2,1)S(1)} %all-to-all-done.own_ref), channel_id=1, source_target_pairs={{0,1},{1,0},{2,3},{3,2},{4,5},{5,4},{6,7},{7,6},{8,9},{9,8},{10,11... | collective-permute-start | bytes 2064392 | tf_op jit(solution)/shard_map/ppermute | solution.py:641
  25.1 16.8 %all-to-all-start.1 = ((bf16[8,144,384]{2,1,0:T(8,128)(2,1)}), bf16[8,144,384]{2,1,0:T(8,128)(2,1)S(1)}, u32[]{:S(2)}, u32[]{:S(2)}) async-start(bf16[8,144,384]{2,1,0:T(8,128)(2,1)} %get-tuple-element.37), calls=%async_computation.1 | async-start | bytes 1769472 | tf_op jit(solution)/shard_map/all_to_all | solution.py:629
  41.9 4.7 %collective-permute-start.1 = (bf16[2560,128]{1,0:T(8,128)(2,1)}, bf16[2560,128]{1,0:T(8,128)(2,1)S(1)}, u32[]{:S(2)}, u32[]{:S(2)}) collective-permute-start(bf16[2560,128]{1,0:T(8,128)(2,1)} %get-tuple-element.38), channel_id=1, source_target_pairs={{0,1},{1,0},{2,3},{3,2},{4,5},{5,4},{6,7},{7,6},{8,9},{9,8},{10,11... | collective-permute-start | bytes 1966088 | tf_op jit(solution)/shard_map/ppermute | solution.py:641
  66.0 27.6 %all-to-all-start.3 = ((bf16[8,80,128]{2,1,0:T(8,128)(2,1)}), bf16[8,80,128]{2,1,0:T(8,128)(2,1)S(1)}, u32[]{:S(2)}, u32[]{:S(2)}) async-start(bf16[8,80,128]{2,1,0:T(8,128)(2,1)} %broadcast_in_dim.6), calls=%async_computation.3 | async-start | bytes 327680 | tf_op jit(solution)/shard_map/all_to_all | solution.py:629
  110.5 6.4 %collective-permute-start.2 = (bf16[2560,128]{1,0:T(8,128)(2,1)S(1)}, bf16[2560,128]{1,0:T(8,128)(2,1)S(1)}, u32[]{:S(2)}, u32[]{:S(2)}) collective-permute-start(bf16[2560,128]{1,0:T(8,128)(2,1)S(1)} %bitcast.9), channel_id=1, source_target_pairs={{0,1},{1,0},{2,3},{3,2},{4,5},{5,4},{6,7},{7,6},{8,9},{9,8},{10,11... | collective-permute-start | bytes 1966088 | tf_op jit(solution)/shard_map/ppermute | solution.py:641
